TPU v7x, 32 devices: a whole 2x2x4 slice. The times are simulated.
32 devices in a mesh: tpoint: 2 (over y), ao: 4 (over z), aux: 2 (over x), rep: 2 (over core).
Axes of the slice: x: 2, y: 2, z: 4, core: 2. Of those that a mesh axis runs over, the one named last changes fastest.
Arguments:
- tensor: bfloat16 [1024, 8, 4096], P(('aux', 'rep'), None, 'ao'), may hold values from -0.4375 to 0.4375
- block_mask: int32 [8, 8], replicated, may hold values 0 or 1
- occ_green: bfloat16 [16, 3, 64, 64], P(('tpoint', 'ao')), parts along dimension 0, may hold values from -0.75 to 0.75
- virt_green: bfloat16 [16, 3, 64, 64], P(('tpoint', 'ao')), parts along dimension 0, may hold values from -0.75 to 0.75
- green_mask: int32 [8, 3], replicated, may hold values 0 or 1
Outputs:
- response: float32 [512, 1024], P(('tpoint', 'ao'), ('aux', 'rep')), parts along dimension 0
There are 2 independent parts, one for each index of `tpoint`. A program takes and returns all parts, laid end to end along the dimension named above; an argument that names none is the same for every part. Nothing has to cross between parts.
All inputs are finite; a program needn't handle non-finite values.
Results may differ from a plain program's by a relative error of at most 0.0041.
Values may be sent and summed in bfloat16 or wider, within the bound.
No kernel may reach another device: no remote copies, remote signals or barrier semaphores. Data moves between devices by JAX's collectives and lax.ppermute only.
A program may use at most 128 MiB of HBM per device.

v0:
```python
import jax
import jax.numpy as jnp
from jax import lax
from jax.sharding import PartitionSpec as P

AOB = 64
RB = 128
SL = 64


def padded_2(cells, sides, width):
    for axis, dim in sides:
        count = lax.axis_size(axis)
        ends = count - 1
        head = lax.slice_in_dim(cells, 0, width, axis=dim)
        tail = lax.slice_in_dim(cells, cells.shape[dim] - width, cells.shape[dim], axis=dim)
        cells = jnp.concatenate(
            [
                lax.ppermute(tail, axis, [(i, (i + 1) % count) for i in range(ends)]),
                cells,
                lax.ppermute(head, axis, [((i + 1) % count, i) for i in range(ends)]),
            ],
            axis=dim,
        )
    return cells


def contract_slab(padded, occ, virt, blocks_dev, reach):
    total = None
    for offset in range(2 * reach + 1):
        near = padded[:, offset : offset + blocks_dev]
        inner = jnp.einsum(
            "rimn,ins->rims", near, virt[:, offset], preferred_element_type=jnp.float32
        ).astype(jnp.bfloat16)
        term = jnp.einsum(
            "ilm,rims->rils", occ[:, offset], inner, preferred_element_type=jnp.float32
        )
        total = term if total is None else total + term
    return total


def per_device(tensor, block_mask, occ_green, virt_green, green_mask):
    work = lax.all_to_all(tensor, "ao", split_axis=1, concat_axis=2, tiled=True)
    rows_dev = work.shape[0]
    blocks_dev = work.shape[1]
    reach = (occ_green.shape[1] - 1) // 2
    ao_index = lax.axis_index("ao")
    shard = lax.axis_index(("aux", "rep"))
    first_block = ao_index * blocks_dev
    total_blocks = blocks_dev * lax.axis_size("ao")
    block_cols = lax.dynamic_slice_in_dim(block_mask, first_block, blocks_dev, 1)
    per_shard = rows_dev // RB
    mask_rows = lax.dynamic_slice_in_dim(block_cols, shard * per_shard, per_shard, 0)
    row_mask = jnp.repeat(mask_rows, RB, axis=0).astype(jnp.bfloat16)
    masked = work * row_mask[:, :, None]
    local_pairs = lax.dynamic_slice_in_dim(green_mask, first_block, blocks_dev, 0)
    neighbour = (
        first_block + jnp.arange(blocks_dev)[:, None] + jnp.arange(2 * reach + 1)[None, :] - reach
    )
    valid = ((neighbour >= 0) & (neighbour < total_blocks)).astype(jnp.int32)
    pair = (local_pairs * valid).astype(jnp.bfloat16)
    occ = occ_green * pair[:, :, None, None]
    virt = virt_green * pair[:, :, None, None]
    own_rows = masked[:SL].reshape(SL, blocks_dev, AOB, AOB)
    padded = padded_2(own_rows, (("ao", 1),), reach)
    own_total = contract_slab(padded, occ, virt, blocks_dev, reach)
    own_sums = own_total.astype(jnp.bfloat16).reshape(SL, blocks_dev, AOB * AOB)
    sums = lax.all_gather(own_sums, ("aux", "rep"), axis=0, tiled=True)
    partial_terms = lax.dot_general(
        sums, masked, (((1, 2), (1, 2)), ((), ())), preferred_element_type=jnp.float32
    )
    return lax.psum_scatter(partial_terms, "ao", scatter_dimension=0, tiled=True)


def solution(mesh):
    return jax.shard_map(
        per_device,
        mesh=mesh,
        in_specs=(
            P(("aux", "rep"), None, "ao"),
            P(),
            P(("tpoint", "ao"), None, None, None),
            P(("tpoint", "ao"), None, None, None),
            P(),
        ),
        out_specs=P(("tpoint", "ao"), ("aux", "rep")),
        check_vma=False,
    )
```

profile of v0, /device:TPU:0, one launch (start us, length us, event | category | flops | bytes accessed | tf_op | source)
XLA Modules:
  0.0 231.9 jit_solution(8457050848024228041)
XLA Ops:
  6.5 6.5 %copy.16 = bf16[256,8,1024]{2,0,1:T(8,128)(2,1)} copy(bf16[256,8,1024]{2,1,0:T(8,128)(2,1)} %param.5) | data formatting | bytes 8388608 | tf_op args[0]
  13.0 0.0 copy-start.1
  13.0 0.0 copy-start.2
  13.0 0.0 copy-start.3
  13.0 6.4 %all-to-all-start = ((bf16[256,8,1024]{2,0,1:T(8,128)(2,1)}), bf16[256,8,1024]{2,0,1:T(8,128)(2,1)}, u32[]{:S(2)}, u32[]{:S(2)}) async-start(bf16[256,8,1024]{2,0,1:T(8,128)(2,1)} %copy.16), calls=%async_computation | async-start | bytes 8388608 | tf_op jit(solution)/shard_map/all_to_all | solution.py:43
  19.5 0.0 all-gather.2.cloned.1.call-start
  19.5 0.8 dynamic-slice_convert_fusion
  20.2 0.1 copy.18
  20.3 0.1 broadcast_bitcast_fusion
  20.4 0.0 copy-done.1
  20.4 0.1 copy.19
  20.6 0.0 copy-done.2
  20.6 0.1 copy.15
  20.7 0.0 copy-done.3
  20.7 0.1 select_convert_fusion
  20.8 92.1 %all-to-all-done = bf16[256,8,1024]{2,0,1:T(8,128)(2,1)} async-done(((bf16[256,8,1024]{2,0,1:T(8,128)(2,1)}), bf16[256,8,1024]{2,0,1:T(8,128)(2,1)}, u32[]{:S(2)}, u32[]{:S(2)}) %all-to-all-start) | async-done | bytes 4194336 | tf_op jit(solution)/shard_map/all_to_all | solution.py:43
  112.9 2.7 %copy.36 = bf16[4,2,32,8,1024]{4,3,0,2,1:T(8,128)(2,1)S(1)} copy(bf16[4,2,32,8,1024]{4,3,2,1,0:T(8,128)(2,1)} %bitcast.35) | data formatting | bytes 8388608 | tf_op jit(solution)/shard_map/all_to_all | solution.py:43
  115.6 0.3 broadcast_multiply_fusion
  115.9 0.0 copy-start
  115.9 1.9 copy-done
  117.9 0.1 slice.47
  117.9 2.3 reshape.19
  120.2 1.5 fusion.24
  121.8 1.3 collective-permute-start
  123.1 0.1 broadcast_multiply_fusion.2
  123.2 1.5 collective-permute-start.1
  124.7 4.6 %fusion.5 = f32[2,64,64,64]{3,2,1,0:T(8,128)} fusion(bf16[64,2,64,64]{3,2,0,1:T(8,128)(2,1)S(1)} %reshape.19, bf16[2,3,64,64]{2,3,0,1:T(8,128)(2,1)S(1)} %get-tuple-element.8, bf16[2,3,64,64]{2,3,0,1:T(8,128)(2,1)S(1)} %get-tuple-element.7), kind=kOutput, calls=%fused_computation.8 | convolution fusion | flops 134742016 | bytes 4259840 | tf_op jit(solution)/shard_map/ilm,rims->rils/dot_general | solution.py:35
  129.3 15.8 %collective-permute-done = bf16[64,1,64,64]{3,2,0,1:T(8,128)(2,1)S(1)} collective-permute-done((bf16[64,1,64,64]{3,2,0,1:T(8,128)(2,1)}, bf16[64,1,64,64]{3,2,0,1:T(8,128)(2,1)S(1)}, u32[]{:S(2)}, u32[]{:S(2)}) %collective-permute-start) | collective-permute-done | bytes 524320 | tf_op jit(solution)/shard_map/ppermute | solution.py:19
  145.2 4.6 %fusion.7 = f32[2,64,64,64]{3,2,1,0:T(8,128)} fusion(bf16[64,2,64,64]{3,2,0,1:T(8,128)(2,1)S(1)} %reshape.19, bf16[64,1,64,64]{3,2,0,1:T(8,128)(2,1)S(1)} %collective-permute-done, bf16[2,3,64,64]{2,3,0,1:T(8,128)(2,1)S(1)} %get-tuple-element.8, bf16[2,3,64,64]{2,3,0,1:T(8,128)(2,1)S(1)} %get-tuple-element.7), kind=kOutput, calls=%fused_computation.10 | convolution fusion | flops 136839168 | bytes 5308416 | tf_op jit(solution)/shard_map/ilm,rims->rils/dot_general | solution.py:35
  149.8 0.0 collective-permute-done.1
  149.8 7.8 %fusion.14 = bf16[64,2,64,64]{2,3,0,1:T(8,128)(2,1)} fusion(bf16[64,1,64,64]{3,2,0,1:T(8,128)(2,1)} %collective-permute-done.1, bf16[64,2,64,64]{3,2,0,1:T(8,128)(2,1)S(1)} %reshape.19, f32[2,64,64,64]{3,2,1,0:T(8,128)} %fusion.7, f32[2,64,64,64]{3,2,1,0:T(8,128)} %fusion.5, bf16[2,3,64,64]{2,3,0,1:T(8,128)(2,1)S(1)} %get-tuple-element.8, ...), kind=kOutput, calls=%fused_computation.17 | convolution fusion | flops 138412032 | bytes 7929856 | tf_op jit(solution)/shard_map/ilm,rims->rils/dot_general | solution.py:35
  157.6 3.1 %copy.23 = bf16[64,2,64,64]{3,2,0,1:T(8,128)(2,1)S(1)} copy(bf16[64,2,64,64]{2,3,0,1:T(8,128)(2,1)} %fusion.14) | data formatting | bytes 2097152 | tf_op jit(solution)/shard_map/convert_element_type | solution.py:67
  160.7 2.5 %reshape.20 = bf16[64,2,4096]{2,0,1:T(8,128)(2,1)} reshape(bf16[64,2,64,64]{3,2,0,1:T(8,128)(2,1)S(1)} %copy.23) | data formatting | bytes 2097152 | tf_op jit(solution)/shard_map/reshape | solution.py:67
  163.2 0.0 all-gather.2.cloned.1.call-update
  163.3 0.0 reduce-scatter.2.cloned.1.call-start
  163.3 36.4 %all-gather.2.cloned.1.call-done = bf16[256,2,4096]{2,0,1:T(8,128)(2,1)} async-done(((bf16[64,2,4096]{2,0,1:T(8,128)(2,1)}), bf16[256,2,4096]{2,0,1:T(8,128)(2,1)}) %all-gather.2.cloned.1.call-update) | async-done | bytes 4194320 | tf_op jit(solution)/shard_map/all_gather | solution.py:68
  199.7 5.5 %convolution_bitcast_fusion = f32[256,256]{1,0:T(8,128)} fusion(bf16[256,2,4096]{2,0,1:T(8,128)(2,1)} %all-gather.2.cloned.1.call-done, bf16[256,2,4096]{2,0,1:T(8,128)(2,1)} %copy-done), kind=kOutput, calls=%fused_computation.18 | convolution fusion | flops 1073741824 | bytes 8650752 | tf_op jit(solution)/shard_map/dot_general | solution.py:69
  205.2 0.0 reduce-scatter.2.cloned.1.call-update
  205.2 19.8 %reduce-scatter.2.cloned.1.call-done = f32[64,256]{1,0:T(8,128)} async-done(((f32[256,256]{1,0:T(8,128)}), f32[64,256]{1,0:T(8,128)}) %reduce-scatter.2.cloned.1.call-update) | async-done | bytes 65552 | tf_op jit(solution)/shard_map/reduce_scatter | solution.py:72
  (2 shorter events, 0.0 us)
Async XLA Ops:
  13.0 7.4 %copy-start.1 = (bf16[2,3,64,64]{3,2,1,0:T(8,128)(2,1)S(1)}, bf16[2,3,64,64]{3,2,1,0:T(8,128)(2,1)}, u32[]{:S(2)}) copy-start(bf16[2,3,64,64]{3,2,1,0:T(8,128)(2,1)} %param.7) | copy-start | bytes 147460
  13.0 7.5 %copy-start.2 = (bf16[2,3,64,64]{3,2,1,0:T(8,128)(2,1)S(1)}, bf16[2,3,64,64]{3,2,1,0:T(8,128)(2,1)}, u32[]{:S(2)}) copy-start(bf16[2,3,64,64]{3,2,1,0:T(8,128)(2,1)} %param.8) | copy-start | bytes 147460
  13.0 7.7 %copy-start.3 = (s32[8,3]{0,1:T(4,128)S(1)}, s32[8,3]{0,1:T(4,128)}, u32[]{:S(2)}) copy-start(s32[8,3]{0,1:T(4,128)} %param.9) | copy-start | bytes 292
  13.0 99.9 %all-to-all-start = ((bf16[256,8,1024]{2,0,1:T(8,128)(2,1)}), bf16[256,8,1024]{2,0,1:T(8,128)(2,1)}, u32[]{:S(2)}, u32[]{:S(2)}) async-start(bf16[256,8,1024]{2,0,1:T(8,128)(2,1)} %copy.16), calls=%async_computation | async-start | bytes 8388608 | tf_op jit(solution)/shard_map/all_to_all | solution.py:43
  19.5 180.2 %all-gather.2.cloned.1.call-start = ((), (), s32[]{:S(2)}) async-start(), calls=%async_computation.2 | async-start | bytes 5242880 | tf_op jit(solution)/shard_map/all_gather | solution.py:68
  115.9 1.9 copy-start
  121.8 23.4 %collective-permute-start = (bf16[64,1,64,64]{3,2,0,1:T(8,128)(2,1)}, bf16[64,1,64,64]{3,2,0,1:T(8,128)(2,1)S(1)}, u32[]{:S(2)}, u32[]{:S(2)}) collective-permute-start(bf16[64,1,64,64]{3,2,0,1:T(8,128)(2,1)} %get-tuple-element.5), channel_id=1, source_target_pairs={{0,4},{4,8},{8,12},{1,5},{5,9},{9,13},{2,6},{6,10},{10,14},{3,7},{... | collective-permute-start | bytes 1572872 | tf_op jit(solution)/shard_map/ppermute | solution.py:19
  123.2 26.6 %collective-permute-start.1 = (bf16[64,1,64,64]{3,2,0,1:T(8,128)(2,1)}, bf16[64,1,64,64]{3,2,0,1:T(8,128)(2,1)}, u32[]{:S(2)}, u32[]{:S(2)}) collective-permute-start(bf16[64,1,64,64]{3,2,0,1:T(8,128)(2,1)} %get-tuple-element.6), channel_id=1, source_target_pairs={{4,0},{8,4},{12,8},{5,1},{9,5},{13,9},{6,2},{10,6},{14,10},{7,3},{... | collective-permute-start | bytes 1572872 | tf_op jit(solution)/shard_map/ppermute | solution.py:21
  163.3 61.7 %reduce-scatter.2.cloned.1.call-start = ((), (), s32[]{:S(2)}) async-start(), calls=%async_computation.3 | async-start | bytes 327680 | tf_op jit(solution)/shard_map/reduce_scatter | solution.py:72
Sparse Core Ops, SparseCore 0:
  163.4 36.2 all-gather.1
  205.3 19.6 reduce-scatter.1
where the time goes:
time: 232 us
  waiting for transfers between devices  164 us (71%)
  matrix products  22.6 us (10%)
  local copies, waits for them, and re-layouts  21.1 us (9%)
  between operations  13.5 us (6%)
  starting transfers between devices  9.31 us (4%)
    all_to_all x1, waiting for transfers between devices, per_device(): work = lax.all_to_all(tensor, 'ao', split_axis=1, concat_axis=2, tiled=True)  92.1 us
    all_gather x1, waiting for transfers between devices, per_device(): sums = lax.all_gather(own_sums, ('aux', 'rep'), axis=0, tiled=True)  36.4 us
    reduce_scatter x1, waiting for transfers between devices, per_device(): lax.psum_scatter(partial_terms, 'ao', scatter_dimension=0, tiled=True)  19.8 us
    dot_general x3, matrix products, contract_slab(): jnp.einsum('ilm,rims->rils', occ[:, offset], inner, preferred_element_typ...  17.1 us
    ppermute x1, waiting for transfers between devices, padded_2(): lax.ppermute(tail, axis, [(i, (i + 1) % count) for i in range(ends)])  15.8 us
    unnamed x13, local copies, waits for them, and re-layouts  8.77 us
    all_to_all x1, starting transfers between devices, per_device(): work = lax.all_to_all(tensor, 'ao', split_axis=1, concat_axis=2, tiled=True)  6.45 us
    dot_general x1, matrix products, per_device(): lax.dot_general(sums, masked, (((1, 2), (1, 2)), ((), ())), preferred_ele...  5.47 us
  transfers between devices with their start and end apart: 5, of which 4 were waited for; matrix products, arithmetic and copies ran while one was open for 5% of the time, Pallas kernels for 0%

commit v1 on v0

v1 whole, which is shorter than its diff:
```python
import jax
import jax.numpy as jnp
from jax import lax
from jax.sharding import PartitionSpec as P

AOB = 64
RB = 128
SL = 64


def green_blocks(occ_all, virt_all, green_mask, slab_mask):
    blocks, width = green_mask.shape
    reach = (width - 1) // 2
    neighbour = jnp.arange(blocks)[:, None] + jnp.arange(width)[None, :] - reach
    valid = (neighbour >= 0) & (neighbour < blocks)
    near_mask = slab_mask[jnp.clip(neighbour, 0, blocks - 1)]
    pair = jnp.where(valid, green_mask, 0)
    occ = occ_all * pair.astype(jnp.bfloat16)[:, :, None, None]
    virt = virt_all * (pair * near_mask).astype(jnp.bfloat16)[:, :, None, None]
    return occ, virt


def per_device(tensor, block_mask, occ_green, virt_green, green_mask):
    rows_dev, blocks, cols = tensor.shape
    reach = (occ_green.shape[1] - 1) // 2
    shard = lax.axis_index(("aux", "rep"))
    per_shard = rows_dev // RB
    mask_rows = lax.dynamic_slice_in_dim(block_mask, shard * per_shard, per_shard, 0)
    row_mask = jnp.repeat(mask_rows, RB, axis=0).astype(jnp.bfloat16)
    masked = tensor * row_mask[:, :, None]
    slab = lax.all_to_all(tensor[:SL], "ao", split_axis=0, concat_axis=2, tiled=True)
    occ_all = lax.all_gather(occ_green, "ao", axis=0, tiled=True)
    virt_all = lax.all_gather(virt_green, "ao", axis=0, tiled=True)
    occ, virt = green_blocks(occ_all, virt_all, green_mask, mask_rows[0])
    own = slab.shape[0]
    padded = jnp.pad(slab.reshape(own, blocks, AOB, AOB), ((0, 0), (reach, reach), (0, 0), (0, 0)))
    total = None
    for offset in range(2 * reach + 1):
        near = padded[:, offset : offset + blocks]
        inner = jnp.einsum(
            "rimn,ins->rims", near, virt[:, offset], preferred_element_type=jnp.float32
        ).astype(jnp.bfloat16)
        term = jnp.einsum(
            "ilm,rims->rils", occ[:, offset], inner, preferred_element_type=jnp.float32
        )
        total = term if total is None else total + term
    own_sums = total.astype(jnp.bfloat16).reshape(own, blocks, AOB * AOB)
    back = lax.all_to_all(own_sums, "ao", split_axis=2, concat_axis=0, tiled=True)
    sums = lax.all_gather(back, ("aux", "rep"), axis=0, tiled=True)
    partial_terms = lax.dot_general(
        sums, masked, (((1, 2), (1, 2)), ((), ())), preferred_element_type=jnp.float32
    )
    return lax.psum_scatter(partial_terms, "ao", scatter_dimension=0, tiled=True)


def solution(mesh):
    return jax.shard_map(
        per_device,
        mesh=mesh,
        in_specs=(
            P(("aux", "rep"), None, "ao"),
            P(),
            P(("tpoint", "ao"), None, None, None),
            P(("tpoint", "ao"), None, None, None),
            P(),
        ),
        out_specs=P(("tpoint", "ao"), ("aux", "rep")),
        check_vma=False,
    )
```

time: 232 us -> 223 us (0.961)
  waiting for transfers between devices: 164 us -> 48.9 us
  blocking collectives: 0 us -> 72.6 us
  local copies, waits for them, and re-layouts: 21.1 us -> 49.6 us
  other arithmetic: 1.27 us -> 6.2 us
  starting transfers between devices: 9.31 us -> 6.36 us
  matrix products: 22.6 us -> 25.3 us
    all_to_all x1, waiting for transfers between devices: 92.1 us -> 0.01 us  [per_device(): lax.all_to_all(tensor[:SL], 'ao', split_axis=0, concat_axis=2, tiled=True)]
    all_gather x0 -> x2, blocking collectives: none -> 48.1 us  [the longest x1 32.9 us: per_device(): virt_all = lax.all_gather(virt_green, 'ao', axis=0, tiled=True)]
    all_to_all x0 -> x1, blocking collectives: none -> 24.5 us  [per_device(): lax.all_to_all(own_sums, 'ao', split_axis=2, concat_axis=0, tiled=True)]
    ppermute x2 -> x0, waiting for transfers between devices: 15.8 us -> none  [the longest x1 15.8 us: padded_2(): lax.ppermute(tail, axis, [(i, (i + 1) % count) for i in range(ends)])]
    reshape x2, local copies, waits for them, and re-layouts: 4.8 us -> 16.9 us  [the longest x1 15.6 us: per_device(): own_sums = total.astype(jnp.bfloat16).reshape(own, blocks, AOB * AOB)]
    all_to_all x1 -> x3, local copies, waits for them, and re-layouts: 2.67 us -> 11.9 us  [the longest x2 11 us: per_device(): lax.all_to_all(own_sums, 'ao', split_axis=2, concat_axis=0, tiled=True)]
    unnamed x13 -> x11, local copies, waits for them, and re-layouts: 8.77 us -> 17.4 us
    all_gather x1, waiting for transfers between devices: 36.4 us -> 29.1 us  [per_device(): sums = lax.all_gather(back, ('aux', 'rep'), axis=0, tiled=True)]
  transfers between devices with their start and end apart: 5 -> 3, of which waited for: 4 -> 2; matrix products, arithmetic and copies ran while one was open for 5% -> 3% of each run, Pallas kernels for 0% -> 0%
where the time goes in v1:
time: 223 us; the launch traced here: 222 us
  blocking collectives  72.6 us (33%)
  local copies, waits for them, and re-layouts  49.6 us (22%)
  waiting for transfers between devices  48.9 us (22%)
  matrix products  25.3 us (11%)
  between operations  13.5 us (6%)
  starting transfers between devices  6.36 us (3%)
  other arithmetic  6.2 us (3%)
    all_gather x1, blocking collectives, per_device(): virt_all = lax.all_gather(virt_green, 'ao', axis=0, tiled=True)  32.9 us
    all_gather x1, waiting for transfers between devices, per_device(): sums = lax.all_gather(back, ('aux', 'rep'), axis=0, tiled=True)  29.1 us
    all_to_all x1, blocking collectives, per_device(): lax.all_to_all(own_sums, 'ao', split_axis=2, concat_axis=0, tiled=True)  24.5 us
    reduce_scatter x1, waiting for transfers between devices, per_device(): lax.psum_scatter(partial_terms, 'ao', scatter_dimension=0, tiled=True)  19.7 us
    unnamed x11, local copies, waits for them, and re-layouts  17.4 us
    dot_general x3, matrix products, per_device(): jnp.einsum('ilm,rims->rils', occ[:, offset], inner, preferred_element_typ...  16 us
    reshape x1, local copies, waits for them, and re-layouts, per_device(): own_sums = total.astype(jnp.bfloat16).reshape(own, blocks, AOB * AOB)  15.6 us
    all_gather x1, blocking collectives, per_device(): occ_all = lax.all_gather(occ_green, 'ao', axis=0, tiled=True)  15.2 us
  transfers between devices with their start and end apart: 3, of which 2 were waited for; matrix products, arithmetic and copies ran while one was open for 3% of the time, Pallas kernels for 0%

profile of v1, /device:TPU:0, one launch (start us, length us, event | category | flops | bytes accessed | tf_op | source)
XLA Modules:
  0.0 222.5 jit_solution(1261384483652285942)
XLA Ops:
  6.5 2.3 %slice.33 = bf16[64,8,1024]{2,1,0:T(8,128)(2,1)} slice(bf16[256,8,1024]{2,1,0:T(8,128)(2,1)} %param.5), slice={[0:64], [0:8], [0:1024]} | slice | bytes 2097152 | tf_op jit(solution)/shard_map/slice | solution.py:31
  8.8 6.3 %all-to-all-start = ((bf16[64,8,1024]{2,1,0:T(8,128)(2,1)}), bf16[64,8,1024]{2,1,0:T(8,128)(2,1)S(1)}, u32[]{:S(2)}, u32[]{:S(2)}) async-start(bf16[64,8,1024]{2,1,0:T(8,128)(2,1)} %slice.33), calls=%async_computation | async-start | bytes 2097152 | tf_op jit(solution)/shard_map/all_to_all | solution.py:31
  15.1 0.0 all-gather.2.cloned.1.call-start
  15.1 0.1 reshape.51
  15.2 0.7 fusion.31
  15.9 0.0 copy-start.2
  15.9 0.0 copy-start.1
  15.9 0.0 copy-start.3
  16.0 0.7 gather_fusion
  16.7 0.1 reshape.50
  16.7 0.1 copy.43
  16.8 0.0 copy-done.2
  16.8 32.9 %all_gather.9 = bf16[8,3,64,64]{3,2,1,0:T(8,128)(2,1)S(1)} all-gather(bf16[2,3,64,64]{3,2,1,0:T(8,128)(2,1)S(1)} %copy-done.2), channel_id=1, replica_groups=mesh['tpoint'=2,'ao'=4,'aux'=2,'rep'=2] {'ao'}, dimensions={0}, use_global_device_ids=true | all-gather | bytes 245760 | tf_op jit(solution)/shard_map/all_gather | solution.py:33
  49.8 0.2 copy.44
  50.0 0.0 copy-done.1
  50.1 15.2 %all_gather.10 = bf16[8,3,64,64]{3,2,0,1:T(8,128)(2,1)S(1)} all-gather(bf16[2,3,64,64]{3,2,0,1:T(8,128)(2,1)S(1)} %copy.47), channel_id=1, replica_groups=mesh['tpoint'=2,'ao'=4,'aux'=2,'rep'=2] {'ao'}, dimensions={0}, use_global_device_ids=true | all-gather | bytes 245760 | tf_op jit(solution)/shard_map/all_gather | solution.py:32
  65.2 0.0 copy-done.3
  65.2 0.1 broadcast_multiply_fusion.2
  65.3 0.9 broadcast_multiply_fusion.1
  66.2 0.0 all-to-all-done
  66.2 0.9 copy.79
  67.1 1.3 reshape.47
  68.4 0.0 copy-start
  68.4 5.6 %fusion.5 = f32[8,16,64,64]{3,2,1,0:T(8,128)} fusion(bf16[8,3,64,64]{3,2,0,1:T(8,128)(2,1)} %broadcast_multiply_fusion.1, bf16[8,3,64,64]{2,3,0,1:T(8,128)(2,1)S(1)} %broadcast_multiply_fusion.2, bf16[16,8,64,64]{3,2,1,0:T(8,128)(2,1)S(1)} %reshape.47), kind=kOutput, calls=%fused_computation.9 | convolution fusion | flops 134742016 | bytes 4456448 | tf_op jit(solution)/shard_map/ilm,rims->rils/dot_general | solution.py:43
  74.0 0.0 copy-done
  74.0 4.4 %fusion.7 = f32[8,16,64,64]{3,2,1,0:T(8,128)} fusion(bf16[8,3,64,64]{3,2,0,1:T(8,128)(2,1)S(1)} %copy-done, bf16[8,3,64,64]{2,3,0,1:T(8,128)(2,1)S(1)} %broadcast_multiply_fusion.2, bf16[16,8,64,64]{3,2,1,0:T(8,128)(2,1)S(1)} %reshape.47), kind=kOutput, calls=%fused_computation.11 | convolution fusion | flops 134742016 | bytes 4456448 | tf_op jit(solution)/shard_map/ilm,rims->rils/dot_general | solution.py:43
  78.4 6.0 %fusion.14 = bf16[16,8,64,64]{2,3,0,1:T(8,128)(2,1)} fusion(f32[8,16,64,64]{3,2,1,0:T(8,128)} %fusion.7, f32[8,16,64,64]{3,2,1,0:T(8,128)} %fusion.5, bf16[8,3,64,64]{3,2,0,1:T(8,128)(2,1)S(1)} %copy-done, bf16[8,3,64,64]{2,3,0,1:T(8,128)(2,1)S(1)} %broadcast_multiply_fusion.2, bf16[16,8,64,64]{3,2,1,0:T(8,128)(2,1)S(1)} %reshape.47), kind=kOutput, calls=%fused_computation.18 | convolution fusion | flops 136314880 | bytes 7602176 | tf_op jit(solution)/shard_map/ilm,rims->rils/dot_general | solution.py:43
  84.5 15.6 %copy.60 = bf16[16,8,64,64]{0,1,3,2:T(8,128)(2,1)} copy(bf16[16,8,64,64]{2,3,0,1:T(8,128)(2,1)} %fusion.14) | data formatting | bytes 2097152 | tf_op jit(solution)/shard_map/reshape | solution.py:47
  100.0 10.2 %reshape.65 = bf16[4,2,65536]{2,1,0:T(2,128)(2,1)S(1)} reshape(bf16[4096,8,16]{2,1,0:T(8,128)(2,1)} %bitcast.70) | data formatting | bytes 2097152
  110.3 24.5 %all_to_all.33 = bf16[4,2,65536]{2,1,0:T(2,128)(2,1)S(1)} all-to-all(bf16[4,2,65536]{2,1,0:T(2,128)(2,1)S(1)} %reshape.65), channel_id=1, replica_groups=mesh['tpoint'=2,'ao'=4,'aux'=2,'rep'=2] {'ao'}, dimensions={0} | all-to-all | bytes 2097152 | tf_op jit(solution)/shard_map/all_to_all | solution.py:48
  134.8 7.1 %reshape.66 = bf16[4096,8,16]{2,1,0:T(8,128)(2,1)} reshape(bf16[4,2,65536]{2,1,0:T(2,128)(2,1)S(1)} %all_to_all.33) | data formatting | bytes 2097152
  141.9 9.4 %copy.61 = bf16[16,8,4,1024]{3,2,1,0:T(4,128)(2,1)S(1)} copy(bf16[16,8,4,1024]{0,1,3,2:T(8,128)(2,1)} %bitcast.71) | data formatting | bytes 2097152 | tf_op jit(solution)/shard_map/all_to_all | solution.py:48
  151.3 1.6 copy.52
  152.9 0.0 all-gather.2.cloned.1.call-update
  152.9 0.0 reduce-scatter.2.cloned.1.call-start
  153.0 4.5 %broadcast_multiply_fusion = bf16[256,8,1024]{2,1,0:T(8,128)(2,1)} fusion(bf16[256,8,1024]{2,1,0:T(8,128)(2,1)} %param.5, bf16[256,8]{1,0:T(8,128)(2,1)S(1)} %bitcast.76), kind=kLoop, calls=%fused_computation.13 | loop fusion | flops 2097152 | bytes 8392704 | tf_op jit(solution)/shard_map/mul | solution.py:30
  157.5 29.1 %all-gather.2.cloned.1.call-done = bf16[256,8,1024]{2,0,1:T(8,128)(2,1)} async-done(((bf16[64,8,1024]{2,0,1:T(8,128)(2,1)}), bf16[256,8,1024]{2,0,1:T(8,128)(2,1)}) %all-gather.2.cloned.1.call-update) | async-done | bytes 4194320 | tf_op jit(solution)/shard_map/all_gather | solution.py:49
  186.7 9.2 %fusion.17 = f32[256,256]{1,0:T(8,128)} fusion(bf16[256,8,1024]{2,0,1:T(8,128)(2,1)} %all-gather.2.cloned.1.call-done, bf16[256,8,1024]{2,1,0:T(8,128)(2,1)} %broadcast_multiply_fusion), kind=kOutput, calls=%fused_computation.19 | convolution fusion | flops 1073741824 | bytes 8650752 | tf_op jit(solution)/shard_map/dot_general | solution.py:50
  195.9 0.0 reduce-scatter.2.cloned.1.call-update
  195.9 19.7 %reduce-scatter.2.cloned.1.call-done = f32[64,256]{1,0:T(8,128)} async-done(((f32[256,256]{1,0:T(8,128)}), f32[64,256]{1,0:T(8,128)}) %reduce-scatter.2.cloned.1.call-update) | async-done | bytes 65552 | tf_op jit(solution)/shard_map/reduce_scatter | solution.py:53
  (6 shorter events, 0.0 us)
Async XLA Ops:
  8.8 57.4 %all-to-all-start = ((bf16[64,8,1024]{2,1,0:T(8,128)(2,1)}), bf16[64,8,1024]{2,1,0:T(8,128)(2,1)S(1)}, u32[]{:S(2)}, u32[]{:S(2)}) async-start(bf16[64,8,1024]{2,1,0:T(8,128)(2,1)} %slice.33), calls=%async_computation | async-start | bytes 2097152 | tf_op jit(solution)/shard_map/all_to_all | solution.py:31
  15.1 171.5 %all-gather.2.cloned.1.call-start = ((), (), s32[]{:S(2)}) async-start(), calls=%async_computation.3 | async-start | bytes 5242880 | tf_op jit(solution)/shard_map/all_gather | solution.py:49
  15.9 0.9 copy-start.2
  15.9 34.1 %copy-start.1 = (bf16[2,3,64,64]{3,2,1,0:T(8,128)(2,1)S(1)}, bf16[2,3,64,64]{3,2,1,0:T(8,128)(2,1)}, u32[]{:S(2)}) copy-start(bf16[2,3,64,64]{3,2,1,0:T(8,128)(2,1)} %param.7) | copy-start | bytes 147460
  15.9 49.3 %copy-start.3 = (s32[8,3]{0,1:T(4,128)S(1)}, s32[8,3]{0,1:T(4,128)}, u32[]{:S(2)}) copy-start(s32[8,3]{0,1:T(4,128)} %param.9) | copy-start | bytes 292
  68.4 5.6 %copy-start = (bf16[8,3,64,64]{3,2,0,1:T(8,128)(2,1)S(1)}, bf16[8,3,64,64]{3,2,0,1:T(8,128)(2,1)}, u32[]{:S(2)}) copy-start(bf16[8,3,64,64]{3,2,0,1:T(8,128)(2,1)} %broadcast_multiply_fusion.1) | copy-start | bytes 589828
  152.9 62.7 %reduce-scatter.2.cloned.1.call-start = ((), (), s32[]{:S(2)}) async-start(), calls=%async_computation.4 | async-start | bytes 327680 | tf_op jit(solution)/shard_map/reduce_scatter | solution.py:53
Sparse Core Ops, SparseCore 0:
  153.0 33.5 all-gather.1
  196.0 19.5 reduce-scatter.1

commit v2 on v1

--- a/solution.py
+++ b/solution.py
@@ -1,37 +1,38 @@
+import functools
+
 import jax
 import jax.numpy as jnp
 from jax import lax
+from jax.experimental import pallas as pl
+from jax.experimental.pallas import tpu as pltpu
 from jax.sharding import PartitionSpec as P
 
 AOB = 64
 RB = 128
 SL = 64
-
-
-def green_blocks(occ_all, virt_all, green_mask, slab_mask):
+LANES = 128
+PAIR = LANES // AOB
+
+
+def pair_masks(green_mask, slab_mask):
     blocks, width = green_mask.shape
     reach = (width - 1) // 2
     neighbour = jnp.arange(blocks)[:, None] + jnp.arange(width)[None, :] - reach
     valid = (neighbour >= 0) & (neighbour < blocks)
     near_mask = slab_mask[jnp.clip(neighbour, 0, blocks - 1)]
     pair = jnp.where(valid, green_mask, 0)
-    occ = occ_all * pair.astype(jnp.bfloat16)[:, :, None, None]
-    virt = virt_all * (pair * near_mask).astype(jnp.bfloat16)[:, :, None, None]
-    return occ, virt
-
-
-def per_device(tensor, block_mask, occ_green, virt_green, green_mask):
-    rows_dev, blocks, cols = tensor.shape
+    return pair.astype(jnp.bfloat16), (pair * near_mask).astype(jnp.bfloat16)
+
+
+def gathered_plan(tensor, masked, slab_mask, occ_green, virt_green, green_mask):
+    blocks = tensor.shape[1]
     reach = (occ_green.shape[1] - 1) // 2
-    shard = lax.axis_index(("aux", "rep"))
-    per_shard = rows_dev // RB
-    mask_rows = lax.dynamic_slice_in_dim(block_mask, shard * per_shard, per_shard, 0)
-    row_mask = jnp.repeat(mask_rows, RB, axis=0).astype(jnp.bfloat16)
-    masked = tensor * row_mask[:, :, None]
     slab = lax.all_to_all(tensor[:SL], "ao", split_axis=0, concat_axis=2, tiled=True)
     occ_all = lax.all_gather(occ_green, "ao", axis=0, tiled=True)
     virt_all = lax.all_gather(virt_green, "ao", axis=0, tiled=True)
-    occ, virt = green_blocks(occ_all, virt_all, green_mask, mask_rows[0])
+    occ_mask, virt_mask = pair_masks(green_mask, slab_mask)
+    occ = occ_all * occ_mask[:, :, None, None]
+    virt = virt_all * virt_mask[:, :, None, None]
     own = slab.shape[0]
     padded = jnp.pad(slab.reshape(own, blocks, AOB, AOB), ((0, 0), (reach, reach), (0, 0), (0, 0)))
     total = None
@@ -53,6 +54,234 @@
     return lax.psum_scatter(partial_terms, "ao", scatter_dimension=0, tiled=True)
 
 
+def swap(value, axis, step):
+    count = lax.axis_size(axis)
+    return lax.ppermute(value, axis, [(i, i ^ step) for i in range(count)])
+
+
+def contract_kernel(planes, *refs):
+    chunks = refs[:planes]
+    occ_ref, virt_ref = refs[planes : planes + 2]
+    outs = refs[planes + 2 : 2 * planes + 2]
+    even_ref, odd_ref, weight_ref, inner_ref, sums_ref = refs[2 * planes + 2 :]
+    own, blocks, cols = chunks[0].shape
+    width = virt_ref.shape[1]
+    reach = (width - 1) // 2
+    units = cols // LANES
+    pairs = own // PAIR
+    rows = planes * units
+    f32 = jnp.float32
+    for plane, chunk in enumerate(chunks):
+        for p in range(own):
+            value = chunk[p].astype(f32)
+            target = even_ref if p % 2 == 0 else odd_ref
+            for u in range(units):
+                start = (p // 2) * rows + plane * units + u
+                target[pl.ds(start, blocks, stride=pairs * rows), :] = value[
+                    :, u * LANES : (u + 1) * LANES
+                ]
+    nothing = jnp.zeros((AOB, LANES), jnp.bfloat16)
+    for m in range(blocks):
+        for k in range(width):
+            if not 0 <= m + k - reach < blocks:
+                inner_ref[m, :, k * AOB : (k + 1) * AOB, :] = jnp.zeros(
+                    (pairs // 2, AOB, 2 * LANES), jnp.bfloat16
+                )
+    for j in range(blocks):
+        at = slice(j * pairs * rows, (j + 1) * pairs * rows)
+        near = jnp.concatenate([even_ref[at, :], odd_ref[at, :]], axis=1).astype(jnp.bfloat16)
+        for k in range(width):
+            m = j + reach - k
+            if not 0 <= m < blocks:
+                continue
+            for side in range(2):
+                block = virt_ref[m, k, side]
+                for half in range(2):
+                    top = (side * 2 + half) * AOB
+                    for out_half in range(2):
+                        weight_ref[
+                            j, k, top : top + AOB, out_half * LANES : (out_half + 1) * LANES
+                        ] = block if half == out_half else nothing
+            inner = jnp.dot(near, weight_ref[j, k], preferred_element_type=f32).astype(jnp.bfloat16)
+            for pair in range(pairs):
+                for half in range(2):
+                    top = k * AOB + half * rows
+                    inner_ref[
+                        m,
+                        pair // 2,
+                        top : top + rows,
+                        (pair % 2) * LANES : (pair % 2 + 1) * LANES,
+                    ] = inner[pair * rows : (pair + 1) * rows, half * LANES : (half + 1) * LANES]
+    low = lax.broadcasted_iota(jnp.int32, (rows, LANES), 1) < AOB
+    for m in range(blocks):
+        for group in range(pairs // 2):
+            total = jnp.dot(occ_ref[m], inner_ref[m, group], preferred_element_type=f32)
+            for side in range(2):
+                lanes = slice(side * LANES, (side + 1) * LANES)
+                first, second = total[:rows, lanes], total[rows:, lanes]
+                even = jnp.where(low, first, pltpu.roll(second, AOB, 1))
+                odd = jnp.where(low, pltpu.roll(first, AOB, 1), second)
+                for part, value in enumerate((even, odd)):
+                    p = (group * 2 + side) * 2 + part
+                    for plane in range(planes):
+                        start = (m * planes + plane) * units * own + p
+                        sums_ref[pl.ds(start, units, stride=own), :] = value[
+                            plane * units : (plane + 1) * units
+                        ]
+        for plane in range(planes):
+            for u in range(units):
+                start = ((m * planes + plane) * units + u) * own
+                outs[plane][m, :, u * LANES : (u + 1) * LANES] = sums_ref[
+                    start : start + own, :
+                ].astype(jnp.bfloat16)
+
+
+def contract(chunks, occ, virt):
+    planes = len(chunks)
+    own, blocks, cols = chunks[0].shape
+    width = virt.shape[1]
+    units = cols // LANES
+    pairs = own // PAIR
+    rows = planes * units
+    whole = pl.BlockSpec(memory_space=pltpu.VMEM)
+    flops = 2 * blocks * width * own * AOB * AOB * AOB * 4
+    return pl.pallas_call(
+        functools.partial(contract_kernel, planes),
+        out_shape=[jax.ShapeDtypeStruct((blocks, own, cols), jnp.bfloat16)] * planes,
+        in_specs=[whole] * (planes + 2),
+        out_specs=[whole] * planes,
+        scratch_shapes=[
+            pltpu.VMEM((blocks * pairs * rows, LANES), jnp.float32),
+            pltpu.VMEM((blocks * pairs * rows, LANES), jnp.float32),
+            pltpu.VMEM((blocks, width, 2 * LANES, 2 * LANES), jnp.bfloat16),
+            pltpu.VMEM((blocks, pairs // 2, width * AOB, 2 * LANES), jnp.bfloat16),
+            pltpu.VMEM((blocks * rows * own, LANES), jnp.float32),
+        ],
+        compiler_params=pltpu.CompilerParams(vmem_limit_bytes=40 * 1024 * 1024),
+        cost_estimate=pl.CostEstimate(flops=flops, bytes_accessed=3 << 20, transcendentals=0),
+        name="contract_slab",
+    )(*chunks, occ, virt)
+
+
+def response_kernel(count, *refs):
+    parts = refs[:count]
+    masked_ref, out_ref = refs[count:]
+    step = pl.program_id(0)
+
+    @pl.when(step == 0)
+    def _():
+        out_ref[...] = jnp.zeros_like(out_ref)
+
+    total = None
+    for m in range(masked_ref.shape[0]):
+        left = jnp.concatenate([part[m] for part in parts], axis=0)
+        term = lax.dot_general(
+            left, masked_ref[m], (((1,), (1,)), ((), ())), preferred_element_type=jnp.float32
+        )
+        total = term if total is None else total + term
+    out_ref[...] += total
+
+
+def response(parts, masked):
+    blocks, own, cols = parts[0].shape
+    rows_dev = masked.shape[1]
+    count = len(parts)
+    per_step = 2
+    return pl.pallas_call(
+        functools.partial(response_kernel, count),
+        grid=(blocks // per_step,),
+        out_shape=jax.ShapeDtypeStruct((count * own, rows_dev), jnp.float32),
+        in_specs=[pl.BlockSpec((per_step, own, cols), lambda s: (s, 0, 0))] * count
+        + [pl.BlockSpec((per_step, rows_dev, cols), lambda s: (s, 0, 0))],
+        out_specs=pl.BlockSpec((count * own, rows_dev), lambda s: (0, 0)),
+        compiler_params=pltpu.CompilerParams(vmem_limit_bytes=24 * 1024 * 1024),
+        cost_estimate=pl.CostEstimate(
+            flops=2 * count * own * rows_dev * blocks * cols,
+            bytes_accessed=2 * rows_dev * blocks * cols,
+            transcendentals=0,
+        ),
+        name="response_terms",
+    )(*parts, masked)
+
+
+def swapped_plan(tensor, masked, slab_mask, occ_green, virt_green, green_mask):
+    planes = lax.axis_size("ao")
+    steps = range(1, planes)
+    z = lax.axis_index("ao")
+    core = lax.axis_index("rep")
+    shard = lax.axis_index(("aux", "rep"))
+    own = SL // planes
+    cols = tensor.shape[2]
+    units = cols // LANES
+    blocks = tensor.shape[1]
+
+    def rows_of(plane):
+        return lax.dynamic_slice_in_dim(tensor, plane * own, own, 0)
+
+    chunks = [rows_of(z)] + [swap(rows_of(z ^ k), "ao", k) for k in steps]
+    mine = jnp.where(core == 0, occ_green, virt_green)
+    stacked = jnp.stack([mine] + [swap(mine, "ao", k) for k in steps])
+    order = jnp.arange(planes) ^ z
+    mine_all = stacked[order].reshape((blocks,) + mine.shape[1:])
+    other_all = swap(mine_all, "rep", 1)
+    occ_mask, virt_mask = pair_masks(green_mask, slab_mask)
+    occ = jnp.where(core == 0, mine_all, other_all) * occ_mask[:, :, None, None]
+    virt = jnp.where(core == 0, other_all, mine_all) * virt_mask[:, :, None, None]
+    place = jnp.arange(AOB)
+    source = (
+        (z ^ (place // units % planes)) * (AOB // planes)
+        + PAIR * (place % units)
+        + place // (planes * units)
+    )
+    select = (source[:, None] == jnp.arange(AOB)[None, :]).astype(jnp.bfloat16)
+    occ = jnp.einsum("ai,mkij->mkaj", select, occ)
+    occ = jnp.einsum("mkaj,bj->makb", occ, select).reshape(blocks, AOB, -1)
+    virt = jnp.stack(
+        [
+            jnp.pad(virt, ((0, 0), (0, 0), (0, 0), (0, LANES - AOB))),
+            jnp.pad(virt, ((0, 0), (0, 0), (0, 0), (LANES - AOB, 0))),
+        ],
+        axis=2,
+    )
+    sums = contract(chunks, occ, virt)
+    terms = []
+    for k in range(planes):
+        near = sums[k] if k == 0 else swap(sums[k], "ao", k)
+        far = swap(near, "aux", 1)
+        terms.append(
+            response([near, swap(near, "rep", 1), far, swap(far, "rep", 1)], masked).reshape(
+                planes, own, -1
+            )
+        )
+    terms = jnp.stack(terms)
+
+    def block_for(k):
+        kept = lax.dynamic_index_in_dim(terms, shard ^ z ^ k, 1, keepdims=False)
+        return jnp.stack([kept[p ^ k] for p in range(planes)])
+
+    total = block_for(0)
+    for k in steps:
+        total = total + swap(block_for(k).astype(jnp.bfloat16), "ao", k).astype(jnp.float32)
+    return total[order].reshape(SL, -1)
+
+
+def per_device(tensor, block_mask, occ_green, virt_green, green_mask):
+    rows_dev, blocks, cols = tensor.shape
+    shard = lax.axis_index(("aux", "rep"))
+    per_shard = rows_dev // RB
+    mask_rows = lax.dynamic_slice_in_dim(block_mask, shard * per_shard, per_shard, 0)
+    row_mask = jnp.repeat(mask_rows, RB, axis=0).astype(jnp.bfloat16)
+    planes = lax.axis_size("ao")
+    simple = planes == 4 and lax.axis_size("aux") == 2 and lax.axis_size("rep") == 2
+    if simple and cols * planes == AOB * AOB and SL // planes % 16 == 0:
+        masked = jnp.swapaxes(tensor, 0, 1) * row_mask.T[:, :, None]
+        plan = swapped_plan
+    else:
+        masked = tensor * row_mask[:, :, None]
+        plan = gathered_plan
+    return plan(tensor, masked, mask_rows[0], occ_green, virt_green, green_mask)
+
+
 def solution(mesh):
     return jax.shard_map(
         per_device,

time: 223 us -> 108 us (0.48)
  blocking collectives: 72.6 us -> 0 us
  local copies, waits for them, and re-layouts: 49.6 us -> 7.82 us
  matrix products: 25.3 us -> 0.72 us
  starting transfers between devices: 6.36 us -> 27.1 us
  Pallas kernels: 0 us -> 14.4 us
  between operations: 13.5 us -> 0.26 us
    ppermute x0 -> x25, waiting for transfers between devices: none -> 49.4 us  [swap(): return lax.ppermute(value, axis, [(i, i ^ step) for i in range(count)])]
    all_gather x2 -> x0, blocking collectives: 48.1 us -> none  [the longest x1 32.9 us: per_device(): virt_all = lax.all_gather(virt_green, 'ao', axis=0, tiled=True)]
    all_gather x1 -> x0, waiting for transfers between devices: 29.1 us -> none  [per_device(): sums = lax.all_gather(back, ('aux', 'rep'), axis=0, tiled=True)]
    ppermute x0 -> x25, starting transfers between devices: none -> 27.1 us  [swap(): return lax.ppermute(value, axis, [(i, i ^ step) for i in range(count)])]
    dot_general x4 -> x1, matrix products: 25.3 us -> 0.72 us  [swapped_plan(): occ = jnp.einsum('mkaj,bj->makb', occ, select).reshape(blocks, AOB, -1)]
    all_to_all x1 -> x0, blocking collectives: 24.5 us -> none  [per_device(): lax.all_to_all(own_sums, 'ao', split_axis=2, concat_axis=0, tiled=True)]
    reduce_scatter x1 -> x0, waiting for transfers between devices: 19.7 us -> none  [per_device(): lax.psum_scatter(partial_terms, 'ao', scatter_dimension=0, tiled=True)]
    reshape x2 -> x1, local copies, waits for them, and re-layouts: 16.9 us -> 0.2 us  [swapped_plan(): occ = jnp.einsum('mkaj,bj->makb', occ, select).reshape(blocks, AOB, -1)]
  transfers between devices with their start and end apart: 3 -> 25, of which waited for: 2 -> 9; matrix products, arithmetic and copies ran while one was open for 3% -> 11% of each run, Pallas kernels for 0% -> 7%
where the time goes in v2:
time: 108 us
  waiting for transfers between devices  49.4 us (46%)
  starting transfers between devices  27.1 us (25%)
  Pallas kernels  14.4 us (13%)
  other arithmetic  8.01 us (7%)
  local copies, waits for them, and re-layouts  7.82 us (7%)
    ppermute x25, waiting for transfers between devices, swap(): return lax.ppermute(value, axis, [(i, i ^ step) for i in range(count)])  49.4 us
    ppermute x25, starting transfers between devices, swap(): return lax.ppermute(value, axis, [(i, i ^ step) for i in range(count)])  27.1 us
    pallas_call x4, Pallas kernels, response(): pl.pallas_call(functools.partial(response_kernel, count), grid=(blocks //...  11 us
    mul x1, other arithmetic, per_device(): masked = jnp.swapaxes(tensor, 0, 1) * row_mask.T[:, :, None]  5.97 us
    pallas_call x1, Pallas kernels, contract(): pl.pallas_call(functools.partial(contract_kernel, planes), out_shape=[jax...  3.48 us
    unnamed x9, local copies, waits for them, and re-layouts  2.65 us
  transfers between devices with their start and end apart: 25, of which 9 were waited for; matrix products, arithmetic and copies ran while one was open for 11% of the time, Pallas kernels for 7%

profile of v2, /device:TPU:0, one launch (start us, length us, event | category | flops | bytes accessed | tf_op | source)
XLA Modules:
  0.0 107.8 jit_solution(15446089471566099435)
XLA Ops:
  0.0 0.9 broadcast_select_fusion
  0.9 3.1 %collective-permute-start.3 = (bf16[2,3,64,64]{3,2,1,0:T(8,128)(2,1)S(1)}, bf16[2,3,64,64]{3,2,1,0:T(8,128)(2,1)S(1)}, u32[]{:S(2)}, u32[]{:S(2)}) collective-permute-start(bf16[2,3,64,64]{3,2,1,0:T(8,128)(2,1)S(1)} %broadcast_select_fusion), channel_id=1, source_target_pairs={{0,4},{4,0},{8,12},{12,8},{1,5},{5,1},{9,13},{13,9},{2,6},{6,2},{1... | collective-permute-start | bytes 147464 | tf_op jit(solution)/shard_map/ppermute | solution.py:59
  4.0 2.6 %collective-permute-start.4 = (bf16[2,3,64,64]{3,2,1,0:T(8,128)(2,1)S(1)}, bf16[2,3,64,64]{3,2,1,0:T(8,128)(2,1)S(1)}, u32[]{:S(2)}, u32[]{:S(2)}) collective-permute-start(bf16[2,3,64,64]{3,2,1,0:T(8,128)(2,1)S(1)} %broadcast_select_fusion), channel_id=1, source_target_pairs={{0,8},{4,12},{8,0},{12,4},{1,9},{5,13},{9,1},{13,5},{2,10},{6,14},... | collective-permute-start | bytes 147464 | tf_op jit(solution)/shard_map/ppermute | solution.py:59
  6.6 2.0 %constant_dynamic-slice_fusion.1 = (bf16[16,8,1024]{2,1,0:T(8,128)(2,1)S(1)}, bf16[16,8,1024]{2,1,0:T(8,128)(2,1)S(1)}, bf16[16,8,1024]{2,1,0:T(8,128)(2,1)}, bf16[16,8,1024]{2,1,0:T(8,128)(2,1)S(1)}) fusion(bf16[256,8,1024]{2,1,0:T(8,128)(2,1)} %param.5, s32[]{:T(128)S(6)} %select_n.111, s32[]{:T(128)S(6)} %select_n.110, s32[]{:T(128)S(6)} %select_n.109, ...), kind=kLoop, calls=%fused_computation.55 | loop fusion | bytes 2097168 | tf_op jit(solution)/shard_map/dynamic_slice | solution.py:219
  8.6 0.9 collective-permute-start
  9.5 3.5 %collective-permute-start.1 = (bf16[16,8,1024]{2,1,0:T(8,128)(2,1)S(1)}, bf16[16,8,1024]{2,1,0:T(8,128)(2,1)S(1)}, u32[]{:S(2)}, u32[]{:S(2)}) collective-permute-start(bf16[16,8,1024]{2,1,0:T(8,128)(2,1)S(1)} %get-tuple-element.16), channel_id=1, source_target_pairs={{0,8},{4,12},{8,0},{12,4},{1,9},{5,13},{9,1},{13,5},{2,10},{6,14},... | collective-permute-start | bytes 786440 | tf_op jit(solution)/shard_map/ppermute | solution.py:59
  13.0 0.7 fusion.28
  13.7 0.1 reshape.146
  13.8 0.7 gather_fusion.1
  14.5 0.1 reshape.145
  14.6 0.1 copy.10
  14.7 0.1 pad_maximum_fusion.1
  14.8 0.6 gather_fusion
  15.6 1.7 %collective-permute-done.6 = bf16[8,3,64,64]{3,2,1,0:T(8,128)(2,1)S(1)} collective-permute-done((bf16[8,3,64,64]{3,2,1,0:T(8,128)(2,1)S(1)}, bf16[8,3,64,64]{3,2,1,0:T(8,128)(2,1)S(1)}, u32[]{:S(2)}, u32[]{:S(2)}) %collective-permute-start.6) | collective-permute-done | bytes 196640 | tf_op jit(solution)/shard_map/ppermute | solution.py:59
  17.3 0.7 fusion
  18.0 0.2 copy.12.refs_4_
  18.2 0.1 select_multiply_fusion
  18.3 0.2 pad_bitcast_fusion.1
  18.6 3.7 %collective-permute-done.refs_1_ = bf16[16,8,1024]{2,1,0:T(8,128)(2,1)S(1)} collective-permute-done((bf16[16,8,1024]{2,1,0:T(8,128)(2,1)}, bf16[16,8,1024]{2,1,0:T(8,128)(2,1)S(1)}, u32[]{:S(2)}, u32[]{:S(2)}) %collective-permute-start) | collective-permute-done | bytes 262176 | tf_op jit(solution)/shard_map/ppermute | solution.py:59
  22.3 11.2 %collective-permute-done.1.refs_2_ = bf16[16,8,1024]{2,1,0:T(8,128)(2,1)S(1)} collective-permute-done((bf16[16,8,1024]{2,1,0:T(8,128)(2,1)S(1)}, bf16[16,8,1024]{2,1,0:T(8,128)(2,1)S(1)}, u32[]{:S(2)}, u32[]{:S(2)}) %collective-permute-start.1) | collective-permute-done | bytes 262176 | tf_op jit(solution)/shard_map/ppermute | solution.py:59
  33.5 3.5 %contract_slab.1 = (bf16[8,16,1024]{2,1,0:T(8,128)(2,1)S(1)}, bf16[8,16,1024]{2,1,0:T(8,128)(2,1)S(1)}, bf16[8,16,1024]{2,1,0:T(8,128)(2,1)S(1)}, bf16[8,16,1024]{2,1,0:T(8,128)(2,1)S(1)}) custom-call(bf16[16,8,1024]{2,1,0:T(8,128)(2,1)S(1)} %get-tuple-element.18.refs_0_, bf16[16,8,1024]{2,1,0:T(8,128)(2,1)S(1)} %collective-permute-done.refs_1_, ...), custom_call_target="tpu_custom_call" | custom-call | flops 805306368 | bytes 3145728 | tf_op jit(solution)/shard_map/contract_slab/pallas_call | solution.py:148
  37.0 1.5 %collective-permute-start.8 = (bf16[8,16,1024]{2,1,0:T(8,128)(2,1)S(1)}, bf16[8,16,1024]{2,1,0:T(8,128)(2,1)S(1)}, u32[]{:S(2)}, u32[]{:S(2)}) collective-permute-start(bf16[8,16,1024]{2,1,0:T(8,128)(2,1)S(1)} %get-tuple-element.9.refs_0_), channel_id=1, source_target_pairs={{0,2},{2,0},{1,3},{3,1},{4,6},{6,4},{5,7},{7,5},{8,10},{10,8},{9,1... | collective-permute-start | bytes 786440 | tf_op jit(solution)/shard_map/ppermute | solution.py:59
  38.5 5.0 %collective-permute-start.10 = (bf16[8,16,1024]{2,1,0:T(8,128)(2,1)S(1)}, bf16[8,16,1024]{2,1,0:T(8,128)(2,1)S(1)}, u32[]{:S(2)}, u32[]{:S(2)}) collective-permute-start(bf16[8,16,1024]{2,1,0:T(8,128)(2,1)S(1)} %get-tuple-element.10), channel_id=1, source_target_pairs={{0,4},{4,0},{8,12},{12,8},{1,5},{5,1},{9,13},{13,9},{2,6},{6,2},{1... | collective-permute-start | bytes 786440 | tf_op jit(solution)/shard_map/ppermute | solution.py:59
  43.6 1.0 collective-permute-start.14
  44.6 1.5 %collective-permute-start.18 = (bf16[8,16,1024]{2,1,0:T(8,128)(2,1)S(1)}, bf16[8,16,1024]{2,1,0:T(8,128)(2,1)S(1)}, u32[]{:S(2)}, u32[]{:S(2)}) collective-permute-start(bf16[8,16,1024]{2,1,0:T(8,128)(2,1)S(1)} %get-tuple-element.12), channel_id=1, source_target_pairs={{0,12},{4,8},{8,4},{12,0},{1,13},{5,9},{9,5},{13,1},{2,14},{6,10},... | collective-permute-start | bytes 786440 | tf_op jit(solution)/shard_map/ppermute | solution.py:59
  46.0 0.2 collective-permute-start.9
  46.3 4.5 %collective-permute-done.10.refs_0_ = bf16[8,16,1024]{2,1,0:T(8,128)(2,1)S(1)} collective-permute-done((bf16[8,16,1024]{2,1,0:T(8,128)(2,1)S(1)}, bf16[8,16,1024]{2,1,0:T(8,128)(2,1)S(1)}, u32[]{:S(2)}, u32[]{:S(2)}) %collective-permute-start.10) | collective-permute-done | bytes 262176 | tf_op jit(solution)/shard_map/ppermute | solution.py:59
  50.7 0.6 collective-permute-start.12
  51.3 13.5 %collective-permute-done.14.refs_0_ = bf16[8,16,1024]{2,1,0:T(8,128)(2,1)S(1)} collective-permute-done((bf16[8,16,1024]{2,1,0:T(8,128)(2,1)S(1)}, bf16[8,16,1024]{2,1,0:T(8,128)(2,1)S(1)}, u32[]{:S(2)}, u32[]{:S(2)}) %collective-permute-start.14) | collective-permute-done | bytes 262176 | tf_op jit(solution)/shard_map/ppermute | solution.py:59
  64.8 0.5 collective-permute-start.16
  65.3 1.5 %collective-permute-start.20 = (bf16[8,16,1024]{2,1,0:T(8,128)(2,1)S(1)}, bf16[8,16,1024]{2,1,0:T(8,128)(2,1)S(1)}, u32[]{:S(2)}, u32[]{:S(2)}) collective-permute-start(bf16[8,16,1024]{2,1,0:T(8,128)(2,1)S(1)} %collective-permute-done.18.refs_0_), channel_id=1, source_target_pairs={{0,2},{2,0},{1,3},{3,1},{4,6},{6,4},{5,7},{7,5},{8,10},{10,8},{9,1... | collective-permute-start | bytes 786440 | tf_op jit(solution)/shard_map/ppermute | solution.py:59
  66.9 0.5 collective-permute-start.19
  67.4 0.1 collective-permute-start.13
  67.5 6.5 %collective-permute-done.16.refs_2_ = bf16[8,16,1024]{2,1,0:T(8,128)(2,1)S(1)} collective-permute-done((bf16[8,16,1024]{2,1,0:T(8,128)(2,1)S(1)}, bf16[8,16,1024]{2,1,0:T(8,128)(2,1)S(1)}, u32[]{:S(2)}, u32[]{:S(2)}) %collective-permute-start.16) | collective-permute-done | bytes 262176 | tf_op jit(solution)/shard_map/ppermute | solution.py:59
  74.0 3.9 %collective-permute-done.20.refs_2_ = bf16[8,16,1024]{2,1,0:T(8,128)(2,1)S(1)} collective-permute-done((bf16[8,16,1024]{2,1,0:T(8,128)(2,1)S(1)}, bf16[8,16,1024]{2,1,0:T(8,128)(2,1)S(1)}, u32[]{:S(2)}, u32[]{:S(2)}) %collective-permute-start.20) | collective-permute-done | bytes 262176 | tf_op jit(solution)/shard_map/ppermute | solution.py:59
  78.0 6.0 %bitcast_multiply_fusion.refs_4_ = bf16[8,256,1024]{2,1,0:T(8,128)(2,1)} fusion(bf16[256,8,1024]{2,1,0:T(8,128)(2,1)S(1)} %copy-done.2, bf16[8,256]{1,0:T(8,128)(2,1)S(1)} %broadcast_bitcast_fusion), kind=kLoop, calls=%fused_computation.3 | loop fusion | flops 2097152 | bytes 8392704 | tf_op jit(solution)/shard_map/mul | solution.py:277
  83.9 2.2 %copy-done = bf16[8,256,1024]{2,1,0:T(8,128)(2,1)S(1)} copy-done((bf16[8,256,1024]{2,1,0:T(8,128)(2,1)S(1)}, bf16[8,256,1024]{2,1,0:T(8,128)(2,1)}, u32[]{:S(2)}) %copy-start) | copy-done | bytes 4194328
  86.1 1.8 %response_terms.4 = f32[64,256]{1,0:T(8,128)S(1)} custom-call(bf16[8,16,1024]{2,1,0:T(8,128)(2,1)S(1)} %get-tuple-element.9.refs_0_, bf16[8,16,1024]{2,1,0:T(8,128)(2,1)S(1)} %collective-permute-done.7.refs_1_, bf16[8,16,1024]{2,1,0:T(8,128)(2,1)S(1)} %collective-permute-done.8.refs_2_, bf16[8,16,1024]{2,1,0:T(8,128)(2,1)S(1)} %collective-permute-done.9.refs_3_, ...), custom_call_target="tpu_custom_call" | custom-call | flops 268435456 | bytes 4194304 | tf_op jit(solution)/shard_map/response_terms/pallas_call | solution.py:190
  88.0 0.4 copy-done.1
  88.3 3.0 %response_terms.5 = f32[64,256]{1,0:T(8,128)S(1)} custom-call(bf16[8,16,1024]{2,1,0:T(8,128)(2,1)S(1)} %collective-permute-done.10.refs_0_, bf16[8,16,1024]{2,1,0:T(8,128)(2,1)S(1)} %collective-permute-done.11.refs_1_, bf16[8,16,1024]{2,1,0:T(8,128)(2,1)S(1)} %collective-permute-done.12.refs_2_, bf16[8,16,1024]{2,1,0:T(8,128)(2,1)} %collective-permute-done.13.refs_3_, ...), custom_call_target="tpu_custom_call" | custom-call | flops 268435456 | bytes 4194304 | tf_op jit(solution)/shard_map/response_terms/pallas_call | solution.py:190
  91.4 3.1 %response_terms.6 = f32[64,256]{1,0:T(8,128)S(1)} custom-call(bf16[8,16,1024]{2,1,0:T(8,128)(2,1)S(1)} %collective-permute-done.14.refs_0_, bf16[8,16,1024]{2,1,0:T(8,128)(2,1)S(1)} %collective-permute-done.15.refs_1_, bf16[8,16,1024]{2,1,0:T(8,128)(2,1)S(1)} %collective-permute-done.16.refs_2_, bf16[8,16,1024]{2,1,0:T(8,128)(2,1)} %collective-permute-done.17.refs_3_, ...), custom_call_target="tpu_custom_call" | custom-call | flops 268435456 | bytes 4194304 | tf_op jit(solution)/shard_map/response_terms/pallas_call | solution.py:190
  94.5 3.1 %response_terms.7 = f32[64,256]{1,0:T(8,128)S(1)} custom-call(bf16[8,16,1024]{2,1,0:T(8,128)(2,1)S(1)} %collective-permute-done.18.refs_0_, bf16[8,16,1024]{2,1,0:T(8,128)(2,1)S(1)} %collective-permute-done.19.refs_1_, bf16[8,16,1024]{2,1,0:T(8,128)(2,1)S(1)} %collective-permute-done.20.refs_2_, bf16[8,16,1024]{2,1,0:T(8,128)(2,1)} %collective-permute-done.21.refs_3_, ...), custom_call_target="tpu_custom_call" | custom-call | flops 268435456 | bytes 4194304 | tf_op jit(solution)/shard_map/response_terms/pallas_call | solution.py:190
  97.6 0.6 collective-permute-start.22
  98.3 2.6 %collective-permute-start.23 = (bf16[4,16,256]{2,1,0:T(8,128)(2,1)S(1)}, bf16[4,16,256]{2,1,0:T(8,128)(2,1)S(1)}, u32[]{:S(2)}, u32[]{:S(2)}) collective-permute-start(bf16[4,16,256]{2,1,0:T(8,128)(2,1)S(1)} %pad_maximum_fusion.4), channel_id=1, source_target_pairs={{0,8},{4,12},{8,0},{12,4},{1,9},{5,13},{9,1},{13,5},{2,10},{6,14},... | collective-permute-start | bytes 98312 | tf_op jit(solution)/shard_map/ppermute | solution.py:59
  100.9 1.3 %collective-permute-start.24 = (bf16[4,16,256]{2,1,0:T(8,128)(2,1)S(1)}, bf16[4,16,256]{2,1,0:T(8,128)(2,1)S(1)}, u32[]{:S(2)}, u32[]{:S(2)}) collective-permute-start(bf16[4,16,256]{2,1,0:T(8,128)(2,1)S(1)} %pad_maximum_fusion.5), channel_id=1, source_target_pairs={{0,12},{4,8},{8,4},{12,0},{1,13},{5,9},{9,5},{13,1},{2,14},{6,10},... | collective-permute-start | bytes 98312 | tf_op jit(solution)/shard_map/ppermute | solution.py:59
  102.2 1.4 %collective-permute-done.23 = bf16[4,16,256]{2,1,0:T(8,128)(2,1)S(1)} collective-permute-done((bf16[4,16,256]{2,1,0:T(8,128)(2,1)S(1)}, bf16[4,16,256]{2,1,0:T(8,128)(2,1)S(1)}, u32[]{:S(2)}, u32[]{:S(2)}) %collective-permute-start.23) | collective-permute-done | bytes 32800 | tf_op jit(solution)/shard_map/ppermute | solution.py:59
  103.6 3.0 %collective-permute-done.24 = bf16[4,16,256]{2,1,0:T(8,128)(2,1)S(1)} collective-permute-done((bf16[4,16,256]{2,1,0:T(8,128)(2,1)S(1)}, bf16[4,16,256]{2,1,0:T(8,128)(2,1)S(1)}, u32[]{:S(2)}, u32[]{:S(2)}) %collective-permute-start.24) | collective-permute-done | bytes 32800 | tf_op jit(solution)/shard_map/ppermute | solution.py:59
  106.6 1.2 %gather_fusion.2 = f32[4,16,256]{2,1,0:T(8,128)} fusion(f32[4,16,256]{2,1,0:T(8,128)S(1)} %fusion.10, s32[1024]{0:T(1024)S(1)} %pad_clamp_fusion.1), kind=kCustom, calls=%fused_computation.2 | custom fusion | bytes 131088 | tf_op jit(solution)/shard_map/gather | solution.py:265
  (48 shorter events, 0.5 us)
Async XLA Ops:
  0.0 14.6 %copy-start.3 = (s32[8,3]{0,1:T(4,128)S(1)}, s32[8,3]{0,1:T(4,128)}, u32[]{:S(2)}) copy-start(s32[8,3]{0,1:T(4,128)} %param.9) | copy-start | bytes 292
  0.9 13.7 %collective-permute-start.3 = (bf16[2,3,64,64]{3,2,1,0:T(8,128)(2,1)S(1)}, bf16[2,3,64,64]{3,2,1,0:T(8,128)(2,1)S(1)}, u32[]{:S(2)}, u32[]{:S(2)}) collective-permute-start(bf16[2,3,64,64]{3,2,1,0:T(8,128)(2,1)S(1)} %broadcast_select_fusion), channel_id=1, source_target_pairs={{0,4},{4,0},{8,12},{12,8},{1,5},{5,1},{9,13},{13,9},{2,6},{6,2},{1... | collective-permute-start | bytes 147464 | tf_op jit(solution)/shard_map/ppermute | solution.py:59
  4.0 10.7 %collective-permute-start.4 = (bf16[2,3,64,64]{3,2,1,0:T(8,128)(2,1)S(1)}, bf16[2,3,64,64]{3,2,1,0:T(8,128)(2,1)S(1)}, u32[]{:S(2)}, u32[]{:S(2)}) collective-permute-start(bf16[2,3,64,64]{3,2,1,0:T(8,128)(2,1)S(1)} %broadcast_select_fusion), channel_id=1, source_target_pairs={{0,8},{4,12},{8,0},{12,4},{1,9},{5,13},{9,1},{13,5},{2,10},{6,14},... | collective-permute-start | bytes 147464 | tf_op jit(solution)/shard_map/ppermute | solution.py:59
  6.6 8.1 %collective-permute-start.5 = (bf16[2,3,64,64]{3,2,1,0:T(8,128)(2,1)S(1)}, bf16[2,3,64,64]{3,2,1,0:T(8,128)(2,1)S(1)}, u32[]{:S(2)}, u32[]{:S(2)}) collective-permute-start(bf16[2,3,64,64]{3,2,1,0:T(8,128)(2,1)S(1)} %broadcast_select_fusion), channel_id=1, source_target_pairs={{0,12},{4,8},{8,4},{12,0},{1,13},{5,9},{9,5},{13,1},{2,14},{6,10},... | collective-permute-start | bytes 147464 | tf_op jit(solution)/shard_map/ppermute | solution.py:59
  8.6 13.7 %collective-permute-start = (bf16[16,8,1024]{2,1,0:T(8,128)(2,1)}, bf16[16,8,1024]{2,1,0:T(8,128)(2,1)S(1)}, u32[]{:S(2)}, u32[]{:S(2)}) collective-permute-start(bf16[16,8,1024]{2,1,0:T(8,128)(2,1)} %get-tuple-element.17), channel_id=1, source_target_pairs={{0,4},{4,0},{8,12},{12,8},{1,5},{5,1},{9,13},{13,9},{2,6},{6,2},{1... | collective-permute-start | bytes 786440 | tf_op jit(solution)/shard_map/ppermute | solution.py:59
  9.5 24.0 %collective-permute-start.1 = (bf16[16,8,1024]{2,1,0:T(8,128)(2,1)S(1)}, bf16[16,8,1024]{2,1,0:T(8,128)(2,1)S(1)}, u32[]{:S(2)}, u32[]{:S(2)}) collective-permute-start(bf16[16,8,1024]{2,1,0:T(8,128)(2,1)S(1)} %get-tuple-element.16), channel_id=1, source_target_pairs={{0,8},{4,12},{8,0},{12,4},{1,9},{5,13},{9,1},{13,5},{2,10},{6,14},... | collective-permute-start | bytes 786440 | tf_op jit(solution)/shard_map/ppermute | solution.py:59
  14.7 18.8 %collective-permute-start.2 = (bf16[16,8,1024]{2,1,0:T(8,128)(2,1)S(1)}, bf16[16,8,1024]{2,1,0:T(8,128)(2,1)S(1)}, u32[]{:S(2)}, u32[]{:S(2)}) collective-permute-start(bf16[16,8,1024]{2,1,0:T(8,128)(2,1)S(1)} %get-tuple-element.15), channel_id=1, source_target_pairs={{0,12},{4,8},{8,4},{12,0},{1,13},{5,9},{9,5},{13,1},{2,14},{6,10},... | collective-permute-start | bytes 786440 | tf_op jit(solution)/shard_map/ppermute | solution.py:59
  15.5 1.8 %collective-permute-start.6 = (bf16[8,3,64,64]{3,2,1,0:T(8,128)(2,1)S(1)}, bf16[8,3,64,64]{3,2,1,0:T(8,128)(2,1)S(1)}, u32[]{:S(2)}, u32[]{:S(2)}) collective-permute-start(bf16[8,3,64,64]{3,2,1,0:T(8,128)(2,1)S(1)} %bitcast.78), channel_id=1, source_target_pairs={{0,1},{1,0},{2,3},{3,2},{4,5},{5,4},{6,7},{7,6},{8,9},{9,8},{10,11... | collective-permute-start | bytes 589832 | tf_op jit(solution)/shard_map/ppermute | solution.py:59
  18.2 59.8 %copy-start.2 = (bf16[256,8,1024]{2,1,0:T(8,128)(2,1)S(1)}, bf16[256,8,1024]{2,1,0:T(8,128)(2,1)}, u32[]{:S(2)}) copy-start(bf16[256,8,1024]{2,1,0:T(8,128)(2,1)} %param.5) | copy-start | bytes 12582916
  37.0 9.1 %collective-permute-start.8 = (bf16[8,16,1024]{2,1,0:T(8,128)(2,1)S(1)}, bf16[8,16,1024]{2,1,0:T(8,128)(2,1)S(1)}, u32[]{:S(2)}, u32[]{:S(2)}) collective-permute-start(bf16[8,16,1024]{2,1,0:T(8,128)(2,1)S(1)} %get-tuple-element.9.refs_0_), channel_id=1, source_target_pairs={{0,2},{2,0},{1,3},{3,1},{4,6},{6,4},{5,7},{7,5},{8,10},{10,8},{9,1... | collective-permute-start | bytes 786440 | tf_op jit(solution)/shard_map/ppermute | solution.py:59
  38.5 12.2 %collective-permute-start.10 = (bf16[8,16,1024]{2,1,0:T(8,128)(2,1)S(1)}, bf16[8,16,1024]{2,1,0:T(8,128)(2,1)S(1)}, u32[]{:S(2)}, u32[]{:S(2)}) collective-permute-start(bf16[8,16,1024]{2,1,0:T(8,128)(2,1)S(1)} %get-tuple-element.10), channel_id=1, source_target_pairs={{0,4},{4,0},{8,12},{12,8},{1,5},{5,1},{9,13},{13,9},{2,6},{6,2},{1... | collective-permute-start | bytes 786440 | tf_op jit(solution)/shard_map/ppermute | solution.py:59
  43.5 7.7 %collective-permute-start.7 = (bf16[8,16,1024]{2,1,0:T(8,128)(2,1)S(1)}, bf16[8,16,1024]{2,1,0:T(8,128)(2,1)S(1)}, u32[]{:S(2)}, u32[]{:S(2)}) collective-permute-start(bf16[8,16,1024]{2,1,0:T(8,128)(2,1)S(1)} %get-tuple-element.9.refs_0_), channel_id=1, source_target_pairs={{0,1},{1,0},{2,3},{3,2},{4,5},{5,4},{6,7},{7,6},{8,9},{9,8},{10,11... | collective-permute-start | bytes 786440 | tf_op jit(solution)/shard_map/ppermute | solution.py:59
  43.6 21.3 %collective-permute-start.14 = (bf16[8,16,1024]{2,1,0:T(8,128)(2,1)S(1)}, bf16[8,16,1024]{2,1,0:T(8,128)(2,1)S(1)}, u32[]{:S(2)}, u32[]{:S(2)}) collective-permute-start(bf16[8,16,1024]{2,1,0:T(8,128)(2,1)S(1)} %get-tuple-element.11), channel_id=1, source_target_pairs={{0,8},{4,12},{8,0},{12,4},{1,9},{5,13},{9,1},{13,5},{2,10},{6,14},... | collective-permute-start | bytes 786440 | tf_op jit(solution)/shard_map/ppermute | solution.py:59
  44.6 20.8 %collective-permute-start.18 = (bf16[8,16,1024]{2,1,0:T(8,128)(2,1)S(1)}, bf16[8,16,1024]{2,1,0:T(8,128)(2,1)S(1)}, u32[]{:S(2)}, u32[]{:S(2)}) collective-permute-start(bf16[8,16,1024]{2,1,0:T(8,128)(2,1)S(1)} %get-tuple-element.12), channel_id=1, source_target_pairs={{0,12},{4,8},{8,4},{12,0},{1,13},{5,9},{9,5},{13,1},{2,14},{6,10},... | collective-permute-start | bytes 786440 | tf_op jit(solution)/shard_map/ppermute | solution.py:59
  46.0 20.9 %collective-permute-start.9 = (bf16[8,16,1024]{2,1,0:T(8,128)(2,1)S(1)}, bf16[8,16,1024]{2,1,0:T(8,128)(2,1)S(1)}, u32[]{:S(2)}, u32[]{:S(2)}) collective-permute-start(bf16[8,16,1024]{2,1,0:T(8,128)(2,1)S(1)} %collective-permute-done.8.refs_2_), channel_id=1, source_target_pairs={{0,1},{1,0},{2,3},{3,2},{4,5},{5,4},{6,7},{7,6},{8,9},{9,8},{10,11... | collective-permute-start | bytes 786440 | tf_op jit(solution)/shard_map/ppermute | solution.py:59
  50.7 16.2 %collective-permute-start.12 = (bf16[8,16,1024]{2,1,0:T(8,128)(2,1)S(1)}, bf16[8,16,1024]{2,1,0:T(8,128)(2,1)S(1)}, u32[]{:S(2)}, u32[]{:S(2)}) collective-permute-start(bf16[8,16,1024]{2,1,0:T(8,128)(2,1)S(1)} %collective-permute-done.10.refs_0_), channel_id=1, source_target_pairs={{0,2},{2,0},{1,3},{3,1},{4,6},{6,4},{5,7},{7,5},{8,10},{10,8},{9,1... | collective-permute-start | bytes 786440 | tf_op jit(solution)/shard_map/ppermute | solution.py:59
  51.3 16.1 %collective-permute-start.11 = (bf16[8,16,1024]{2,1,0:T(8,128)(2,1)S(1)}, bf16[8,16,1024]{2,1,0:T(8,128)(2,1)S(1)}, u32[]{:S(2)}, u32[]{:S(2)}) collective-permute-start(bf16[8,16,1024]{2,1,0:T(8,128)(2,1)S(1)} %collective-permute-done.10.refs_0_), channel_id=1, source_target_pairs={{0,1},{1,0},{2,3},{3,2},{4,5},{5,4},{6,7},{7,6},{8,9},{9,8},{10,11... | collective-permute-start | bytes 786440 | tf_op jit(solution)/shard_map/ppermute | solution.py:59
  64.8 9.2 %collective-permute-start.16 = (bf16[8,16,1024]{2,1,0:T(8,128)(2,1)S(1)}, bf16[8,16,1024]{2,1,0:T(8,128)(2,1)S(1)}, u32[]{:S(2)}, u32[]{:S(2)}) collective-permute-start(bf16[8,16,1024]{2,1,0:T(8,128)(2,1)S(1)} %collective-permute-done.14.refs_0_), channel_id=1, source_target_pairs={{0,2},{2,0},{1,3},{3,1},{4,6},{6,4},{5,7},{7,5},{8,10},{10,8},{9,1... | collective-permute-start | bytes 786440 | tf_op jit(solution)/shard_map/ppermute | solution.py:59
  65.3 12.6 %collective-permute-start.20 = (bf16[8,16,1024]{2,1,0:T(8,128)(2,1)S(1)}, bf16[8,16,1024]{2,1,0:T(8,128)(2,1)S(1)}, u32[]{:S(2)}, u32[]{:S(2)}) collective-permute-start(bf16[8,16,1024]{2,1,0:T(8,128)(2,1)S(1)} %collective-permute-done.18.refs_0_), channel_id=1, source_target_pairs={{0,2},{2,0},{1,3},{3,1},{4,6},{6,4},{5,7},{7,5},{8,10},{10,8},{9,1... | collective-permute-start | bytes 786440 | tf_op jit(solution)/shard_map/ppermute | solution.py:59
  66.9 24.5 %collective-permute-start.15 = (bf16[8,16,1024]{2,1,0:T(8,128)(2,1)S(1)}, bf16[8,16,1024]{2,1,0:T(8,128)(2,1)S(1)}, u32[]{:S(2)}, u32[]{:S(2)}) collective-permute-start(bf16[8,16,1024]{2,1,0:T(8,128)(2,1)S(1)} %collective-permute-done.14.refs_0_), channel_id=1, source_target_pairs={{0,1},{1,0},{2,3},{3,2},{4,5},{5,4},{6,7},{7,6},{8,9},{9,8},{10,11... | collective-permute-start | bytes 786440 | tf_op jit(solution)/shard_map/ppermute | solution.py:59
  66.9 27.5 %collective-permute-start.19 = (bf16[8,16,1024]{2,1,0:T(8,128)(2,1)S(1)}, bf16[8,16,1024]{2,1,0:T(8,128)(2,1)S(1)}, u32[]{:S(2)}, u32[]{:S(2)}) collective-permute-start(bf16[8,16,1024]{2,1,0:T(8,128)(2,1)S(1)} %collective-permute-done.18.refs_0_), channel_id=1, source_target_pairs={{0,1},{1,0},{2,3},{3,2},{4,5},{5,4},{6,7},{7,6},{8,9},{9,8},{10,11... | collective-permute-start | bytes 786440 | tf_op jit(solution)/shard_map/ppermute | solution.py:59
  67.4 20.5 %collective-permute-start.13 = (bf16[8,16,1024]{2,1,0:T(8,128)(2,1)S(1)}, bf16[8,16,1024]{2,1,0:T(8,128)(2,1)}, u32[]{:S(2)}, u32[]{:S(2)}) collective-permute-start(bf16[8,16,1024]{2,1,0:T(8,128)(2,1)S(1)} %collective-permute-done.12.refs_2_), channel_id=1, source_target_pairs={{0,1},{1,0},{2,3},{3,2},{4,5},{5,4},{6,7},{7,6},{8,9},{9,8},{10,11... | collective-permute-start | bytes 786440 | tf_op jit(solution)/shard_map/ppermute | solution.py:59
  74.0 17.3 %collective-permute-start.17 = (bf16[8,16,1024]{2,1,0:T(8,128)(2,1)S(1)}, bf16[8,16,1024]{2,1,0:T(8,128)(2,1)}, u32[]{:S(2)}, u32[]{:S(2)}) collective-permute-start(bf16[8,16,1024]{2,1,0:T(8,128)(2,1)S(1)} %collective-permute-done.16.refs_2_), channel_id=1, source_target_pairs={{0,1},{1,0},{2,3},{3,2},{4,5},{5,4},{6,7},{7,6},{8,9},{9,8},{10,11... | collective-permute-start | bytes 786440 | tf_op jit(solution)/shard_map/ppermute | solution.py:59
  78.0 16.5 %collective-permute-start.21 = (bf16[8,16,1024]{2,1,0:T(8,128)(2,1)S(1)}, bf16[8,16,1024]{2,1,0:T(8,128)(2,1)}, u32[]{:S(2)}, u32[]{:S(2)}) collective-permute-start(bf16[8,16,1024]{2,1,0:T(8,128)(2,1)S(1)} %collective-permute-done.20.refs_2_), channel_id=1, source_target_pairs={{0,1},{1,0},{2,3},{3,2},{4,5},{5,4},{6,7},{7,6},{8,9},{9,8},{10,11... | collective-permute-start | bytes 786440 | tf_op jit(solution)/shard_map/ppermute | solution.py:59
  83.9 2.2 %copy-start = (bf16[8,256,1024]{2,1,0:T(8,128)(2,1)S(1)}, bf16[8,256,1024]{2,1,0:T(8,128)(2,1)}, u32[]{:S(2)}) copy-start(bf16[8,256,1024]{2,1,0:T(8,128)(2,1)} %bitcast_multiply_fusion.refs_4_) | copy-start | bytes 12582916
  86.1 2.2 %copy-start.1 = (bf16[8,256,1024]{2,1,0:T(8,128)(2,1)S(1)}, bf16[8,256,1024]{2,1,0:T(8,128)(2,1)}, u32[]{:S(2)}) copy-start(bf16[8,256,1024]{2,1,0:T(8,128)(2,1)} %bitcast_multiply_fusion.refs_4_) | copy-start | bytes 12582916
  97.6 4.6 %collective-permute-start.22 = (bf16[4,16,256]{2,1,0:T(8,128)(2,1)S(1)}, bf16[4,16,256]{2,1,0:T(8,128)(2,1)S(1)}, u32[]{:S(2)}, u32[]{:S(2)}) collective-permute-start(bf16[4,16,256]{2,1,0:T(8,128)(2,1)S(1)} %pad_maximum_fusion.3), channel_id=1, source_target_pairs={{0,4},{4,0},{8,12},{12,8},{1,5},{5,1},{9,13},{13,9},{2,6},{6,2},{1... | collective-permute-start | bytes 98312 | tf_op jit(solution)/shard_map/ppermute | solution.py:59
  98.3 5.3 %collective-permute-start.23 = (bf16[4,16,256]{2,1,0:T(8,128)(2,1)S(1)}, bf16[4,16,256]{2,1,0:T(8,128)(2,1)S(1)}, u32[]{:S(2)}, u32[]{:S(2)}) collective-permute-start(bf16[4,16,256]{2,1,0:T(8,128)(2,1)S(1)} %pad_maximum_fusion.4), channel_id=1, source_target_pairs={{0,8},{4,12},{8,0},{12,4},{1,9},{5,13},{9,1},{13,5},{2,10},{6,14},... | collective-permute-start | bytes 98312 | tf_op jit(solution)/shard_map/ppermute | solution.py:59
  100.9 5.7 %collective-permute-start.24 = (bf16[4,16,256]{2,1,0:T(8,128)(2,1)S(1)}, bf16[4,16,256]{2,1,0:T(8,128)(2,1)S(1)}, u32[]{:S(2)}, u32[]{:S(2)}) collective-permute-start(bf16[4,16,256]{2,1,0:T(8,128)(2,1)S(1)} %pad_maximum_fusion.5), channel_id=1, source_target_pairs={{0,12},{4,8},{8,4},{12,0},{1,13},{5,9},{9,5},{13,1},{2,14},{6,10},... | collective-permute-start | bytes 98312 | tf_op jit(solution)/shard_map/ppermute | solution.py:59

commit v3 on v2

--- a/solution.py
+++ b/solution.py
@@ -12,6 +12,7 @@
 SL = 64
 LANES = 128
 PAIR = LANES // AOB
+TINY = pl.CostEstimate(flops=1, bytes_accessed=1, transcendentals=0)
 
 
 def pair_masks(green_mask, slab_mask):
@@ -24,13 +25,15 @@
     return pair.astype(jnp.bfloat16), (pair * near_mask).astype(jnp.bfloat16)
 
 
-def gathered_plan(tensor, masked, slab_mask, occ_green, virt_green, green_mask):
+def gathered_plan(tensor, mask_rows, occ_green, virt_green, green_mask):
     blocks = tensor.shape[1]
+    row_mask = jnp.repeat(mask_rows, RB, axis=0).astype(jnp.bfloat16)
+    masked = tensor * row_mask[:, :, None]
     reach = (occ_green.shape[1] - 1) // 2
     slab = lax.all_to_all(tensor[:SL], "ao", split_axis=0, concat_axis=2, tiled=True)
     occ_all = lax.all_gather(occ_green, "ao", axis=0, tiled=True)
     virt_all = lax.all_gather(virt_green, "ao", axis=0, tiled=True)
-    occ_mask, virt_mask = pair_masks(green_mask, slab_mask)
+    occ_mask, virt_mask = pair_masks(green_mask, mask_rows[0])
     occ = occ_all * occ_mask[:, :, None, None]
     virt = virt_all * virt_mask[:, :, None, None]
     own = slab.shape[0]
@@ -60,20 +63,21 @@
 
 
 def contract_kernel(planes, *refs):
-    chunks = refs[:planes]
-    occ_ref, virt_ref = refs[planes : planes + 2]
-    outs = refs[planes + 2 : 2 * planes + 2]
-    even_ref, odd_ref, weight_ref, inner_ref, sums_ref = refs[2 * planes + 2 :]
-    own, blocks, cols = chunks[0].shape
+    halves = refs[: 2 * planes]
+    occ_ref, virt_ref = refs[2 * planes : 2 * planes + 2]
+    outs = refs[2 * planes + 2 : 3 * planes + 2]
+    even_ref, odd_ref, weight_ref, inner_ref, sums_ref = refs[3 * planes + 2 :]
+    blocks, own, cols = outs[0].shape
     width = virt_ref.shape[1]
     reach = (width - 1) // 2
     units = cols // LANES
     pairs = own // PAIR
     rows = planes * units
     f32 = jnp.float32
-    for plane, chunk in enumerate(chunks):
+    for plane in range(planes):
         for p in range(own):
-            value = chunk[p].astype(f32)
+            half = halves[2 * plane + p // (own // 2)]
+            value = half[p % (own // 2)].astype(f32)
             target = even_ref if p % 2 == 0 else odd_ref
             for u in range(units):
                 start = (p // 2) * rows + plane * units + u
@@ -136,19 +140,19 @@
                 ].astype(jnp.bfloat16)
 
 
-def contract(chunks, occ, virt):
-    planes = len(chunks)
-    own, blocks, cols = chunks[0].shape
+def contract(halves, occ, virt):
+    planes = len(halves) // 2
+    half, blocks, cols = halves[1].shape
+    own = 2 * half
     width = virt.shape[1]
     units = cols // LANES
     pairs = own // PAIR
     rows = planes * units
     whole = pl.BlockSpec(memory_space=pltpu.VMEM)
-    flops = 2 * blocks * width * own * AOB * AOB * AOB * 4
     return pl.pallas_call(
         functools.partial(contract_kernel, planes),
         out_shape=[jax.ShapeDtypeStruct((blocks, own, cols), jnp.bfloat16)] * planes,
-        in_specs=[whole] * (planes + 2),
+        in_specs=[whole] * (2 * planes + 2),
         out_specs=[whole] * planes,
         scratch_shapes=[
             pltpu.VMEM((blocks * pairs * rows, LANES), jnp.float32),
@@ -157,74 +161,183 @@
             pltpu.VMEM((blocks, pairs // 2, width * AOB, 2 * LANES), jnp.bfloat16),
             pltpu.VMEM((blocks * rows * own, LANES), jnp.float32),
         ],
-        compiler_params=pltpu.CompilerParams(vmem_limit_bytes=40 * 1024 * 1024),
-        cost_estimate=pl.CostEstimate(flops=flops, bytes_accessed=3 << 20, transcendentals=0),
+        compiler_params=pltpu.CompilerParams(vmem_limit_bytes=20 * 1024 * 1024),
+        cost_estimate=TINY,
         name="contract_slab",
-    )(*chunks, occ, virt)
-
-
-def response_kernel(count, *refs):
-    parts = refs[:count]
-    masked_ref, out_ref = refs[count:]
-    step = pl.program_id(0)
-
-    @pl.when(step == 0)
-    def _():
-        out_ref[...] = jnp.zeros_like(out_ref)
-
-    total = None
-    for m in range(masked_ref.shape[0]):
-        left = jnp.concatenate([part[m] for part in parts], axis=0)
-        term = lax.dot_general(
-            left, masked_ref[m], (((1,), (1,)), ((), ())), preferred_element_type=jnp.float32
+    )(*halves, occ, virt)
+
+
+def add_terms(k, near, far, rows_ref, keep_ref, core, cross_refs, into_ref):
+    blocks, own, cols = near.shape
+    rows = rows_ref.shape[0] // blocks
+    right = jnp.concatenate(
+        [near[...].reshape(blocks * own, cols), far[...].reshape(blocks * own, cols)], axis=0
+    )
+    some = 64
+    group = lax.broadcasted_iota(jnp.int32, (some, LANES), 1) // own
+    for part in range(rows // some):
+        cross = lax.dot_general(
+            rows_ref[part * some * blocks : (part + 1) * some * blocks, :],
+            right,
+            (((1,), (1,)), ((), ())),
+            preferred_element_type=jnp.float32,
         )
-        total = term if total is None else total + term
-    out_ref[...] += total
-
-
-def response(parts, masked):
+        keep = keep_ref[core, part * some // RB][None, :]
+        for side in range(2):
+            hold = cross_refs.at[part % 2, side]
+            hold[...] = cross[:, side * LANES : (side + 1) * LANES]
+            total = hold[pl.ds(0, some, stride=blocks), :]
+            for m in range(1, blocks):
+                total = jnp.where(group == m, hold[pl.ds(m, some, stride=blocks), :], total)
+            total = total * keep
+            shift = LANES // 2
+            while shift >= own:
+                total = total + pltpu.roll(total, shift, 1)
+                shift //= 2
+            at = slice(part * some, (part + 1) * some)
+            into_ref[core, at, :] = jnp.where(
+                group == 2 * k + side, total, into_ref[core, at, :]
+            )
+
+
+def first_kernel(count, keep_ref, *refs):
+    parts, sources = refs[: 2 * count], refs[2 * count : 2 * count + 2]
+    out_ref, *kept = refs[2 * count + 2 : 2 * count + 5]
+    cross_refs, sem = refs[2 * count + 5 :]
+    copies = [pltpu.make_async_copy(sources[c], kept[c], sem.at[c]) for c in range(2)]
+    for copy in copies:
+        copy.start()
+    out_ref[...] = jnp.zeros_like(out_ref)
+    for core in range(2):
+        copies[core].wait()
+        for k in range(count):
+            add_terms(k, parts[2 * k], parts[2 * k + 1], kept[core], keep_ref, core, cross_refs, out_ref)
+
+
+def next_kernel(k, keep_ref, near_ref, far_ref, own_ref, other_ref, early_ref, out_ref, cross_refs):
+    out_ref[...] = early_ref[...]
+    for core, rows_ref in enumerate((own_ref, other_ref)):
+        add_terms(k, near_ref, far_ref, rows_ref, keep_ref, core, cross_refs, out_ref)
+
+
+def last_kernel(
+    place_ref, keep_ref, near_ref, far_ref, own_ref, other_ref, early_ref, out_ref, hold_ref, turn_ref, cross_refs
+):
+    count, own = out_ref.shape[0], near_ref.shape[1]
+    hold_ref[...] = early_ref[...]
+    for core, rows_ref in enumerate((own_ref, other_ref)):
+        add_terms(count - 1, near_ref, far_ref, rows_ref, keep_ref, core, cross_refs, hold_ref)
+        turn_ref[core] = hold_ref[core].T
+    for route in range(count):
+        side, core = place_ref[0] ^ (route // 2), place_ref[1] ^ (route % 2)
+        for p in range(count):
+            start = pl.multiple_of((2 * (p ^ route) + side) * own, own)
+            out_ref[route, p * own : (p + 1) * own, :] = turn_ref[
+                core, pl.ds(start, own), :
+            ].astype(jnp.bfloat16)
+
+
+WHOLE = pl.BlockSpec(memory_space=pltpu.VMEM)
+PARAMS = pltpu.CompilerParams(vmem_limit_bytes=20 * 1024 * 1024)
+
+
+def cross_scratch(blocks):
+    return pltpu.VMEM((2, 2, 64 * blocks, LANES), jnp.float32)
+
+
+def first_terms(keep, parts, sources):
     blocks, own, cols = parts[0].shape
-    rows_dev = masked.shape[1]
-    count = len(parts)
-    per_step = 2
+    rows = sources[0].shape[0]
     return pl.pallas_call(
-        functools.partial(response_kernel, count),
-        grid=(blocks // per_step,),
-        out_shape=jax.ShapeDtypeStruct((count * own, rows_dev), jnp.float32),
-        in_specs=[pl.BlockSpec((per_step, own, cols), lambda s: (s, 0, 0))] * count
-        + [pl.BlockSpec((per_step, rows_dev, cols), lambda s: (s, 0, 0))],
-        out_specs=pl.BlockSpec((count * own, rows_dev), lambda s: (0, 0)),
-        compiler_params=pltpu.CompilerParams(vmem_limit_bytes=24 * 1024 * 1024),
-        cost_estimate=pl.CostEstimate(
-            flops=2 * count * own * rows_dev * blocks * cols,
-            bytes_accessed=2 * rows_dev * blocks * cols,
-            transcendentals=0,
-        ),
-        name="response_terms",
-    )(*parts, masked)
-
-
-def swapped_plan(tensor, masked, slab_mask, occ_green, virt_green, green_mask):
+        functools.partial(first_kernel, len(parts) // 2),
+        out_shape=[jax.ShapeDtypeStruct((2, rows // blocks, LANES), jnp.float32)]
+        + [pltpu.VMEM((rows, cols), jnp.bfloat16)] * 2,
+        in_specs=[WHOLE] * (len(parts) + 1) + [pl.BlockSpec(memory_space=pl.ANY)] * 2,
+        out_specs=[WHOLE] * 3,
+        scratch_shapes=[cross_scratch(blocks), pltpu.SemaphoreType.DMA((2,))],
+        compiler_params=PARAMS,
+        cost_estimate=TINY,
+        name="first_terms",
+    )(keep, *parts, *sources)
+
+
+def next_terms(k, keep, near, far, rows, early):
+    return pl.pallas_call(
+        functools.partial(next_kernel, k),
+        out_shape=jax.ShapeDtypeStruct(early.shape, jnp.float32),
+        in_specs=[WHOLE] * 6,
+        out_specs=WHOLE,
+        scratch_shapes=[cross_scratch(near.shape[0])],
+        compiler_params=PARAMS,
+        cost_estimate=TINY,
+        name="next_terms",
+    )(keep, near, far, *rows, early)
+
+
+def last_terms(place, keep, near, far, rows, early):
+    own = near.shape[1]
+    rows_dev = early.shape[1]
+    count = LANES // (2 * own)
+    return pl.pallas_call(
+        last_kernel,
+        out_shape=jax.ShapeDtypeStruct((count, count * own, rows_dev), jnp.bfloat16),
+        in_specs=[pl.BlockSpec(memory_space=pltpu.SMEM)] + [WHOLE] * 6,
+        out_specs=WHOLE,
+        scratch_shapes=[
+            pltpu.VMEM(early.shape, jnp.float32),
+            pltpu.VMEM((2, LANES, rows_dev), jnp.float32),
+            cross_scratch(near.shape[0]),
+        ],
+        compiler_params=PARAMS,
+        cost_estimate=TINY,
+        name="last_terms",
+    )(place, keep, near, far, *rows, early)
+
+
+def routed(value, route):
+    pairs = []
+    for z in range(4):
+        for core in range(2):
+            to_z = 2 * ((z // 2) ^ (route // 2)) + core
+            to_core = (z % 2) ^ (route % 2)
+            pairs.append((2 * z + core, 2 * to_z + to_core))
+    return lax.ppermute(value, ("ao", "rep"), pairs)
+
+
+def after(value, *others):
+    return lax.optimization_barrier((value,) + others)[0]
+
+
+def swapped_plan(tensor, mask_rows, other_mask_rows, occ_green, virt_green, green_mask):
     planes = lax.axis_size("ao")
     steps = range(1, planes)
     z = lax.axis_index("ao")
     core = lax.axis_index("rep")
-    shard = lax.axis_index(("aux", "rep"))
+    aux = lax.axis_index("aux")
+    side = lax.axis_index("tpoint")
     own = SL // planes
-    cols = tensor.shape[2]
+    half = own // 2
+    rows_dev, blocks, cols = tensor.shape
     units = cols // LANES
-    blocks = tensor.shape[1]
-
-    def rows_of(plane):
-        return lax.dynamic_slice_in_dim(tensor, plane * own, own, 0)
-
-    chunks = [rows_of(z)] + [swap(rows_of(z ^ k), "ao", k) for k in steps]
-    mine = jnp.where(core == 0, occ_green, virt_green)
-    stacked = jnp.stack([mine] + [swap(mine, "ao", k) for k in steps])
+
+    def rows_of(plane, part):
+        return lax.dynamic_slice_in_dim(tensor, plane * own + part * half, half, 0)
+
+    mine = jnp.where(core == 0, occ_green, virt_green).reshape(-1, blocks, cols)
+    leaving = [jnp.concatenate([rows_of(z ^ k, side), mine]) for k in steps]
+    direct = [swap(leaving[k - 1], "ao", k) for k in steps]
+    halves = [rows_of(z, side), rows_of(z, 1 - side)]
+    for value in direct:
+        halves += [value, swap(value[:half], "tpoint", 1)]
+    stacked = jnp.stack([mine] + [value[half:] for value in direct])
     order = jnp.arange(planes) ^ z
-    mine_all = stacked[order].reshape((blocks,) + mine.shape[1:])
-    other_all = swap(mine_all, "rep", 1)
-    occ_mask, virt_mask = pair_masks(green_mask, slab_mask)
+    other = swap(stacked, "rep", 1)
+    shape = (blocks,) + occ_green.shape[1:]
+    mine_all = stacked[order].reshape(shape)
+    other_all = other[order].reshape(shape)
+    rows = tensor.reshape(rows_dev * blocks, cols)
+    rows = (rows, swap(rows, "rep", 1))
+    occ_mask, virt_mask = pair_masks(green_mask, mask_rows[0])
     occ = jnp.where(core == 0, mine_all, other_all) * occ_mask[:, :, None, None]
     virt = jnp.where(core == 0, other_all, mine_all) * virt_mask[:, :, None, None]
     place = jnp.arange(AOB)
@@ -243,43 +356,42 @@
         ],
         axis=2,
     )
-    sums = contract(chunks, occ, virt)
-    terms = []
-    for k in range(planes):
-        near = sums[k] if k == 0 else swap(sums[k], "ao", k)
-        far = swap(near, "aux", 1)
-        terms.append(
-            response([near, swap(near, "rep", 1), far, swap(far, "rep", 1)], masked).reshape(
-                planes, own, -1
-            )
-        )
-    terms = jnp.stack(terms)
-
-    def block_for(k):
-        kept = lax.dynamic_index_in_dim(terms, shard ^ z ^ k, 1, keepdims=False)
-        return jnp.stack([kept[p ^ k] for p in range(planes)])
-
-    total = block_for(0)
-    for k in steps:
-        total = total + swap(block_for(k).astype(jnp.bfloat16), "ao", k).astype(jnp.float32)
-    return total[order].reshape(SL, -1)
+    sums = contract(halves, occ, virt)
+    near = [sums[0], swap(sums[1], "ao", 1), swap(sums[2], "ao", 2)]
+    near.append(swap(after(sums[3], near[1]), "ao", 3))
+    far = [swap(value, "aux", 1) for value in (sums[0], sums[1], near[2], near[3])]
+    far[1] = swap(far[1], "ao", 1)
+    keep = jnp.repeat(jnp.stack([mask_rows, other_mask_rows]), own, axis=2).astype(jnp.float32)
+    early, *rows = first_terms(keep, [near[0], far[0], near[1], far[1]], rows)
+    early = next_terms(2, keep, near[2], far[2], rows, early)
+    place = jnp.stack([(z // 2) ^ aux, (z % 2) ^ core]).astype(jnp.int32)
+    leaving = last_terms(place, keep, near[3], far[3], rows, early)
+    total = None
+    for route in range(planes):
+        term = routed(leaving[route], route).astype(jnp.float32)
+        total = term if total is None else total + term
+    index = jnp.arange(2 * planes)
+    home = index ^ (2 * (2 * (z // 2) + core) + side)
+    return total.reshape(2 * planes, half, -1)[home].reshape(SL, -1)
 
 
 def per_device(tensor, block_mask, occ_green, virt_green, green_mask):
     rows_dev, blocks, cols = tensor.shape
     shard = lax.axis_index(("aux", "rep"))
     per_shard = rows_dev // RB
-    mask_rows = lax.dynamic_slice_in_dim(block_mask, shard * per_shard, per_shard, 0)
-    row_mask = jnp.repeat(mask_rows, RB, axis=0).astype(jnp.bfloat16)
     planes = lax.axis_size("ao")
-    simple = planes == 4 and lax.axis_size("aux") == 2 and lax.axis_size("rep") == 2
-    if simple and cols * planes == AOB * AOB and SL // planes % 16 == 0:
-        masked = jnp.swapaxes(tensor, 0, 1) * row_mask.T[:, :, None]
-        plan = swapped_plan
-    else:
-        masked = tensor * row_mask[:, :, None]
-        plan = gathered_plan
-    return plan(tensor, masked, mask_rows[0], occ_green, virt_green, green_mask)
+
+    def mask_of(index):
+        return lax.dynamic_slice_in_dim(block_mask, index * per_shard, per_shard, 0)
+
+    sizes = tuple(lax.axis_size(axis) for axis in ("tpoint", "ao", "aux", "rep"))
+    simple = sizes == (2, 4, 2, 2) and cols * planes == AOB * AOB and SL // planes == 16
+    simple = simple and blocks * 16 == LANES and rows_dev % RB == 0 and occ_green.shape[1] == 3
+    if simple:
+        return swapped_plan(
+            tensor, mask_of(shard), mask_of(shard ^ 1), occ_green, virt_green, green_mask
+        )
+    return gathered_plan(tensor, mask_of(shard), occ_green, virt_green, green_mask)
 
 
 def solution(mesh):

time: 108 us -> 93.5 us (0.87)
  waiting for transfers between devices: 49.4 us -> 40.6 us
  other arithmetic: 8.01 us -> 1.35 us
  starting transfers between devices: 27.1 us -> 25.3 us
  Pallas kernels: 14.4 us -> 16.1 us
    ppermute x25 -> x16, waiting for transfers between devices: 49.4 us -> 35.1 us  [swap(): return lax.ppermute(value, axis, [(i, i ^ step) for i in range(count)])]
    ppermute x25 -> x16, starting transfers between devices: 27.1 us -> 20.5 us  [swap(): return lax.ppermute(value, axis, [(i, i ^ step) for i in range(count)])]
    mul x1 -> x0, other arithmetic: 5.97 us -> none  [per_device(): masked = jnp.swapaxes(tensor, 0, 1) * row_mask.T[:, :, None]]
    ppermute x0 -> x4, waiting for transfers between devices: none -> 5.56 us  [routed(): return lax.ppermute(value, ('ao', 'rep'), pairs)]
    ppermute x0 -> x4, starting transfers between devices: none -> 4.81 us  [routed(): return lax.ppermute(value, ('ao', 'rep'), pairs)]
    pallas_call x4 -> x3, Pallas kernels: 11 us -> 12.6 us  [the longest x1 6.13 us: first_terms(): pl.pallas_call(functools.partial(first_kernel, len(parts) // 2), out_shap...]
    gather x2 -> x3, local copies, waits for them, and re-layouts: 1.8 us -> 2.3 us  [the longest x1 1.18 us: swapped_plan(): return total.reshape(2 * planes, half, -1)[home].reshape(SL, -1)]
    unnamed x9 -> x5, local copies, waits for them, and re-layouts: 2.65 us -> 2.27 us
  transfers between devices with their start and end apart: 25 -> 20, of which waited for: 9 -> 12; matrix products, arithmetic and copies ran while one was open for 11% -> 8% of each run, Pallas kernels for 7% -> 13%
where the time goes in v3:
time: 93.5 us; the launch traced here: 93.3 us
  waiting for transfers between devices  40.6 us (43%)
  starting transfers between devices  25.3 us (27%)
  Pallas kernels  16.1 us (17%)
  local copies, waits for them, and re-layouts  8.86 us (9%)
  other arithmetic  1.35 us (1%)
    ppermute x16, waiting for transfers between devices, swap(): return lax.ppermute(value, axis, [(i, i ^ step) for i in range(count)])  35.1 us
    ppermute x16, starting transfers between devices, swap(): return lax.ppermute(value, axis, [(i, i ^ step) for i in range(count)])  20.5 us
    pallas_call x1, Pallas kernels, first_terms(): pl.pallas_call(functools.partial(first_kernel, len(parts) // 2), out_shap...  6.13 us
    ppermute x4, waiting for transfers between devices, routed(): return lax.ppermute(value, ('ao', 'rep'), pairs)  5.56 us
    ppermute x4, starting transfers between devices, routed(): return lax.ppermute(value, ('ao', 'rep'), pairs)  4.81 us
    pallas_call x1, Pallas kernels, last_terms(): pl.pallas_call(last_kernel, out_shape=jax.ShapeDtypeStruct((count, count...  3.56 us
    pallas_call x1, Pallas kernels, contract(): pl.pallas_call(functools.partial(contract_kernel, planes), out_shape=[jax...  3.46 us
    pallas_call x1, Pallas kernels, next_terms(): pl.pallas_call(functools.partial(next_kernel, k), out_shape=jax.ShapeDtyp...  2.9 us
  transfers between devices with their start and end apart: 20, of which 12 were waited for; matrix products, arithmetic and copies ran while one was open for 8% of the time, Pallas kernels for 13%

profile of v3, /device:TPU:0, one launch (start us, length us, event | category | flops | bytes accessed | tf_op | source)
XLA Modules:
  0.0 93.3 jit_solution(2309382300122581858)
XLA Ops:
  0.0 0.5 collective-permute-start.13
  0.5 0.9 broadcast_select_fusion.2
  1.4 0.1 reshape.132
  1.5 1.2 %constant_dynamic-slice_fusion = (bf16[8,8,1024]{2,1,0:T(8,128)(2,1)S(1)}, bf16[8,8,1024]{2,1,0:T(8,128)(2,1)S(1)}, bf16[8,8,1024]{2,1,0:T(8,128)(2,1)S(1)}, bf1...) fusion(bf16[256,8,1024]{2,1,0:T(8,128)(2,1)} %param.5, s32[]{:T(128)S(6)} %select_n.138, s32[]{:T(128)S(6)} %select_n.137, ...), kind=kLoop, calls=%fused_computation.50 | loop fusion | bytes 1310740 | tf_op jit(solution)/shard_map/dynamic_slice | solution.py:324
  2.8 4.7 %collective-permute-start.4 = (bf16[11,8,1024]{2,1,0:T(8,128)(2,1)S(1)}, bf16[11,8,1024]{2,1,0:T(8,128)(2,1)S(1)}, u32[]{:S(2)}, u32[]{:S(2)}) collective-permute-start(bf16[11,8,1024]{2,1,0:T(8,128)(2,1)S(1)} %get-tuple-element.34), channel_id=1, source_target_pairs={{0,12},{4,8},{8,4},{12,0},{1,13},{5,9},{9,5},{13,1},{2,14},{6,10},... | collective-permute-start | bytes 540680 | tf_op jit(solution)/shard_map/ppermute | solution.py:62
  7.5 0.6 collective-permute-start
  8.1 0.1 stack_reshape.3
  8.3 0.8 constant_dynamic-slice_fusion.6
  9.1 0.7 gather_fusion.2
  9.9 0.1 copy.9
  10.0 3.0 %collective-permute-done.4.refs_6_ = bf16[11,8,1024]{2,1,0:T(8,128)(2,1)S(1)} collective-permute-done((bf16[11,8,1024]{2,1,0:T(8,128)(2,1)S(1)}, bf16[11,8,1024]{2,1,0:T(8,128)(2,1)S(1)}, u32[]{:S(2)}, u32[]{:S(2)}) %collective-permute-start.4) | collective-permute-done | bytes 180256 | tf_op jit(solution)/shard_map/ppermute | solution.py:62
  13.0 10.4 %collective-permute-done.2.refs_4_ = bf16[11,8,1024]{2,1,0:T(8,128)(2,1)S(1)} collective-permute-done((bf16[11,8,1024]{2,1,0:T(8,128)(2,1)S(1)}, bf16[11,8,1024]{2,1,0:T(8,128)(2,1)S(1)}, u32[]{:S(2)}, u32[]{:S(2)}) %collective-permute-start.2) | collective-permute-done | bytes 180256 | tf_op jit(solution)/shard_map/ppermute | solution.py:62
  23.6 0.6 gather_fusion
  24.2 1.6 %collective-permute-start.1 = (bf16[8,8,1024]{2,1,0:T(8,128)(2,1)S(1)}, bf16[8,8,1024]{2,1,0:T(8,128)(2,1)S(1)}, u32[]{:S(2)}, u32[]{:S(2)}) collective-permute-start(bf16[8,8,1024]{2,1,0:T(8,128)(2,1)S(1)} %slice.52), channel_id=1, source_target_pairs={{0,16},{16,0},{1,17},{17,1},{2,18},{18,2},{3,19},{19,3},{4,20},{20... | collective-permute-start | bytes 393224 | tf_op jit(solution)/shard_map/ppermute | solution.py:62
  25.8 0.6 collective-permute-start.3
  26.3 1.6 %collective-permute-start.5 = (bf16[8,8,1024]{2,1,0:T(8,128)(2,1)S(1)}, bf16[8,8,1024]{2,1,0:T(8,128)(2,1)S(1)}, u32[]{:S(2)}, u32[]{:S(2)}) collective-permute-start(bf16[8,8,1024]{2,1,0:T(8,128)(2,1)S(1)} %slice.54), channel_id=1, source_target_pairs={{0,16},{16,0},{1,17},{17,1},{2,18},{18,2},{3,19},{19,3},{4,20},{20... | collective-permute-start | bytes 393224 | tf_op jit(solution)/shard_map/ppermute | solution.py:62
  27.9 0.6 gather_fusion.1
  28.5 0.3 select_n.149
  28.8 0.3 select_n.146
  29.1 0.7 fusion
  29.8 0.2 copy.11.refs_8_
  30.0 0.1 broadcast_multiply_fusion
  30.1 0.2 pad_bitcast_fusion.1
  30.5 2.8 %collective-permute-done.3.refs_5_ = bf16[8,8,1024]{2,1,0:T(8,128)(2,1)S(1)} collective-permute-done((bf16[8,8,1024]{2,1,0:T(8,128)(2,1)S(1)}, bf16[8,8,1024]{2,1,0:T(8,128)(2,1)S(1)}, u32[]{:S(2)}, u32[]{:S(2)}) %collective-permute-start.3) | collective-permute-done | bytes 131104 | tf_op jit(solution)/shard_map/ppermute | solution.py:62
  33.3 2.4 %collective-permute-done.5.refs_7_ = bf16[8,8,1024]{2,1,0:T(8,128)(2,1)S(1)} collective-permute-done((bf16[8,8,1024]{2,1,0:T(8,128)(2,1)S(1)}, bf16[8,8,1024]{2,1,0:T(8,128)(2,1)S(1)}, u32[]{:S(2)}, u32[]{:S(2)}) %collective-permute-start.5) | collective-permute-done | bytes 131104 | tf_op jit(solution)/shard_map/ppermute | solution.py:62
  35.7 3.5 %contract_slab.1 = (bf16[8,16,1024]{2,1,0:T(8,128)(2,1)S(1)}, bf16[8,16,1024]{2,1,0:T(8,128)(2,1)S(1)}, bf16[8,16,1024]{2,1,0:T(8,128)(2,1)S(1)}, bf16[8,16,1024]{2,1,0:T(8,128)(2,1)S(1)}) custom-call(bf16[8,8,1024]{2,1,0:T(8,128)(2,1)S(1)} %get-tuple-element.25.refs_0_, bf16[8,8,1024]{2,1,0:T(8,128)(2,1)S(1)} %get-tuple-element.24.refs_1_, ...), custom_call_target="tpu_custom_call" | custom-call | flops 1 | bytes 1 | tf_op jit(solution)/shard_map/contract_slab/pallas_call | solution.py:152
  39.3 1.6 %collective-permute-start.11 = (bf16[8,16,1024]{2,1,0:T(8,128)(2,1)S(1)}, bf16[8,16,1024]{2,1,0:T(8,128)(2,1)S(1)}, u32[]{:S(2)}, u32[]{:S(2)}) collective-permute-start(bf16[8,16,1024]{2,1,0:T(8,128)(2,1)S(1)} %get-tuple-element.14), channel_id=1, source_target_pairs={{0,2},{2,0},{1,3},{3,1},{4,6},{6,4},{5,7},{7,5},{8,10},{10,8},{9,1... | collective-permute-start | bytes 786440 | tf_op jit(solution)/shard_map/ppermute | solution.py:62
  40.8 3.0 %collective-permute-start.14 = (bf16[8,16,1024]{2,1,0:T(8,128)(2,1)S(1)}, bf16[8,16,1024]{2,1,0:T(8,128)(2,1)S(1)}, u32[]{:S(2)}, u32[]{:S(2)}) collective-permute-start(bf16[8,16,1024]{2,1,0:T(8,128)(2,1)S(1)} %get-tuple-element.19), channel_id=1, source_target_pairs={{0,8},{4,12},{8,0},{12,4},{1,9},{5,13},{9,1},{13,5},{2,10},{6,14},... | collective-permute-start | bytes 786440 | tf_op jit(solution)/shard_map/ppermute | solution.py:62
  43.8 7.6 %collective-permute-done.7.refs_2_ = bf16[8,16,1024]{2,1,0:T(8,128)(2,1)S(1)} collective-permute-done((bf16[8,16,1024]{2,1,0:T(8,128)(2,1)S(1)}, bf16[8,16,1024]{2,1,0:T(8,128)(2,1)S(1)}, u32[]{:S(2)}, u32[]{:S(2)}) %collective-permute-start.7) | collective-permute-done | bytes 262176 | tf_op jit(solution)/shard_map/ppermute | solution.py:62
  51.4 1.4 %collective-permute-start.8 = (bf16[8,16,1024]{2,1,0:T(8,128)(2,1)S(1)}, bf16[8,16,1024]{2,1,0:T(8,128)(2,1)S(1)}, u32[]{:S(2)}, u32[]{:S(2)}) collective-permute-start(bf16[8,16,1024]{2,1,0:T(8,128)(2,1)S(1)} %get-tuple-element.15), channel_id=1, source_target_pairs={{0,12},{4,8},{8,4},{12,0},{1,13},{5,9},{9,5},{13,1},{2,14},{6,10},... | collective-permute-start | bytes 786440 | tf_op jit(solution)/shard_map/ppermute | solution.py:62
  52.7 2.5 %collective-permute-start.10 = (bf16[8,16,1024]{2,1,0:T(8,128)(2,1)S(1)}, bf16[8,16,1024]{2,1,0:T(8,128)(2,1)S(1)}, u32[]{:S(2)}, u32[]{:S(2)}) collective-permute-start(bf16[8,16,1024]{2,1,0:T(8,128)(2,1)S(1)} %get-tuple-element.16.refs_0_), channel_id=1, source_target_pairs={{0,2},{2,0},{1,3},{3,1},{4,6},{6,4},{5,7},{7,5},{8,10},{10,8},{9,1... | collective-permute-start | bytes 786440 | tf_op jit(solution)/shard_map/ppermute | solution.py:62
  55.2 6.6 %collective-permute-done.14.near_ref = bf16[8,16,1024]{2,1,0:T(8,128)(2,1)S(1)} collective-permute-done((bf16[8,16,1024]{2,1,0:T(8,128)(2,1)S(1)}, bf16[8,16,1024]{2,1,0:T(8,128)(2,1)S(1)}, u32[]{:S(2)}, u32[]{:S(2)}) %collective-permute-start.14) | collective-permute-done | bytes 262176 | tf_op jit(solution)/shard_map/ppermute | solution.py:62
  61.9 0.5 collective-permute-done.8.near_ref
  62.4 2.5 %collective-permute-start.9 = (bf16[8,16,1024]{2,1,0:T(8,128)(2,1)S(1)}, bf16[8,16,1024]{2,1,0:T(8,128)(2,1)S(1)}, u32[]{:S(2)}, u32[]{:S(2)}) collective-permute-start(bf16[8,16,1024]{2,1,0:T(8,128)(2,1)S(1)} %collective-permute-done.8.near_ref), channel_id=1, source_target_pairs={{0,2},{2,0},{1,3},{3,1},{4,6},{6,4},{5,7},{7,5},{8,10},{10,8},{9,1... | collective-permute-start | bytes 786440 | tf_op jit(solution)/shard_map/ppermute | solution.py:62
  65.0 0.1 convert_element_type.29.keep_ref
  65.1 1.7 %collective-permute-done.12.refs_3_ = bf16[8,16,1024]{2,1,0:T(8,128)(2,1)S(1)} collective-permute-done((bf16[8,16,1024]{2,1,0:T(8,128)(2,1)S(1)}, bf16[8,16,1024]{2,1,0:T(8,128)(2,1)S(1)}, u32[]{:S(2)}, u32[]{:S(2)}) %collective-permute-start.12) | collective-permute-done | bytes 262176 | tf_op jit(solution)/shard_map/ppermute | solution.py:62
  66.8 2.2 %copy-done = bf16[256,8,1024]{2,1,0:T(8,128)(2,1)S(1)} copy-done((bf16[256,8,1024]{2,1,0:T(8,128)(2,1)S(1)}, bf16[256,8,1024]{2,1,0:T(8,128)(2,1)}, u32[]{:S(2)}) %copy-start) | copy-done | bytes 4194328
  69.0 6.1 %first_terms.1 = (f32[2,256,128]{2,1,0:T(8,128)S(1)}, bf16[2048,1024]{1,0:T(8,128)(2,1)S(1)}, bf16[2048,1024]{1,0:T(8,128)(2,1)S(1)}) custom-call(f32[2,2,128]{2,1,0:T(2,128)S(1)} %convert_element_type.29.keep_ref, bf16[8,16,1024]{2,1,0:T(8,128)(2,1)S(1)} %get-tuple-element.16.refs_0_, bf16[8,16,1024]{2,1,0:T(8,128)(2,1)S(1)} %collective-permute-done.10.refs_1_, ...), custom_call_target="tpu_custom_call" | custom-call | flops 1 | bytes 1 | tf_op jit(solution)/shard_map/first_terms/pallas_call | solution.py:251
  75.2 2.9 %next_terms.1.early_ref = f32[2,256,128]{2,1,0:T(8,128)S(1)} custom-call(f32[2,2,128]{2,1,0:T(2,128)S(1)} %convert_element_type.29.keep_ref, bf16[8,16,1024]{2,1,0:T(8,128)(2,1)S(1)} %collective-permute-done.14.near_ref, bf16[8,16,1024]{2,1,0:T(8,128)(2,1)S(1)} %collective-permute-done.15.far_ref, bf16[2048,1024]{1,0:T(8,128)(2,1)S(1)} %get-tuple-element.17.own_ref, ...), custom_call_target="tpu_custom_call" | custom-call | flops 1 | bytes 1 | tf_op jit(solution)/shard_map/next_terms/pallas_call | solution.py:265
  78.1 3.6 %last_terms.1 = bf16[4,64,256]{2,1,0:T(8,128)(2,1)S(1)} custom-call(s32[2]{0:T(128)S(1)} %pad_add_fusion.place_ref, f32[2,2,128]{2,1,0:T(2,128)S(1)} %convert_element_type.29.keep_ref, bf16[8,16,1024]{2,1,0:T(8,128)(2,1)S(1)} %collective-permute-done.8.near_ref, bf16[8,16,1024]{2,1,0:T(8,128)(2,1)S(1)} %collective-permute-done.9.far_ref, ...), custom_call_target="tpu_custom_call" | custom-call | flops 1 | bytes 1 | tf_op jit(solution)/shard_map/last_terms/pallas_call | solution.py:281
  81.7 0.7 collective-permute-start.16
  82.3 2.3 %collective-permute-start.17 = (bf16[64,256]{1,0:T(8,128)(2,1)S(1)}, bf16[64,256]{1,0:T(8,128)(2,1)S(1)}, u32[]{:S(2)}, u32[]{:S(2)}) collective-permute-start(bf16[64,256]{1,0:T(8,128)(2,1)S(1)} %get-tuple-element.33), channel_id=1, source_target_pairs={{0,1},{1,5},{4,0},{5,4},{8,9},{9,13},{12,8},{13,12},{2,3},{3,7},{6... | collective-permute-start | bytes 98312 | tf_op jit(solution)/shard_map/ppermute | solution.py:304
  84.6 1.7 %collective-permute-start.18 = (bf16[64,256]{1,0:T(8,128)(2,1)S(1)}, bf16[64,256]{1,0:T(8,128)(2,1)S(1)}, u32[]{:S(2)}, u32[]{:S(2)}) collective-permute-start(bf16[64,256]{1,0:T(8,128)(2,1)S(1)} %get-tuple-element.32), channel_id=1, source_target_pairs={{0,8},{1,12},{4,9},{5,13},{8,0},{9,4},{12,1},{13,5},{2,10},{3,14},... | collective-permute-start | bytes 98312 | tf_op jit(solution)/shard_map/ppermute | solution.py:304
  86.3 0.1 collective-permute-start.19
  86.5 0.9 collective-permute-done.17
  87.4 2.2 %collective-permute-done.18 = bf16[64,256]{1,0:T(8,128)(2,1)S(1)} collective-permute-done((bf16[64,256]{1,0:T(8,128)(2,1)S(1)}, bf16[64,256]{1,0:T(8,128)(2,1)S(1)}, u32[]{:S(2)}, u32[]{:S(2)}) %collective-permute-start.18) | collective-permute-done | bytes 32800 | tf_op jit(solution)/shard_map/ppermute | solution.py:304
  89.5 2.5 %collective-permute-done.19 = bf16[64,256]{1,0:T(8,128)(2,1)S(1)} collective-permute-done((bf16[64,256]{1,0:T(8,128)(2,1)S(1)}, bf16[64,256]{1,0:T(8,128)(2,1)S(1)}, u32[]{:S(2)}, u32[]{:S(2)}) %collective-permute-start.19) | collective-permute-done | bytes 32800 | tf_op jit(solution)/shard_map/ppermute | solution.py:304
  92.1 1.2 %gather_fusion.3 = f32[8,8,256]{2,1,0:T(8,128)} fusion(f32[8,8,256]{2,1,0:T(8,128)S(1)} %add_bitcast_fusion, s32[1024]{0:T(1024)S(1)} %pad_clamp_fusion), kind=kCustom, calls=%fused_computation.3 | custom fusion | bytes 131104 | tf_op jit(solution)/shard_map/gather | solution.py:375
  (43 shorter events, 0.9 us)
Async XLA Ops:
  0.0 9.9 %copy-start.1 = (s32[8,3]{0,1:T(4,128)S(1)}, s32[8,3]{0,1:T(4,128)}, u32[]{:S(2)}) copy-start(s32[8,3]{0,1:T(4,128)} %param.9) | copy-start | bytes 292
  0.0 66.8 %collective-permute-start.13 = (bf16[2048,1024]{1,0:T(8,128)(2,1)}, bf16[2048,1024]{1,0:T(8,128)(2,1)}, u32[]{:S(2)}, u32[]{:S(2)}) collective-permute-start(bf16[2048,1024]{1,0:T(8,128)(2,1)} %bitcast.60), channel_id=1, source_target_pairs={{0,1},{1,0},{2,3},{3,2},{4,5},{5,4},{6,7},{7,6},{8,9},{9,8},{10,11... | collective-permute-start | bytes 12582920 | tf_op jit(solution)/shard_map/ppermute | solution.py:62
  2.8 10.2 %collective-permute-start.4 = (bf16[11,8,1024]{2,1,0:T(8,128)(2,1)S(1)}, bf16[11,8,1024]{2,1,0:T(8,128)(2,1)S(1)}, u32[]{:S(2)}, u32[]{:S(2)}) collective-permute-start(bf16[11,8,1024]{2,1,0:T(8,128)(2,1)S(1)} %get-tuple-element.34), channel_id=1, source_target_pairs={{0,12},{4,8},{8,4},{12,0},{1,13},{5,9},{9,5},{13,1},{2,14},{6,10},... | collective-permute-start | bytes 540680 | tf_op jit(solution)/shard_map/ppermute | solution.py:62
  7.5 16.0 %collective-permute-start.2 = (bf16[11,8,1024]{2,1,0:T(8,128)(2,1)S(1)}, bf16[11,8,1024]{2,1,0:T(8,128)(2,1)S(1)}, u32[]{:S(2)}, u32[]{:S(2)}) collective-permute-start(bf16[11,8,1024]{2,1,0:T(8,128)(2,1)S(1)} %get-tuple-element.35), channel_id=1, source_target_pairs={{0,8},{4,12},{8,0},{12,4},{1,9},{5,13},{9,1},{13,5},{2,10},{6,14},... | collective-permute-start | bytes 540680 | tf_op jit(solution)/shard_map/ppermute | solution.py:62
  7.5 16.0 %collective-permute-start = (bf16[11,8,1024]{2,1,0:T(8,128)(2,1)S(1)}, bf16[11,8,1024]{2,1,0:T(8,128)(2,1)S(1)}, u32[]{:S(2)}, u32[]{:S(2)}) collective-permute-start(bf16[11,8,1024]{2,1,0:T(8,128)(2,1)S(1)} %get-tuple-element.36), channel_id=1, source_target_pairs={{0,4},{4,0},{8,12},{12,8},{1,5},{5,1},{9,13},{13,9},{2,6},{6,2},{1... | collective-permute-start | bytes 540680 | tf_op jit(solution)/shard_map/ppermute | solution.py:62
  23.5 4.5 %collective-permute-start.6 = (bf16[4,3,8,1024]{3,2,1,0:T(8,128)(2,1)S(1)}, bf16[4,3,8,1024]{3,2,1,0:T(8,128)(2,1)S(1)}, u32[]{:S(2)}, u32[]{:S(2)}) collective-permute-start(bf16[4,3,8,1024]{3,2,1,0:T(8,128)(2,1)S(1)} %pad_maximum_fusion.4), channel_id=1, source_target_pairs={{0,1},{1,0},{2,3},{3,2},{4,5},{5,4},{6,7},{7,6},{8,9},{9,8},{10,11... | collective-permute-start | bytes 589832 | tf_op jit(solution)/shard_map/ppermute | solution.py:62
  24.2 6.4 %collective-permute-start.1 = (bf16[8,8,1024]{2,1,0:T(8,128)(2,1)S(1)}, bf16[8,8,1024]{2,1,0:T(8,128)(2,1)S(1)}, u32[]{:S(2)}, u32[]{:S(2)}) collective-permute-start(bf16[8,8,1024]{2,1,0:T(8,128)(2,1)S(1)} %slice.52), channel_id=1, source_target_pairs={{0,16},{16,0},{1,17},{17,1},{2,18},{18,2},{3,19},{19,3},{4,20},{20... | collective-permute-start | bytes 393224 | tf_op jit(solution)/shard_map/ppermute | solution.py:62
  25.8 7.6 %collective-permute-start.3 = (bf16[8,8,1024]{2,1,0:T(8,128)(2,1)S(1)}, bf16[8,8,1024]{2,1,0:T(8,128)(2,1)S(1)}, u32[]{:S(2)}, u32[]{:S(2)}) collective-permute-start(bf16[8,8,1024]{2,1,0:T(8,128)(2,1)S(1)} %slice.53), channel_id=1, source_target_pairs={{0,16},{16,0},{1,17},{17,1},{2,18},{18,2},{3,19},{19,3},{4,20},{20... | collective-permute-start | bytes 393224 | tf_op jit(solution)/shard_map/ppermute | solution.py:62
  26.3 9.4 %collective-permute-start.5 = (bf16[8,8,1024]{2,1,0:T(8,128)(2,1)S(1)}, bf16[8,8,1024]{2,1,0:T(8,128)(2,1)S(1)}, u32[]{:S(2)}, u32[]{:S(2)}) collective-permute-start(bf16[8,8,1024]{2,1,0:T(8,128)(2,1)S(1)} %slice.54), channel_id=1, source_target_pairs={{0,16},{16,0},{1,17},{17,1},{2,18},{18,2},{3,19},{19,3},{4,20},{20... | collective-permute-start | bytes 393224 | tf_op jit(solution)/shard_map/ppermute | solution.py:62
  39.2 12.2 %collective-permute-start.7 = (bf16[8,16,1024]{2,1,0:T(8,128)(2,1)S(1)}, bf16[8,16,1024]{2,1,0:T(8,128)(2,1)S(1)}, u32[]{:S(2)}, u32[]{:S(2)}) collective-permute-start(bf16[8,16,1024]{2,1,0:T(8,128)(2,1)S(1)} %get-tuple-element.14), channel_id=1, source_target_pairs={{0,4},{4,0},{8,12},{12,8},{1,5},{5,1},{9,13},{13,9},{2,6},{6,2},{1... | collective-permute-start | bytes 786440 | tf_op jit(solution)/shard_map/ppermute | solution.py:62
  39.3 16.0 %collective-permute-start.11 = (bf16[8,16,1024]{2,1,0:T(8,128)(2,1)S(1)}, bf16[8,16,1024]{2,1,0:T(8,128)(2,1)S(1)}, u32[]{:S(2)}, u32[]{:S(2)}) collective-permute-start(bf16[8,16,1024]{2,1,0:T(8,128)(2,1)S(1)} %get-tuple-element.14), channel_id=1, source_target_pairs={{0,2},{2,0},{1,3},{3,1},{4,6},{6,4},{5,7},{7,5},{8,10},{10,8},{9,1... | collective-permute-start | bytes 786440 | tf_op jit(solution)/shard_map/ppermute | solution.py:62
  40.8 21.0 %collective-permute-start.14 = (bf16[8,16,1024]{2,1,0:T(8,128)(2,1)S(1)}, bf16[8,16,1024]{2,1,0:T(8,128)(2,1)S(1)}, u32[]{:S(2)}, u32[]{:S(2)}) collective-permute-start(bf16[8,16,1024]{2,1,0:T(8,128)(2,1)S(1)} %get-tuple-element.19), channel_id=1, source_target_pairs={{0,8},{4,12},{8,0},{12,4},{1,9},{5,13},{9,1},{13,5},{2,10},{6,14},... | collective-permute-start | bytes 786440 | tf_op jit(solution)/shard_map/ppermute | solution.py:62
  51.4 11.0 %collective-permute-start.8 = (bf16[8,16,1024]{2,1,0:T(8,128)(2,1)S(1)}, bf16[8,16,1024]{2,1,0:T(8,128)(2,1)S(1)}, u32[]{:S(2)}, u32[]{:S(2)}) collective-permute-start(bf16[8,16,1024]{2,1,0:T(8,128)(2,1)S(1)} %get-tuple-element.15), channel_id=1, source_target_pairs={{0,12},{4,8},{8,4},{12,0},{1,13},{5,9},{9,5},{13,1},{2,14},{6,10},... | collective-permute-start | bytes 786440 | tf_op jit(solution)/shard_map/ppermute | solution.py:62
  52.7 12.4 %collective-permute-start.10 = (bf16[8,16,1024]{2,1,0:T(8,128)(2,1)S(1)}, bf16[8,16,1024]{2,1,0:T(8,128)(2,1)S(1)}, u32[]{:S(2)}, u32[]{:S(2)}) collective-permute-start(bf16[8,16,1024]{2,1,0:T(8,128)(2,1)S(1)} %get-tuple-element.16.refs_0_), channel_id=1, source_target_pairs={{0,2},{2,0},{1,3},{3,1},{4,6},{6,4},{5,7},{7,5},{8,10},{10,8},{9,1... | collective-permute-start | bytes 786440 | tf_op jit(solution)/shard_map/ppermute | solution.py:62
  55.2 11.6 %collective-permute-start.12 = (bf16[8,16,1024]{2,1,0:T(8,128)(2,1)S(1)}, bf16[8,16,1024]{2,1,0:T(8,128)(2,1)S(1)}, u32[]{:S(2)}, u32[]{:S(2)}) collective-permute-start(bf16[8,16,1024]{2,1,0:T(8,128)(2,1)S(1)} %collective-permute-done.11), channel_id=1, source_target_pairs={{0,4},{4,0},{8,12},{12,8},{1,5},{5,1},{9,13},{13,9},{2,6},{6,2},{1... | collective-permute-start | bytes 786440 | tf_op jit(solution)/shard_map/ppermute | solution.py:62
  61.9 13.3 %collective-permute-start.15 = (bf16[8,16,1024]{2,1,0:T(8,128)(2,1)S(1)}, bf16[8,16,1024]{2,1,0:T(8,128)(2,1)S(1)}, u32[]{:S(2)}, u32[]{:S(2)}) collective-permute-start(bf16[8,16,1024]{2,1,0:T(8,128)(2,1)S(1)} %collective-permute-done.14.near_ref), channel_id=1, source_target_pairs={{0,2},{2,0},{1,3},{3,1},{4,6},{6,4},{5,7},{7,5},{8,10},{10,8},{9,1... | collective-permute-start | bytes 786440 | tf_op jit(solution)/shard_map/ppermute | solution.py:62
  62.4 15.7 %collective-permute-start.9 = (bf16[8,16,1024]{2,1,0:T(8,128)(2,1)S(1)}, bf16[8,16,1024]{2,1,0:T(8,128)(2,1)S(1)}, u32[]{:S(2)}, u32[]{:S(2)}) collective-permute-start(bf16[8,16,1024]{2,1,0:T(8,128)(2,1)S(1)} %collective-permute-done.8.near_ref), channel_id=1, source_target_pairs={{0,2},{2,0},{1,3},{3,1},{4,6},{6,4},{5,7},{7,5},{8,10},{10,8},{9,1... | collective-permute-start | bytes 786440 | tf_op jit(solution)/shard_map/ppermute | solution.py:62
  66.8 2.2 %copy-start = (bf16[256,8,1024]{2,1,0:T(8,128)(2,1)S(1)}, bf16[256,8,1024]{2,1,0:T(8,128)(2,1)}, u32[]{:S(2)}) copy-start(bf16[256,8,1024]{2,1,0:T(8,128)(2,1)} %param.5) | copy-start | bytes 12582916
  81.7 4.8 %collective-permute-start.16 = (bf16[64,256]{1,0:T(8,128)(2,1)S(1)}, bf16[64,256]{1,0:T(8,128)(2,1)S(1)}, u32[]{:S(2)}, u32[]{:S(2)}) collective-permute-start(bf16[64,256]{1,0:T(8,128)(2,1)S(1)} %get-tuple-element.30), channel_id=1, source_target_pairs={{0,0},{1,4},{4,1},{5,5},{8,8},{9,12},{12,9},{13,13},{2,2},{3,6},{6... | collective-permute-start | bytes 98312 | tf_op jit(solution)/shard_map/ppermute | solution.py:304
  82.3 5.0 %collective-permute-start.17 = (bf16[64,256]{1,0:T(8,128)(2,1)S(1)}, bf16[64,256]{1,0:T(8,128)(2,1)S(1)}, u32[]{:S(2)}, u32[]{:S(2)}) collective-permute-start(bf16[64,256]{1,0:T(8,128)(2,1)S(1)} %get-tuple-element.33), channel_id=1, source_target_pairs={{0,1},{1,5},{4,0},{5,4},{8,9},{9,13},{12,8},{13,12},{2,3},{3,7},{6... | collective-permute-start | bytes 98312 | tf_op jit(solution)/shard_map/ppermute | solution.py:304
  84.6 4.9 %collective-permute-start.18 = (bf16[64,256]{1,0:T(8,128)(2,1)S(1)}, bf16[64,256]{1,0:T(8,128)(2,1)S(1)}, u32[]{:S(2)}, u32[]{:S(2)}) collective-permute-start(bf16[64,256]{1,0:T(8,128)(2,1)S(1)} %get-tuple-element.32), channel_id=1, source_target_pairs={{0,8},{1,12},{4,9},{5,13},{8,0},{9,4},{12,1},{13,5},{2,10},{3,14},... | collective-permute-start | bytes 98312 | tf_op jit(solution)/shard_map/ppermute | solution.py:304
  86.3 5.7 %collective-permute-start.19 = (bf16[64,256]{1,0:T(8,128)(2,1)S(1)}, bf16[64,256]{1,0:T(8,128)(2,1)S(1)}, u32[]{:S(2)}, u32[]{:S(2)}) collective-permute-start(bf16[64,256]{1,0:T(8,128)(2,1)S(1)} %get-tuple-element.31), channel_id=1, source_target_pairs={{0,9},{1,13},{4,8},{5,12},{8,1},{9,5},{12,0},{13,4},{2,11},{3,15},... | collective-permute-start | bytes 98312 | tf_op jit(solution)/shard_map/ppermute | solution.py:304

commit v4 on v3

--- a/solution.py
+++ b/solution.py
@@ -62,11 +62,11 @@
     return lax.ppermute(value, axis, [(i, i ^ step) for i in range(count)])
 
 
-def contract_kernel(planes, *refs):
-    halves = refs[: 2 * planes]
-    occ_ref, virt_ref = refs[2 * planes : 2 * planes + 2]
-    outs = refs[2 * planes + 2 : 3 * planes + 2]
-    even_ref, odd_ref, weight_ref, inner_ref, sums_ref = refs[3 * planes + 2 :]
+def contract_kernel(planes, part_ref, *refs):
+    pieces = refs[: 2 * planes - 2]
+    occ_ref, virt_ref = refs[2 * planes - 2 : 2 * planes]
+    outs = refs[2 * planes : 3 * planes + 1]
+    even_ref, odd_ref, weight_ref, inner_ref, sums_ref = refs[3 * planes + 1 :]
     blocks, own, cols = outs[0].shape
     width = virt_ref.shape[1]
     reach = (width - 1) // 2
@@ -76,8 +76,11 @@
     f32 = jnp.float32
     for plane in range(planes):
         for p in range(own):
-            half = halves[2 * plane + p // (own // 2)]
-            value = half[p % (own // 2)].astype(f32)
+            if plane < 2:
+                piece, at = pieces[plane], part_ref[0] * (own // 2) ^ p
+            else:
+                piece, at = pieces[2 * plane - 2 + p // (own // 2)], p % (own // 2)
+            value = piece[at].astype(f32)
             target = even_ref if p % 2 == 0 else odd_ref
             for u in range(units):
                 start = (p // 2) * rows + plane * units + u
@@ -135,15 +138,17 @@
         for plane in range(planes):
             for u in range(units):
                 start = ((m * planes + plane) * units + u) * own
-                outs[plane][m, :, u * LANES : (u + 1) * LANES] = sums_ref[
+                into, at = outs[plane], m
+                if plane == planes - 1 and m >= blocks // 2:
+                    into, at = outs[planes], m - blocks // 2
+                into[at, :, u * LANES : (u + 1) * LANES] = sums_ref[
                     start : start + own, :
                 ].astype(jnp.bfloat16)
 
 
-def contract(halves, occ, virt):
-    planes = len(halves) // 2
-    half, blocks, cols = halves[1].shape
-    own = 2 * half
+def contract(part, pieces, occ, virt):
+    planes = len(pieces) // 2 + 1
+    own, blocks, cols = pieces[0].shape
     width = virt.shape[1]
     units = cols // LANES
     pairs = own // PAIR
@@ -151,9 +156,10 @@
     whole = pl.BlockSpec(memory_space=pltpu.VMEM)
     return pl.pallas_call(
         functools.partial(contract_kernel, planes),
-        out_shape=[jax.ShapeDtypeStruct((blocks, own, cols), jnp.bfloat16)] * planes,
-        in_specs=[whole] * (2 * planes + 2),
-        out_specs=[whole] * planes,
+        out_shape=[jax.ShapeDtypeStruct((blocks, own, cols), jnp.bfloat16)] * (planes - 1)
+        + [jax.ShapeDtypeStruct((blocks // 2, own, cols), jnp.bfloat16)] * 2,
+        in_specs=[pl.BlockSpec(memory_space=pltpu.SMEM)] + [whole] * (2 * planes),
+        out_specs=[whole] * (planes + 1),
         scratch_shapes=[
             pltpu.VMEM((blocks * pairs * rows, LANES), jnp.float32),
             pltpu.VMEM((blocks * pairs * rows, LANES), jnp.float32),
@@ -164,134 +170,82 @@
         compiler_params=pltpu.CompilerParams(vmem_limit_bytes=20 * 1024 * 1024),
         cost_estimate=TINY,
         name="contract_slab",
-    )(*halves, occ, virt)
-
-
-def add_terms(k, near, far, rows_ref, keep_ref, core, cross_refs, into_ref):
-    blocks, own, cols = near.shape
-    rows = rows_ref.shape[0] // blocks
-    right = jnp.concatenate(
-        [near[...].reshape(blocks * own, cols), far[...].reshape(blocks * own, cols)], axis=0
-    )
-    some = 64
-    group = lax.broadcasted_iota(jnp.int32, (some, LANES), 1) // own
-    for part in range(rows // some):
-        cross = lax.dot_general(
-            rows_ref[part * some * blocks : (part + 1) * some * blocks, :],
-            right,
-            (((1,), (1,)), ((), ())),
-            preferred_element_type=jnp.float32,
+    )(part.reshape(1), *pieces, occ, virt)
+
+
+def product(right, masked_ref):
+    total = None
+    for m in range(masked_ref.shape[0]):
+        term = lax.dot_general(
+            masked_ref[m], right[m], (((1,), (1,)), ((), ())), preferred_element_type=jnp.float32
         )
-        keep = keep_ref[core, part * some // RB][None, :]
-        for side in range(2):
-            hold = cross_refs.at[part % 2, side]
-            hold[...] = cross[:, side * LANES : (side + 1) * LANES]
-            total = hold[pl.ds(0, some, stride=blocks), :]
-            for m in range(1, blocks):
-                total = jnp.where(group == m, hold[pl.ds(m, some, stride=blocks), :], total)
-            total = total * keep
-            shift = LANES // 2
-            while shift >= own:
-                total = total + pltpu.roll(total, shift, 1)
-                shift //= 2
-            at = slice(part * some, (part + 1) * some)
-            into_ref[core, at, :] = jnp.where(
-                group == 2 * k + side, total, into_ref[core, at, :]
-            )
-
-
-def first_kernel(count, keep_ref, *refs):
-    parts, sources = refs[: 2 * count], refs[2 * count : 2 * count + 2]
-    out_ref, *kept = refs[2 * count + 2 : 2 * count + 5]
-    cross_refs, sem = refs[2 * count + 5 :]
-    copies = [pltpu.make_async_copy(sources[c], kept[c], sem.at[c]) for c in range(2)]
-    for copy in copies:
-        copy.start()
-    out_ref[...] = jnp.zeros_like(out_ref)
+        total = term if total is None else total + term
+    return total
+
+
+WHOLE = pl.BlockSpec(memory_space=pltpu.VMEM)
+SMALL = pltpu.CompilerParams(vmem_limit_bytes=16 * 1024 * 1024)
+
+
+def early_kernel(count, *refs):
+    parts, masked_refs, out_ref = refs[:count], refs[count : count + 2], refs[count + 2]
+    blocks, own, cols = parts[0].shape
+    nothing = jnp.zeros((LANES - count * own, cols), jnp.bfloat16)
+    right = []
+    for m in range(blocks):
+        right.append(jnp.concatenate([part[m] for part in parts] + [nothing], axis=0))
     for core in range(2):
-        copies[core].wait()
-        for k in range(count):
-            add_terms(k, parts[2 * k], parts[2 * k + 1], kept[core], keep_ref, core, cross_refs, out_ref)
-
-
-def next_kernel(k, keep_ref, near_ref, far_ref, own_ref, other_ref, early_ref, out_ref, cross_refs):
-    out_ref[...] = early_ref[...]
-    for core, rows_ref in enumerate((own_ref, other_ref)):
-        add_terms(k, near_ref, far_ref, rows_ref, keep_ref, core, cross_refs, out_ref)
-
-
-def last_kernel(
-    place_ref, keep_ref, near_ref, far_ref, own_ref, other_ref, early_ref, out_ref, hold_ref, turn_ref, cross_refs
-):
-    count, own = out_ref.shape[0], near_ref.shape[1]
-    hold_ref[...] = early_ref[...]
-    for core, rows_ref in enumerate((own_ref, other_ref)):
-        add_terms(count - 1, near_ref, far_ref, rows_ref, keep_ref, core, cross_refs, hold_ref)
-        turn_ref[core] = hold_ref[core].T
+        out_ref[core] = product(right, masked_refs[core])
+
+
+def early_terms(parts, masked):
+    rows_dev = masked[0].shape[1]
+    return pl.pallas_call(
+        functools.partial(early_kernel, len(parts)),
+        out_shape=jax.ShapeDtypeStruct((2, rows_dev, LANES), jnp.float32),
+        in_specs=[WHOLE] * (len(parts) + 2),
+        out_specs=WHOLE,
+        compiler_params=SMALL,
+        cost_estimate=TINY,
+        name="early_terms",
+    )(*parts, *masked)
+
+
+def final_kernel(place_ref, *refs):
+    near, far = refs[:2], refs[2:4]
+    own_ref, other_ref, early_ref, out_ref, hold_ref = refs[4:]
+    count = out_ref.shape[0]
+    part, own, cols = near[0].shape
+    nothing = jnp.zeros((LANES - 2 * own, cols), jnp.bfloat16)
+    right = []
+    for m in range(2 * part):
+        rows = [nothing, near[m // part][m % part], far[m // part][m % part]]
+        right.append(jnp.concatenate(rows, axis=0))
+    for core, masked_ref in enumerate((own_ref, other_ref)):
+        hold_ref[core] = (early_ref[core] + product(right, masked_ref)).T
     for route in range(count):
         side, core = place_ref[0] ^ (route // 2), place_ref[1] ^ (route % 2)
         for p in range(count):
             start = pl.multiple_of((2 * (p ^ route) + side) * own, own)
-            out_ref[route, p * own : (p + 1) * own, :] = turn_ref[
+            out_ref[route, p * own : (p + 1) * own, :] = hold_ref[
                 core, pl.ds(start, own), :
             ].astype(jnp.bfloat16)
 
 
-WHOLE = pl.BlockSpec(memory_space=pltpu.VMEM)
-PARAMS = pltpu.CompilerParams(vmem_limit_bytes=20 * 1024 * 1024)
-
-
-def cross_scratch(blocks):
-    return pltpu.VMEM((2, 2, 64 * blocks, LANES), jnp.float32)
-
-
-def first_terms(keep, parts, sources):
-    blocks, own, cols = parts[0].shape
-    rows = sources[0].shape[0]
-    return pl.pallas_call(
-        functools.partial(first_kernel, len(parts) // 2),
-        out_shape=[jax.ShapeDtypeStruct((2, rows // blocks, LANES), jnp.float32)]
-        + [pltpu.VMEM((rows, cols), jnp.bfloat16)] * 2,
-        in_specs=[WHOLE] * (len(parts) + 1) + [pl.BlockSpec(memory_space=pl.ANY)] * 2,
-        out_specs=[WHOLE] * 3,
-        scratch_shapes=[cross_scratch(blocks), pltpu.SemaphoreType.DMA((2,))],
-        compiler_params=PARAMS,
-        cost_estimate=TINY,
-        name="first_terms",
-    )(keep, *parts, *sources)
-
-
-def next_terms(k, keep, near, far, rows, early):
-    return pl.pallas_call(
-        functools.partial(next_kernel, k),
-        out_shape=jax.ShapeDtypeStruct(early.shape, jnp.float32),
-        in_specs=[WHOLE] * 6,
-        out_specs=WHOLE,
-        scratch_shapes=[cross_scratch(near.shape[0])],
-        compiler_params=PARAMS,
-        cost_estimate=TINY,
-        name="next_terms",
-    )(keep, near, far, *rows, early)
-
-
-def last_terms(place, keep, near, far, rows, early):
-    own = near.shape[1]
-    rows_dev = early.shape[1]
+def final_terms(place, near, far, masked, early):
+    own = near[0].shape[1]
+    rows_dev = masked[0].shape[1]
     count = LANES // (2 * own)
     return pl.pallas_call(
-        last_kernel,
+        final_kernel,
         out_shape=jax.ShapeDtypeStruct((count, count * own, rows_dev), jnp.bfloat16),
-        in_specs=[pl.BlockSpec(memory_space=pltpu.SMEM)] + [WHOLE] * 6,
+        in_specs=[pl.BlockSpec(memory_space=pltpu.SMEM)] + [WHOLE] * 7,
         out_specs=WHOLE,
-        scratch_shapes=[
-            pltpu.VMEM(early.shape, jnp.float32),
-            pltpu.VMEM((2, LANES, rows_dev), jnp.float32),
-            cross_scratch(near.shape[0]),
-        ],
-        compiler_params=PARAMS,
+        scratch_shapes=[pltpu.VMEM((2, LANES, rows_dev), jnp.float32)],
+        compiler_params=SMALL,
         cost_estimate=TINY,
-        name="last_terms",
-    )(place, keep, near, far, *rows, early)
+        name="final_terms",
+    )(place, *near, *far, *masked, early)
 
 
 def routed(value, route):
@@ -308,7 +262,7 @@
     return lax.optimization_barrier((value,) + others)[0]
 
 
-def swapped_plan(tensor, mask_rows, other_mask_rows, occ_green, virt_green, green_mask):
+def swapped_plan(tensor, mask_rows, occ_green, virt_green, green_mask):
     planes = lax.axis_size("ao")
     steps = range(1, planes)
     z = lax.axis_index("ao")
@@ -324,19 +278,22 @@
         return lax.dynamic_slice_in_dim(tensor, plane * own + part * half, half, 0)
 
     mine = jnp.where(core == 0, occ_green, virt_green).reshape(-1, blocks, cols)
-    leaving = [jnp.concatenate([rows_of(z ^ k, side), mine]) for k in steps]
-    direct = [swap(leaving[k - 1], "ao", k) for k in steps]
-    halves = [rows_of(z, side), rows_of(z, 1 - side)]
-    for value in direct:
-        halves += [value, swap(value[:half], "tpoint", 1)]
-    stacked = jnp.stack([mine] + [value[half:] for value in direct])
+    whole = lax.dynamic_slice_in_dim(tensor, (z ^ 1) * own, own, 0)
+    first = swap(jnp.concatenate([whole, mine]), "ao", 1)
+    direct = [swap(jnp.concatenate([rows_of(z ^ k, side), mine]), "ao", k) for k in (2, 3)]
+    hops = {3: swap(direct[1][:half], "tpoint", 1)}
+    hops[2] = swap(direct[0][:half], "tpoint", 1)
+    pieces = [lax.dynamic_slice_in_dim(tensor, z * own, own, 0), first]
+    for k in (2, 3):
+        pieces += [direct[k - 2], hops[k]]
+    stacked = jnp.stack([mine, first[own:], direct[0][half:], direct[1][half:]])
     order = jnp.arange(planes) ^ z
     other = swap(stacked, "rep", 1)
     shape = (blocks,) + occ_green.shape[1:]
     mine_all = stacked[order].reshape(shape)
     other_all = other[order].reshape(shape)
-    rows = tensor.reshape(rows_dev * blocks, cols)
-    rows = (rows, swap(rows, "rep", 1))
+    row_mask = jnp.repeat(mask_rows, RB, axis=0).astype(jnp.bfloat16)
+    masked = jnp.swapaxes(tensor, 0, 1) * row_mask.T[:, :, None]
     occ_mask, virt_mask = pair_masks(green_mask, mask_rows[0])
     occ = jnp.where(core == 0, mine_all, other_all) * occ_mask[:, :, None, None]
     virt = jnp.where(core == 0, other_all, mine_all) * virt_mask[:, :, None, None]
@@ -356,16 +313,22 @@
         ],
         axis=2,
     )
-    sums = contract(halves, occ, virt)
-    near = [sums[0], swap(sums[1], "ao", 1), swap(sums[2], "ao", 2)]
-    near.append(swap(after(sums[3], near[1]), "ao", 3))
-    far = [swap(value, "aux", 1) for value in (sums[0], sums[1], near[2], near[3])]
-    far[1] = swap(far[1], "ao", 1)
-    keep = jnp.repeat(jnp.stack([mask_rows, other_mask_rows]), own, axis=2).astype(jnp.float32)
-    early, *rows = first_terms(keep, [near[0], far[0], near[1], far[1]], rows)
-    early = next_terms(2, keep, near[2], far[2], rows, early)
+    pieces[0], masked = lax.optimization_barrier((pieces[0], masked))
+    sums = contract(side, pieces, occ, virt)
+    masked = (masked, swap(after(masked, sums[0]), "rep", 1))
+    near1, near2 = swap(sums[1], "ao", 1), swap(sums[2], "ao", 2)
+    far0, across = swap(sums[0], "aux", 1), swap(sums[1], "aux", 1)
+    far1 = swap(across, "ao", 1)
+    near3 = [
+        swap(after(sums[3], across, masked[1]), "ao", 3),
+        swap(after(sums[4], near1, far0), "ao", 3),
+    ]
+    far2 = swap(near2, "aux", 1)
+    far3 = [swap(after(near3[0], far1), "aux", 1), swap(near3[1], "aux", 1)]
+    parts = [sums[0], far0, near1, far1, near2, far2]
+    early = early_terms(parts, masked)
     place = jnp.stack([(z // 2) ^ aux, (z % 2) ^ core]).astype(jnp.int32)
-    leaving = last_terms(place, keep, near[3], far[3], rows, early)
+    leaving = final_terms(place, near3, far3, masked, early)
     total = None
     for route in range(planes):
         term = routed(leaving[route], route).astype(jnp.float32)
@@ -388,9 +351,7 @@
     simple = sizes == (2, 4, 2, 2) and cols * planes == AOB * AOB and SL // planes == 16
     simple = simple and blocks * 16 == LANES and rows_dev % RB == 0 and occ_green.shape[1] == 3
     if simple:
-        return swapped_plan(
-            tensor, mask_of(shard), mask_of(shard ^ 1), occ_green, virt_green, green_mask
-        )
+        return swapped_plan(tensor, mask_of(shard), occ_green, virt_green, green_mask)
     return gathered_plan(tensor, mask_of(shard), occ_green, virt_green, green_mask)
 
 

time: 93.5 us -> 87.5 us (0.936)
  the two profiles are of different devices: /device:TPU:0 before, /device:TPU:1 now
where the time goes in v4:
time: 87.5 us; the launch traced here: 87.3 us
  starting transfers between devices  28.1 us (32%)
  waiting for transfers between devices  23 us (26%)
  local copies, waits for them, and re-layouts  14.2 us (16%)
  other arithmetic  12.1 us (14%)
  Pallas kernels  8.72 us (10%)
    ppermute x17, waiting for transfers between devices, swap(): return lax.ppermute(value, axis, [(i, i ^ step) for i in range(count)])  20.5 us
    ppermute x17, starting transfers between devices, swap(): return lax.ppermute(value, axis, [(i, i ^ step) for i in range(count)])  20.1 us
    mul x1, other arithmetic, swapped_plan(): masked = jnp.swapaxes(tensor, 0, 1) * row_mask.T[:, :, None]  10.1 us
    ppermute x4, starting transfers between devices, routed(): return lax.ppermute(value, ('ao', 'rep'), pairs)  8.08 us
    unnamed x15, local copies, waits for them, and re-layouts  7.63 us
    pallas_call x1, Pallas kernels, contract(): pl.pallas_call(functools.partial(contract_kernel, planes), out_shape=[jax...  3.46 us
    pallas_call x1, Pallas kernels, final_terms(): pl.pallas_call(final_kernel, out_shape=jax.ShapeDtypeStruct((count, count...  2.97 us
    ppermute x4, waiting for transfers between devices, routed(): return lax.ppermute(value, ('ao', 'rep'), pairs)  2.56 us
  transfers between devices with their start and end apart: 21, of which 8 were waited for; matrix products, arithmetic and copies ran while one was open for 18% of the time, Pallas kernels for 3%

profile of v4, /device:TPU:1, one launch (start us, length us, event | category | flops | bytes accessed | tf_op | source)
XLA Modules:
  0.0 87.3 jit_solution(16196811037581157495)
XLA Ops:
  0.0 0.9 %broadcast_select_fusion.2 = bf16[2,3,64,64]{3,2,1,0:T(8,128)(2,1)S(1)} fusion(bf16[2,3,64,64]{3,2,1,0:T(8,128)(2,1)} %param.7, bf16[2,3,64,64]{3,2,1,0:T(8,128)(2,1)} %param.8, pred[]{:T(512)S(6)} %eq.12), kind=kLoop, calls=%fused_computation.19 | loop fusion | flops 24576 | bytes 147457 | tf_op jit(solution)/shard_map/jit(_where)/select_n | solution.py:280
  1.0 1.1 %constant_dynamic-slice_fusion.2 = (bf16[16,8,1024]{2,1,0:T(8,128)(2,1)S(1)}, bf16[16,8,1024]{2,1,0:T(8,128)(2,1)S(1)}) fusion(bf16[256,8,1024]{2,1,0:T(8,128)(2,1)} %param.5, s32[]{:T(128)S(6)} %select_n.126, s32[]{:T(128)S(6)} %select_n.124), kind=kLoop, calls=%fused_computation.53 | loop fusion | bytes 1048584 | tf_op jit(solution)/shard_map/dynamic_slice | solution.py:281
  2.2 2.2 %collective-permute-start = (bf16[19,8,1024]{2,1,0:T(8,128)(2,1)S(1)}, bf16[19,8,1024]{2,1,0:T(8,128)(2,1)S(1)}, u32[]{:S(2)}, u32[]{:S(2)}) collective-permute-start(bf16[19,8,1024]{2,1,0:T(8,128)(2,1)S(1)} %pad_maximum_fusion.1), channel_id=1, source_target_pairs={{0,4},{4,0},{8,12},{12,8},{1,5},{5,1},{9,13},{13,9},{2,6},{6,2},{1... | collective-permute-start | bytes 933896 | tf_op jit(solution)/shard_map/ppermute | solution.py:62
  4.4 1.0 %constant_dynamic-slice_fusion = (bf16[8,8,1024]{2,1,0:T(8,128)(2,1)S(1)}, bf16[8,8,1024]{2,1,0:T(8,128)(2,1)S(1)}) fusion(bf16[256,8,1024]{2,1,0:T(8,128)(2,1)} %param.5, s32[]{:T(128)S(6)} %select_n.130, s32[]{:T(128)S(6)} %select_n.129), kind=kLoop, calls=%fused_computation.51 | loop fusion | bytes 524296 | tf_op jit(solution)/shard_map/dynamic_slice | solution.py:278
  5.4 2.4 %collective-permute-start.1 = (bf16[11,8,1024]{2,1,0:T(8,128)(2,1)S(1)}, bf16[11,8,1024]{2,1,0:T(8,128)(2,1)S(1)}, u32[]{:S(2)}, u32[]{:S(2)}) collective-permute-start(bf16[11,8,1024]{2,1,0:T(8,128)(2,1)S(1)} %get-tuple-element.42), channel_id=1, source_target_pairs={{0,8},{4,12},{8,0},{12,4},{1,9},{5,13},{9,1},{13,5},{2,10},{6,14},... | collective-permute-start | bytes 540680 | tf_op jit(solution)/shard_map/ppermute | solution.py:62
  7.9 0.7 fusion.23
  8.7 10.1 %bitcast_multiply_fusion.refs_6_.refs_4_ = bf16[8,256,1024]{2,1,0:T(8,128)(2,1)} fusion(bf16[256,8,1024]{2,1,0:T(8,128)(2,1)} %param.5, bf16[8,256]{1,0:T(8,128)(2,1)S(1)} %broadcast_bitcast_fusion), kind=kLoop, calls=%fused_computation.4 | loop fusion | flops 2097152 | bytes 8392704 | tf_op jit(solution)/shard_map/mul | solution.py:296
  18.9 0.7 gather_fusion.2
  19.8 1.3 %collective-permute-done.3.refs_4_ = bf16[11,8,1024]{2,1,0:T(8,128)(2,1)S(1)} collective-permute-done((bf16[11,8,1024]{2,1,0:T(8,128)(2,1)S(1)}, bf16[11,8,1024]{2,1,0:T(8,128)(2,1)S(1)}, u32[]{:S(2)}, u32[]{:S(2)}) %collective-permute-start.3) | collective-permute-done | bytes 180256 | tf_op jit(solution)/shard_map/ppermute | solution.py:62
  21.2 1.7 %collective-permute-start.5 = (bf16[4,3,8,1024]{3,2,1,0:T(8,128)(2,1)S(1)}, bf16[4,3,8,1024]{3,2,1,0:T(8,128)(2,1)S(1)}, u32[]{:S(2)}, u32[]{:S(2)}) collective-permute-start(bf16[4,3,8,1024]{3,2,1,0:T(8,128)(2,1)S(1)} %pad_maximum_fusion.4), channel_id=1, source_target_pairs={{0,1},{1,0},{2,3},{3,2},{4,5},{5,4},{6,7},{7,6},{8,9},{9,8},{10,11... | collective-permute-start | bytes 589832 | tf_op jit(solution)/shard_map/ppermute | solution.py:62
  22.9 1.3 %collective-permute-start.2 = (bf16[8,8,1024]{2,1,0:T(8,128)(2,1)S(1)}, bf16[8,8,1024]{2,1,0:T(8,128)(2,1)S(1)}, u32[]{:S(2)}, u32[]{:S(2)}) collective-permute-start(bf16[8,8,1024]{2,1,0:T(8,128)(2,1)S(1)} %slice.48), channel_id=1, source_target_pairs={{0,16},{16,0},{1,17},{17,1},{2,18},{18,2},{3,19},{19,3},{4,20},{20... | collective-permute-start | bytes 393224 | tf_op jit(solution)/shard_map/ppermute | solution.py:62
  24.2 0.3 collective-permute-start.4
  24.5 0.6 gather_fusion
  25.0 0.6 gather_fusion.1
  25.7 0.3 select_n.138
  25.9 0.7 fusion
  26.7 0.2 copy.13.refs_6_
  26.9 0.3 select_n.141
  27.3 0.2 pad_bitcast_fusion.1
  27.6 0.5 collective-permute-done.2.refs_3_
  28.0 2.8 %collective-permute-done.4.refs_5_ = bf16[8,8,1024]{2,1,0:T(8,128)(2,1)S(1)} collective-permute-done((bf16[8,8,1024]{2,1,0:T(8,128)(2,1)S(1)}, bf16[8,8,1024]{2,1,0:T(8,128)(2,1)S(1)}, u32[]{:S(2)}, u32[]{:S(2)}) %collective-permute-start.4) | collective-permute-done | bytes 131104 | tf_op jit(solution)/shard_map/ppermute | solution.py:62
  30.8 3.5 %contract_slab.1 = (bf16[8,16,1024]{2,1,0:T(8,128)(2,1)S(1)}, bf16[8,16,1024]{2,1,0:T(8,128)(2,1)S(1)}, bf16[8,16,1024]{2,1,0:T(8,128)(2,1)S(1)}, bf16[4,16,1024...) custom-call(s32[1]{0:T(128)} %bitcast.2.part_ref, bf16[16,8,1024]{2,1,0:T(8,128)(2,1)S(1)} %get-tuple-element.16.refs_0_, ...), custom_call_target="tpu_custom_call" | custom-call | flops 1 | bytes 1 | tf_op jit(solution)/shard_map/contract_slab/pallas_call | solution.py:157
  34.3 0.9 %collective-permute-start.7 = (bf16[8,256,1024]{2,1,0:T(8,128)(2,1)S(1)}, bf16[8,256,1024]{2,1,0:T(8,128)(2,1)S(1)}, u32[]{:S(2)}, u32[]{:S(2)}) collective-permute-start(bf16[8,256,1024]{2,1,0:T(8,128)(2,1)S(1)} %copy-done), channel_id=1, source_target_pairs={{0,1},{1,0},{2,3},{3,2},{4,5},{5,4},{6,7},{7,6},{8,9},{9,8},{10,11... | collective-permute-start | bytes 12582920 | tf_op jit(solution)/shard_map/ppermute | solution.py:62
  35.2 1.2 %collective-permute-start.6 = (bf16[8,16,1024]{2,1,0:T(8,128)(2,1)S(1)}, bf16[8,16,1024]{2,1,0:T(8,128)(2,1)S(1)}, u32[]{:S(2)}, u32[]{:S(2)}) collective-permute-start(bf16[8,16,1024]{2,1,0:T(8,128)(2,1)S(1)} %get-tuple-element.18), channel_id=1, source_target_pairs={{0,2},{2,0},{1,3},{3,1},{4,6},{6,4},{5,7},{7,5},{8,10},{10,8},{9,1... | collective-permute-start | bytes 786440 | tf_op jit(solution)/shard_map/ppermute | solution.py:62
  36.4 2.5 %collective-permute-start.9 = (bf16[8,16,1024]{2,1,0:T(8,128)(2,1)S(1)}, bf16[8,16,1024]{2,1,0:T(8,128)(2,1)S(1)}, u32[]{:S(2)}, u32[]{:S(2)}) collective-permute-start(bf16[8,16,1024]{2,1,0:T(8,128)(2,1)S(1)} %get-tuple-element.18), channel_id=1, source_target_pairs={{0,4},{4,0},{8,12},{12,8},{1,5},{5,1},{9,13},{13,9},{2,6},{6,2},{1... | collective-permute-start | bytes 786440 | tf_op jit(solution)/shard_map/ppermute | solution.py:62
  39.0 0.2 collective-permute-start.10
  39.2 1.0 %collective-permute-start.15 = (bf16[8,16,1024]{2,1,0:T(8,128)(2,1)S(1)}, bf16[8,16,1024]{2,1,0:T(8,128)(2,1)S(1)}, u32[]{:S(2)}, u32[]{:S(2)}) collective-permute-start(bf16[8,16,1024]{2,1,0:T(8,128)(2,1)S(1)} %get-tuple-element.26), channel_id=1, source_target_pairs={{0,8},{4,12},{8,0},{12,4},{1,9},{5,13},{9,1},{13,5},{2,10},{6,14},... | collective-permute-start | bytes 786440 | tf_op jit(solution)/shard_map/ppermute | solution.py:62
  40.2 2.9 %collective-permute-done.6 = bf16[8,16,1024]{2,1,0:T(8,128)(2,1)S(1)} collective-permute-done((bf16[8,16,1024]{2,1,0:T(8,128)(2,1)S(1)}, bf16[8,16,1024]{2,1,0:T(8,128)(2,1)S(1)}, u32[]{:S(2)}, u32[]{:S(2)}) %collective-permute-start.6) | collective-permute-done | bytes 262176 | tf_op jit(solution)/shard_map/ppermute | solution.py:62
  43.1 2.5 %collective-permute-start.12 = (bf16[8,16,1024]{2,1,0:T(8,128)(2,1)S(1)}, bf16[8,16,1024]{2,1,0:T(8,128)(2,1)S(1)}, u32[]{:S(2)}, u32[]{:S(2)}) collective-permute-start(bf16[8,16,1024]{2,1,0:T(8,128)(2,1)S(1)} %collective-permute-done.6), channel_id=1, source_target_pairs={{0,4},{4,0},{8,12},{12,8},{1,5},{5,1},{9,13},{13,9},{2,6},{6,2},{1... | collective-permute-start | bytes 786440 | tf_op jit(solution)/shard_map/ppermute | solution.py:62
  45.6 5.0 %collective-permute-done.9.refs_2_ = bf16[8,16,1024]{2,1,0:T(8,128)(2,1)S(1)} collective-permute-done((bf16[8,16,1024]{2,1,0:T(8,128)(2,1)S(1)}, bf16[8,16,1024]{2,1,0:T(8,128)(2,1)S(1)}, u32[]{:S(2)}, u32[]{:S(2)}) %collective-permute-start.9) | collective-permute-done | bytes 262176 | tf_op jit(solution)/shard_map/ppermute | solution.py:62
  50.6 1.1 %collective-permute-start.11 = (bf16[4,16,1024]{2,1,0:T(8,128)(2,1)S(1)}, bf16[4,16,1024]{2,1,0:T(8,128)(2,1)S(1)}, u32[]{:S(2)}, u32[]{:S(2)}) collective-permute-start(bf16[4,16,1024]{2,1,0:T(8,128)(2,1)S(1)} %get-tuple-element.24), channel_id=1, source_target_pairs={{0,12},{4,8},{8,4},{12,0},{1,13},{5,9},{9,5},{13,1},{2,14},{6,10},... | collective-permute-start | bytes 393224 | tf_op jit(solution)/shard_map/ppermute | solution.py:62
  51.7 2.0 %copy-done.3 = bf16[8,256,1024]{2,1,0:T(8,128)(2,1)} copy-done((bf16[8,256,1024]{2,1,0:T(8,128)(2,1)}, bf16[8,256,1024]{2,1,0:T(8,128)(2,1)S(1)}, u32[]{:S(2)}) %copy-start.3) | copy-done | bytes 4194328
  53.7 2.2 %collective-permute-start.8 = (bf16[4,16,1024]{2,1,0:T(8,128)(2,1)S(1)}, bf16[4,16,1024]{2,1,0:T(8,128)(2,1)S(1)}, u32[]{:S(2)}, u32[]{:S(2)}) collective-permute-start(bf16[4,16,1024]{2,1,0:T(8,128)(2,1)S(1)} %get-tuple-element.22), channel_id=1, source_target_pairs={{0,12},{4,8},{8,4},{12,0},{1,13},{5,9},{9,5},{13,1},{2,14},{6,10},... | collective-permute-start | bytes 393224 | tf_op jit(solution)/shard_map/ppermute | solution.py:62
  55.9 5.4 %collective-permute-done.11.refs_1_ = bf16[4,16,1024]{2,1,0:T(8,128)(2,1)S(1)} collective-permute-done((bf16[4,16,1024]{2,1,0:T(8,128)(2,1)S(1)}, bf16[4,16,1024]{2,1,0:T(8,128)(2,1)S(1)}, u32[]{:S(2)}, u32[]{:S(2)}) %collective-permute-start.11) | collective-permute-done | bytes 131104 | tf_op jit(solution)/shard_map/ppermute | solution.py:62
  61.4 0.3 collective-permute-start.14
  61.6 2.5 %collective-permute-done.8.refs_0_ = bf16[4,16,1024]{2,1,0:T(8,128)(2,1)S(1)} collective-permute-done((bf16[4,16,1024]{2,1,0:T(8,128)(2,1)S(1)}, bf16[4,16,1024]{2,1,0:T(8,128)(2,1)S(1)}, u32[]{:S(2)}, u32[]{:S(2)}) %collective-permute-start.8) | collective-permute-done | bytes 131104 | tf_op jit(solution)/shard_map/ppermute | solution.py:62
  64.2 0.3 collective-permute-start.13
  64.5 2.2 %copy-done.1 = bf16[8,256,1024]{2,1,0:T(8,128)(2,1)S(1)} copy-done((bf16[8,256,1024]{2,1,0:T(8,128)(2,1)S(1)}, bf16[8,256,1024]{2,1,0:T(8,128)(2,1)}, u32[]{:S(2)}) %copy-start.1) | copy-done | bytes 4194328
  66.7 2.2 %copy-done.4 = bf16[8,256,1024]{2,1,0:T(8,128)(2,1)S(1)} copy-done((bf16[8,256,1024]{2,1,0:T(8,128)(2,1)S(1)}, bf16[8,256,1024]{2,1,0:T(8,128)(2,1)}, u32[]{:S(2)}) %copy-start.4) | copy-done | bytes 4194328
  68.9 2.3 %early_terms.1.refs_6_ = f32[2,256,128]{2,1,0:T(8,128)S(1)} custom-call(bf16[8,16,1024]{2,1,0:T(8,128)(2,1)S(1)} %get-tuple-element.20.refs_0_, bf16[8,16,1024]{2,1,0:T(8,128)(2,1)S(1)} %collective-permute-done.10.refs_1_, bf16[8,16,1024]{2,1,0:T(8,128)(2,1)S(1)} %collective-permute-done.9.refs_2_, bf16[8,16,1024]{2,1,0:T(8,128)(2,1)S(1)} %collective-permute-done.12.refs_3_, ...), custom_call_target="tpu_custom_call" | custom-call | flops 1 | bytes 1 | tf_op jit(solution)/shard_map/early_terms/pallas_call | solution.py:203
  71.2 1.1 %copy-done.5 = bf16[8,256,1024]{2,1,0:T(8,128)(2,1)S(1)} copy-done((bf16[8,256,1024]{2,1,0:T(8,128)(2,1)S(1)}, bf16[8,256,1024]{2,1,0:T(8,128)(2,1)}, u32[]{:S(2)}) %copy-start.5) | copy-done | bytes 4194328
  72.4 3.0 %final_terms.1 = bf16[4,64,256]{2,1,0:T(8,128)(2,1)S(1)} custom-call(s32[2]{0:T(128)S(1)} %pad_add_fusion.place_ref, bf16[4,16,1024]{2,1,0:T(8,128)(2,1)S(1)} %collective-permute-done.8.refs_0_, bf16[4,16,1024]{2,1,0:T(8,128)(2,1)S(1)} %collective-permute-done.11.refs_1_, bf16[4,16,1024]{2,1,0:T(8,128)(2,1)S(1)} %collective-permute-done.13.refs_2_, ...), custom_call_target="tpu_custom_call" | custom-call | flops 1 | bytes 1 | tf_op jit(solution)/shard_map/final_terms/pallas_call | solution.py:239
  75.4 1.1 %collective-permute-start.20 = (bf16[64,256]{1,0:T(8,128)(2,1)S(1)}, bf16[64,256]{1,0:T(8,128)(2,1)S(1)}, u32[]{:S(2)}, u32[]{:S(2)}) collective-permute-start(bf16[64,256]{1,0:T(8,128)(2,1)S(1)} %get-tuple-element.38), channel_id=1, source_target_pairs={{0,9},{1,13},{4,8},{5,12},{8,1},{9,5},{12,0},{13,4},{2,11},{3,15},... | collective-permute-start | bytes 98312 | tf_op jit(solution)/shard_map/ppermute | solution.py:258
  76.5 3.9 %collective-permute-start.19 = (bf16[64,256]{1,0:T(8,128)(2,1)S(1)}, bf16[64,256]{1,0:T(8,128)(2,1)S(1)}, u32[]{:S(2)}, u32[]{:S(2)}) collective-permute-start(bf16[64,256]{1,0:T(8,128)(2,1)S(1)} %get-tuple-element.39), channel_id=1, source_target_pairs={{0,8},{1,12},{4,9},{5,13},{8,0},{9,4},{12,1},{13,5},{2,10},{3,14},... | collective-permute-start | bytes 98312 | tf_op jit(solution)/shard_map/ppermute | solution.py:258
  80.4 0.5 collective-permute-start.18
  80.8 2.6 %collective-permute-start.17 = (bf16[64,256]{1,0:T(8,128)(2,1)S(1)}, bf16[64,256]{1,0:T(8,128)(2,1)S(1)}, u32[]{:S(2)}, u32[]{:S(2)}) collective-permute-start(bf16[64,256]{1,0:T(8,128)(2,1)S(1)} %get-tuple-element.37), channel_id=1, source_target_pairs={{0,0},{1,4},{4,1},{5,5},{8,8},{9,12},{12,9},{13,13},{2,2},{3,6},{6... | collective-permute-start | bytes 98312 | tf_op jit(solution)/shard_map/ppermute | solution.py:258
  83.5 2.6 %collective-permute-done.17 = bf16[64,256]{1,0:T(8,128)(2,1)S(1)} collective-permute-done((bf16[64,256]{1,0:T(8,128)(2,1)S(1)}, bf16[64,256]{1,0:T(8,128)(2,1)S(1)}, u32[]{:S(2)}, u32[]{:S(2)}) %collective-permute-start.17) | collective-permute-done | bytes 32800 | tf_op jit(solution)/shard_map/ppermute | solution.py:258
  86.1 1.2 %gather_fusion.3 = f32[8,8,256]{2,1,0:T(8,128)} fusion(f32[8,8,256]{2,1,0:T(8,128)S(1)} %add_bitcast_fusion, s32[1024]{0:T(1024)S(1)} %pad_clamp_fusion), kind=kCustom, calls=%fused_computation.3 | custom fusion | bytes 131104 | tf_op jit(solution)/shard_map/gather | solution.py:338
  (54 shorter events, 1.1 us)
Async XLA Ops:
  2.2 18.9 %collective-permute-start = (bf16[19,8,1024]{2,1,0:T(8,128)(2,1)S(1)}, bf16[19,8,1024]{2,1,0:T(8,128)(2,1)S(1)}, u32[]{:S(2)}, u32[]{:S(2)}) collective-permute-start(bf16[19,8,1024]{2,1,0:T(8,128)(2,1)S(1)} %pad_maximum_fusion.1), channel_id=1, source_target_pairs={{0,4},{4,0},{8,12},{12,8},{1,5},{5,1},{9,13},{13,9},{2,6},{6,2},{1... | collective-permute-start | bytes 933896 | tf_op jit(solution)/shard_map/ppermute | solution.py:62
  5.4 15.7 %collective-permute-start.1 = (bf16[11,8,1024]{2,1,0:T(8,128)(2,1)S(1)}, bf16[11,8,1024]{2,1,0:T(8,128)(2,1)S(1)}, u32[]{:S(2)}, u32[]{:S(2)}) collective-permute-start(bf16[11,8,1024]{2,1,0:T(8,128)(2,1)S(1)} %get-tuple-element.42), channel_id=1, source_target_pairs={{0,8},{4,12},{8,0},{12,4},{1,9},{5,13},{9,1},{13,5},{2,10},{6,14},... | collective-permute-start | bytes 540680 | tf_op jit(solution)/shard_map/ppermute | solution.py:62
  7.8 13.3 %collective-permute-start.3 = (bf16[11,8,1024]{2,1,0:T(8,128)(2,1)S(1)}, bf16[11,8,1024]{2,1,0:T(8,128)(2,1)S(1)}, u32[]{:S(2)}, u32[]{:S(2)}) collective-permute-start(bf16[11,8,1024]{2,1,0:T(8,128)(2,1)S(1)} %get-tuple-element.41), channel_id=1, source_target_pairs={{0,12},{4,8},{8,4},{12,0},{1,13},{5,9},{9,5},{13,1},{2,14},{6,10},... | collective-permute-start | bytes 540680 | tf_op jit(solution)/shard_map/ppermute | solution.py:62
  18.8 0.9 %copy-start.6 = (s32[8,3]{0,1:T(4,128)S(1)}, s32[8,3]{0,1:T(4,128)}, u32[]{:S(2)}) copy-start(s32[8,3]{0,1:T(4,128)} %param.9) | copy-start | bytes 292
  21.2 3.9 %collective-permute-start.5 = (bf16[4,3,8,1024]{3,2,1,0:T(8,128)(2,1)S(1)}, bf16[4,3,8,1024]{3,2,1,0:T(8,128)(2,1)S(1)}, u32[]{:S(2)}, u32[]{:S(2)}) collective-permute-start(bf16[4,3,8,1024]{3,2,1,0:T(8,128)(2,1)S(1)} %pad_maximum_fusion.4), channel_id=1, source_target_pairs={{0,1},{1,0},{2,3},{3,2},{4,5},{5,4},{6,7},{7,6},{8,9},{9,8},{10,11... | collective-permute-start | bytes 589832 | tf_op jit(solution)/shard_map/ppermute | solution.py:62
  22.9 5.2 %collective-permute-start.2 = (bf16[8,8,1024]{2,1,0:T(8,128)(2,1)S(1)}, bf16[8,8,1024]{2,1,0:T(8,128)(2,1)S(1)}, u32[]{:S(2)}, u32[]{:S(2)}) collective-permute-start(bf16[8,8,1024]{2,1,0:T(8,128)(2,1)S(1)} %slice.48), channel_id=1, source_target_pairs={{0,16},{16,0},{1,17},{17,1},{2,18},{18,2},{3,19},{19,3},{4,20},{20... | collective-permute-start | bytes 393224 | tf_op jit(solution)/shard_map/ppermute | solution.py:62
  24.2 6.7 %collective-permute-start.4 = (bf16[8,8,1024]{2,1,0:T(8,128)(2,1)S(1)}, bf16[8,8,1024]{2,1,0:T(8,128)(2,1)S(1)}, u32[]{:S(2)}, u32[]{:S(2)}) collective-permute-start(bf16[8,8,1024]{2,1,0:T(8,128)(2,1)S(1)} %slice.49), channel_id=1, source_target_pairs={{0,16},{16,0},{1,17},{17,1},{2,18},{18,2},{3,19},{19,3},{4,20},{20... | collective-permute-start | bytes 393224 | tf_op jit(solution)/shard_map/ppermute | solution.py:62
  27.1 7.2 %copy-start = (bf16[8,256,1024]{2,1,0:T(8,128)(2,1)S(1)}, bf16[8,256,1024]{2,1,0:T(8,128)(2,1)}, u32[]{:S(2)}) copy-start(bf16[8,256,1024]{2,1,0:T(8,128)(2,1)} %bitcast_multiply_fusion.refs_6_.refs_4_) | copy-start | bytes 12582916
  34.3 17.4 %collective-permute-start.7 = (bf16[8,256,1024]{2,1,0:T(8,128)(2,1)S(1)}, bf16[8,256,1024]{2,1,0:T(8,128)(2,1)S(1)}, u32[]{:S(2)}, u32[]{:S(2)}) collective-permute-start(bf16[8,256,1024]{2,1,0:T(8,128)(2,1)S(1)} %copy-done), channel_id=1, source_target_pairs={{0,1},{1,0},{2,3},{3,2},{4,5},{5,4},{6,7},{7,6},{8,9},{9,8},{10,11... | collective-permute-start | bytes 12582920 | tf_op jit(solution)/shard_map/ppermute | solution.py:62
  35.2 7.9 %collective-permute-start.6 = (bf16[8,16,1024]{2,1,0:T(8,128)(2,1)S(1)}, bf16[8,16,1024]{2,1,0:T(8,128)(2,1)S(1)}, u32[]{:S(2)}, u32[]{:S(2)}) collective-permute-start(bf16[8,16,1024]{2,1,0:T(8,128)(2,1)S(1)} %get-tuple-element.18), channel_id=1, source_target_pairs={{0,2},{2,0},{1,3},{3,1},{4,6},{6,4},{5,7},{7,5},{8,10},{10,8},{9,1... | collective-permute-start | bytes 786440 | tf_op jit(solution)/shard_map/ppermute | solution.py:62
  36.4 14.2 %collective-permute-start.9 = (bf16[8,16,1024]{2,1,0:T(8,128)(2,1)S(1)}, bf16[8,16,1024]{2,1,0:T(8,128)(2,1)S(1)}, u32[]{:S(2)}, u32[]{:S(2)}) collective-permute-start(bf16[8,16,1024]{2,1,0:T(8,128)(2,1)S(1)} %get-tuple-element.18), channel_id=1, source_target_pairs={{0,4},{4,0},{8,12},{12,8},{1,5},{5,1},{9,13},{13,9},{2,6},{6,2},{1... | collective-permute-start | bytes 786440 | tf_op jit(solution)/shard_map/ppermute | solution.py:62
  39.0 11.7 %collective-permute-start.10 = (bf16[8,16,1024]{2,1,0:T(8,128)(2,1)S(1)}, bf16[8,16,1024]{2,1,0:T(8,128)(2,1)S(1)}, u32[]{:S(2)}, u32[]{:S(2)}) collective-permute-start(bf16[8,16,1024]{2,1,0:T(8,128)(2,1)S(1)} %get-tuple-element.20.refs_0_), channel_id=1, source_target_pairs={{0,2},{2,0},{1,3},{3,1},{4,6},{6,4},{5,7},{7,5},{8,10},{10,8},{9,1... | collective-permute-start | bytes 786440 | tf_op jit(solution)/shard_map/ppermute | solution.py:62
  39.2 16.7 %collective-permute-start.15 = (bf16[8,16,1024]{2,1,0:T(8,128)(2,1)S(1)}, bf16[8,16,1024]{2,1,0:T(8,128)(2,1)S(1)}, u32[]{:S(2)}, u32[]{:S(2)}) collective-permute-start(bf16[8,16,1024]{2,1,0:T(8,128)(2,1)S(1)} %get-tuple-element.26), channel_id=1, source_target_pairs={{0,8},{4,12},{8,0},{12,4},{1,9},{5,13},{9,1},{13,5},{2,10},{6,14},... | collective-permute-start | bytes 786440 | tf_op jit(solution)/shard_map/ppermute | solution.py:62
  43.1 18.5 %collective-permute-start.12 = (bf16[8,16,1024]{2,1,0:T(8,128)(2,1)S(1)}, bf16[8,16,1024]{2,1,0:T(8,128)(2,1)S(1)}, u32[]{:S(2)}, u32[]{:S(2)}) collective-permute-start(bf16[8,16,1024]{2,1,0:T(8,128)(2,1)S(1)} %collective-permute-done.6), channel_id=1, source_target_pairs={{0,4},{4,0},{8,12},{12,8},{1,5},{5,1},{9,13},{13,9},{2,6},{6,2},{1... | collective-permute-start | bytes 786440 | tf_op jit(solution)/shard_map/ppermute | solution.py:62
  50.6 10.7 %collective-permute-start.11 = (bf16[4,16,1024]{2,1,0:T(8,128)(2,1)S(1)}, bf16[4,16,1024]{2,1,0:T(8,128)(2,1)S(1)}, u32[]{:S(2)}, u32[]{:S(2)}) collective-permute-start(bf16[4,16,1024]{2,1,0:T(8,128)(2,1)S(1)} %get-tuple-element.24), channel_id=1, source_target_pairs={{0,12},{4,8},{8,4},{12,0},{1,13},{5,9},{9,5},{13,1},{2,14},{6,10},... | collective-permute-start | bytes 393224 | tf_op jit(solution)/shard_map/ppermute | solution.py:62
  51.7 2.0 %copy-start.3 = (bf16[8,256,1024]{2,1,0:T(8,128)(2,1)}, bf16[8,256,1024]{2,1,0:T(8,128)(2,1)S(1)}, u32[]{:S(2)}) copy-start(bf16[8,256,1024]{2,1,0:T(8,128)(2,1)S(1)} %collective-permute-done.7.refs_7_.refs_5_) | copy-start | bytes 12582916
  53.7 10.4 %collective-permute-start.8 = (bf16[4,16,1024]{2,1,0:T(8,128)(2,1)S(1)}, bf16[4,16,1024]{2,1,0:T(8,128)(2,1)S(1)}, u32[]{:S(2)}, u32[]{:S(2)}) collective-permute-start(bf16[4,16,1024]{2,1,0:T(8,128)(2,1)S(1)} %get-tuple-element.22), channel_id=1, source_target_pairs={{0,12},{4,8},{8,4},{12,0},{1,13},{5,9},{9,5},{13,1},{2,14},{6,10},... | collective-permute-start | bytes 393224 | tf_op jit(solution)/shard_map/ppermute | solution.py:62
  55.9 8.6 %collective-permute-start.16 = (bf16[8,16,1024]{2,1,0:T(8,128)(2,1)S(1)}, bf16[8,16,1024]{2,1,0:T(8,128)(2,1)S(1)}, u32[]{:S(2)}, u32[]{:S(2)}) collective-permute-start(bf16[8,16,1024]{2,1,0:T(8,128)(2,1)S(1)} %collective-permute-done.15.refs_4_), channel_id=1, source_target_pairs={{0,2},{2,0},{1,3},{3,1},{4,6},{6,4},{5,7},{7,5},{8,10},{10,8},{9,1... | collective-permute-start | bytes 786440 | tf_op jit(solution)/shard_map/ppermute | solution.py:62
  61.4 9.8 %collective-permute-start.14 = (bf16[4,16,1024]{2,1,0:T(8,128)(2,1)S(1)}, bf16[4,16,1024]{2,1,0:T(8,128)(2,1)S(1)}, u32[]{:S(2)}, u32[]{:S(2)}) collective-permute-start(bf16[4,16,1024]{2,1,0:T(8,128)(2,1)S(1)} %collective-permute-done.11.refs_1_), channel_id=1, source_target_pairs={{0,2},{2,0},{1,3},{3,1},{4,6},{6,4},{5,7},{7,5},{8,10},{10,8},{9,1... | collective-permute-start | bytes 393224 | tf_op jit(solution)/shard_map/ppermute | solution.py:62
  64.2 7.0 %collective-permute-start.13 = (bf16[4,16,1024]{2,1,0:T(8,128)(2,1)S(1)}, bf16[4,16,1024]{2,1,0:T(8,128)(2,1)S(1)}, u32[]{:S(2)}, u32[]{:S(2)}) collective-permute-start(bf16[4,16,1024]{2,1,0:T(8,128)(2,1)S(1)} %collective-permute-done.8.refs_0_), channel_id=1, source_target_pairs={{0,2},{2,0},{1,3},{3,1},{4,6},{6,4},{5,7},{7,5},{8,10},{10,8},{9,1... | collective-permute-start | bytes 393224 | tf_op jit(solution)/shard_map/ppermute | solution.py:62
  64.5 2.2 %copy-start.1 = (bf16[8,256,1024]{2,1,0:T(8,128)(2,1)S(1)}, bf16[8,256,1024]{2,1,0:T(8,128)(2,1)}, u32[]{:S(2)}) copy-start(bf16[8,256,1024]{2,1,0:T(8,128)(2,1)} %bitcast_multiply_fusion.refs_6_.refs_4_) | copy-start | bytes 12582916
  66.7 2.2 %copy-start.4 = (bf16[8,256,1024]{2,1,0:T(8,128)(2,1)S(1)}, bf16[8,256,1024]{2,1,0:T(8,128)(2,1)}, u32[]{:S(2)}) copy-start(bf16[8,256,1024]{2,1,0:T(8,128)(2,1)} %copy-done.3) | copy-start | bytes 12582916
  68.9 2.3 %copy-start.2 = (bf16[8,256,1024]{2,1,0:T(8,128)(2,1)S(1)}, bf16[8,256,1024]{2,1,0:T(8,128)(2,1)}, u32[]{:S(2)}) copy-start(bf16[8,256,1024]{2,1,0:T(8,128)(2,1)} %bitcast_multiply_fusion.refs_6_.refs_4_) | copy-start | bytes 12582916
  68.9 3.5 %copy-start.5 = (bf16[8,256,1024]{2,1,0:T(8,128)(2,1)S(1)}, bf16[8,256,1024]{2,1,0:T(8,128)(2,1)}, u32[]{:S(2)}) copy-start(bf16[8,256,1024]{2,1,0:T(8,128)(2,1)} %copy-done.3) | copy-start | bytes 12582916
  75.4 8.1 %collective-permute-start.20 = (bf16[64,256]{1,0:T(8,128)(2,1)S(1)}, bf16[64,256]{1,0:T(8,128)(2,1)S(1)}, u32[]{:S(2)}, u32[]{:S(2)}) collective-permute-start(bf16[64,256]{1,0:T(8,128)(2,1)S(1)} %get-tuple-element.38), channel_id=1, source_target_pairs={{0,9},{1,13},{4,8},{5,12},{8,1},{9,5},{12,0},{13,4},{2,11},{3,15},... | collective-permute-start | bytes 98312 | tf_op jit(solution)/shard_map/ppermute | solution.py:258
  76.5 7.0 %collective-permute-start.19 = (bf16[64,256]{1,0:T(8,128)(2,1)S(1)}, bf16[64,256]{1,0:T(8,128)(2,1)S(1)}, u32[]{:S(2)}, u32[]{:S(2)}) collective-permute-start(bf16[64,256]{1,0:T(8,128)(2,1)S(1)} %get-tuple-element.39), channel_id=1, source_target_pairs={{0,8},{1,12},{4,9},{5,13},{8,0},{9,4},{12,1},{13,5},{2,10},{3,14},... | collective-permute-start | bytes 98312 | tf_op jit(solution)/shard_map/ppermute | solution.py:258
  80.4 3.1 %collective-permute-start.18 = (bf16[64,256]{1,0:T(8,128)(2,1)S(1)}, bf16[64,256]{1,0:T(8,128)(2,1)S(1)}, u32[]{:S(2)}, u32[]{:S(2)}) collective-permute-start(bf16[64,256]{1,0:T(8,128)(2,1)S(1)} %get-tuple-element.40), channel_id=1, source_target_pairs={{0,1},{1,5},{4,0},{5,4},{8,9},{9,13},{12,8},{13,12},{2,3},{3,7},{6... | collective-permute-start | bytes 98312 | tf_op jit(solution)/shard_map/ppermute | solution.py:258
  80.8 5.2 %collective-permute-start.17 = (bf16[64,256]{1,0:T(8,128)(2,1)S(1)}, bf16[64,256]{1,0:T(8,128)(2,1)S(1)}, u32[]{:S(2)}, u32[]{:S(2)}) collective-permute-start(bf16[64,256]{1,0:T(8,128)(2,1)S(1)} %get-tuple-element.37), channel_id=1, source_target_pairs={{0,0},{1,4},{4,1},{5,5},{8,8},{9,12},{12,9},{13,13},{2,2},{3,6},{6... | collective-permute-start | bytes 98312 | tf_op jit(solution)/shard_map/ppermute | solution.py:258

commit v5 on v4

--- a/solution.py
+++ b/solution.py
@@ -173,47 +173,62 @@
     )(part.reshape(1), *pieces, occ, virt)
 
 
-def product(right, masked_ref):
-    total = None
-    for m in range(masked_ref.shape[0]):
-        term = lax.dot_general(
-            masked_ref[m], right[m], (((1,), (1,)), ((), ())), preferred_element_type=jnp.float32
-        )
-        total = term if total is None else total + term
-    return total
+def add_product(right, rows_ref, keep_ref, core, into_ref):
+    for block in range(rows_ref.shape[1] // RB):
+        at = slice(block * RB, (block + 1) * RB)
+        total = into_ref[core, at, :]
+        for m in range(rows_ref.shape[0]):
+            term = lax.dot_general(
+                rows_ref[m, at, :],
+                right[m],
+                (((1,), (1,)), ((), ())),
+                preferred_element_type=jnp.float32,
+            )
+            total = total + term * keep_ref[core, block, m]
+        into_ref[core, at, :] = total
 
 
 WHOLE = pl.BlockSpec(memory_space=pltpu.VMEM)
 SMALL = pltpu.CompilerParams(vmem_limit_bytes=16 * 1024 * 1024)
 
 
-def early_kernel(count, *refs):
-    parts, masked_refs, out_ref = refs[:count], refs[count : count + 2], refs[count + 2]
+def early_kernel(count, keep_ref, *refs):
+    parts, sources, out_ref = refs[:count], refs[count : count + 2], refs[count + 2]
+    kept, sem = refs[count + 3 : count + 5], refs[count + 5]
+    copies = [pltpu.make_async_copy(sources[c], kept[c], sem.at[c]) for c in range(2)]
+    for copy in copies:
+        copy.start()
     blocks, own, cols = parts[0].shape
     nothing = jnp.zeros((LANES - count * own, cols), jnp.bfloat16)
     right = []
     for m in range(blocks):
         right.append(jnp.concatenate([part[m] for part in parts] + [nothing], axis=0))
+    out_ref[...] = jnp.zeros_like(out_ref)
     for core in range(2):
-        out_ref[core] = product(right, masked_refs[core])
-
-
-def early_terms(parts, masked):
-    rows_dev = masked[0].shape[1]
+        copies[core].wait()
+        add_product(right, kept[core], keep_ref, core, out_ref)
+
+
+def early_terms(keep, parts, rows):
+    rows_dev = rows[0].shape[1]
     return pl.pallas_call(
         functools.partial(early_kernel, len(parts)),
-        out_shape=jax.ShapeDtypeStruct((2, rows_dev, LANES), jnp.float32),
-        in_specs=[WHOLE] * (len(parts) + 2),
-        out_specs=WHOLE,
+        out_shape=[jax.ShapeDtypeStruct((2, rows_dev, LANES), jnp.float32)]
+        + [pltpu.VMEM(value.shape, value.dtype) for value in rows],
+        in_specs=[pl.BlockSpec(memory_space=pltpu.SMEM)]
+        + [WHOLE] * len(parts)
+        + [pl.BlockSpec(memory_space=pl.ANY)] * 2,
+        out_specs=[WHOLE] * 3,
+        scratch_shapes=[pltpu.SemaphoreType.DMA((2,))],
         compiler_params=SMALL,
         cost_estimate=TINY,
         name="early_terms",
-    )(*parts, *masked)
-
-
-def final_kernel(place_ref, *refs):
+    )(keep, *parts, *rows)
+
+
+def final_kernel(place_ref, keep_ref, *refs):
     near, far = refs[:2], refs[2:4]
-    own_ref, other_ref, early_ref, out_ref, hold_ref = refs[4:]
+    own_ref, other_ref, early_ref, out_ref, sum_ref, hold_ref = refs[4:]
     count = out_ref.shape[0]
     part, own, cols = near[0].shape
     nothing = jnp.zeros((LANES - 2 * own, cols), jnp.bfloat16)
@@ -221,8 +236,10 @@
     for m in range(2 * part):
         rows = [nothing, near[m // part][m % part], far[m // part][m % part]]
         right.append(jnp.concatenate(rows, axis=0))
-    for core, masked_ref in enumerate((own_ref, other_ref)):
-        hold_ref[core] = (early_ref[core] + product(right, masked_ref)).T
+    sum_ref[...] = early_ref[...]
+    for core, rows_ref in enumerate((own_ref, other_ref)):
+        add_product(right, rows_ref, keep_ref, core, sum_ref)
+        hold_ref[core] = sum_ref[core].T
     for route in range(count):
         side, core = place_ref[0] ^ (route // 2), place_ref[1] ^ (route % 2)
         for p in range(count):
@@ -232,20 +249,23 @@
             ].astype(jnp.bfloat16)
 
 
-def final_terms(place, near, far, masked, early):
+def final_terms(place, keep, near, far, rows, early):
     own = near[0].shape[1]
-    rows_dev = masked[0].shape[1]
+    rows_dev = rows[0].shape[1]
     count = LANES // (2 * own)
     return pl.pallas_call(
         final_kernel,
         out_shape=jax.ShapeDtypeStruct((count, count * own, rows_dev), jnp.bfloat16),
-        in_specs=[pl.BlockSpec(memory_space=pltpu.SMEM)] + [WHOLE] * 7,
+        in_specs=[pl.BlockSpec(memory_space=pltpu.SMEM)] * 2 + [WHOLE] * 7,
         out_specs=WHOLE,
-        scratch_shapes=[pltpu.VMEM((2, LANES, rows_dev), jnp.float32)],
+        scratch_shapes=[
+            pltpu.VMEM((2, rows_dev, LANES), jnp.float32),
+            pltpu.VMEM((2, LANES, rows_dev), jnp.float32),
+        ],
         compiler_params=SMALL,
         cost_estimate=TINY,
         name="final_terms",
-    )(place, *near, *far, *masked, early)
+    )(place, keep, *near, *far, *rows, early)
 
 
 def routed(value, route):
@@ -262,7 +282,7 @@
     return lax.optimization_barrier((value,) + others)[0]
 
 
-def swapped_plan(tensor, mask_rows, occ_green, virt_green, green_mask):
+def swapped_plan(tensor, mask_rows, other_mask_rows, occ_green, virt_green, green_mask):
     planes = lax.axis_size("ao")
     steps = range(1, planes)
     z = lax.axis_index("ao")
@@ -279,10 +299,14 @@
 
     mine = jnp.where(core == 0, occ_green, virt_green).reshape(-1, blocks, cols)
     whole = lax.dynamic_slice_in_dim(tensor, (z ^ 1) * own, own, 0)
-    first = swap(jnp.concatenate([whole, mine]), "ao", 1)
-    direct = [swap(jnp.concatenate([rows_of(z ^ k, side), mine]), "ao", k) for k in (2, 3)]
-    hops = {3: swap(direct[1][:half], "tpoint", 1)}
-    hops[2] = swap(direct[0][:half], "tpoint", 1)
+    leaving = [jnp.concatenate([rows_of(z ^ k, side), mine]) for k in (2, 3)]
+    first = swap(after(jnp.concatenate([whole, mine]), *leaving), "ao", 1)
+    direct = [swap(leaving[0], "ao", 2)]
+    direct.append(swap(after(leaving[1], direct[0]), "ao", 3))
+    rows = jnp.swapaxes(after(tensor, direct[0]), 0, 1)
+    direct[1], rows = lax.optimization_barrier((direct[1], rows))
+    hops = {2: swap(direct[0][:half], "tpoint", 1)}
+    hops[3] = swap(after(direct[1][:half], hops[2]), "tpoint", 1)
     pieces = [lax.dynamic_slice_in_dim(tensor, z * own, own, 0), first]
     for k in (2, 3):
         pieces += [direct[k - 2], hops[k]]
@@ -292,8 +316,6 @@
     shape = (blocks,) + occ_green.shape[1:]
     mine_all = stacked[order].reshape(shape)
     other_all = other[order].reshape(shape)
-    row_mask = jnp.repeat(mask_rows, RB, axis=0).astype(jnp.bfloat16)
-    masked = jnp.swapaxes(tensor, 0, 1) * row_mask.T[:, :, None]
     occ_mask, virt_mask = pair_masks(green_mask, mask_rows[0])
     occ = jnp.where(core == 0, mine_all, other_all) * occ_mask[:, :, None, None]
     virt = jnp.where(core == 0, other_all, mine_all) * virt_mask[:, :, None, None]
@@ -313,22 +335,22 @@
         ],
         axis=2,
     )
-    pieces[0], masked = lax.optimization_barrier((pieces[0], masked))
     sums = contract(side, pieces, occ, virt)
-    masked = (masked, swap(after(masked, sums[0]), "rep", 1))
+    rows = (rows, swap(after(rows, sums[0]), "rep", 1))
     near1, near2 = swap(sums[1], "ao", 1), swap(sums[2], "ao", 2)
     far0, across = swap(sums[0], "aux", 1), swap(sums[1], "aux", 1)
     far1 = swap(across, "ao", 1)
     near3 = [
-        swap(after(sums[3], across, masked[1]), "ao", 3),
+        swap(after(sums[3], across), "ao", 3),
         swap(after(sums[4], near1, far0), "ao", 3),
     ]
     far2 = swap(near2, "aux", 1)
     far3 = [swap(after(near3[0], far1), "aux", 1), swap(near3[1], "aux", 1)]
     parts = [sums[0], far0, near1, far1, near2, far2]
-    early = early_terms(parts, masked)
+    keep = jnp.stack([mask_rows, other_mask_rows]).astype(jnp.float32)
+    early, *rows = early_terms(keep, parts, rows)
     place = jnp.stack([(z // 2) ^ aux, (z % 2) ^ core]).astype(jnp.int32)
-    leaving = final_terms(place, near3, far3, masked, early)
+    leaving = final_terms(place, keep, near3, far3, rows, early)
     total = None
     for route in range(planes):
         term = routed(leaving[route], route).astype(jnp.float32)
@@ -351,7 +373,8 @@
     simple = sizes == (2, 4, 2, 2) and cols * planes == AOB * AOB and SL // planes == 16
     simple = simple and blocks * 16 == LANES and rows_dev % RB == 0 and occ_green.shape[1] == 3
     if simple:
-        return swapped_plan(tensor, mask_of(shard), occ_green, virt_green, green_mask)
+        masks = mask_of(shard), mask_of(shard ^ 1)
+        return swapped_plan(tensor, *masks, occ_green, virt_green, green_mask)
     return gathered_plan(tensor, mask_of(shard), occ_green, virt_green, green_mask)
 
 

time: 87.5 us -> 83.7 us (0.957)
  other arithmetic: 12.1 us -> 1.37 us
  waiting for transfers between devices: 23 us -> 26.6 us
  Pallas kernels: 8.72 us -> 11.8 us
  starting transfers between devices: 28.1 us -> 29 us
    mul x1 -> x0, other arithmetic: 10.1 us -> none  [swapped_plan(): masked = jnp.swapaxes(tensor, 0, 1) * row_mask.T[:, :, None]]
    unnamed x15 -> x3, local copies, waits for them, and re-layouts: 7.63 us -> 0.08 us
    optimization_barrier x0 -> x1, local copies, waits for them, and re-layouts: none -> 6.47 us  [after(): return lax.optimization_barrier((value,) + others)[0]]
    pallas_call x1, Pallas kernels: 2.3 us -> 5.3 us  [early_terms(): pl.pallas_call(functools.partial(early_kernel, len(parts)), out_shape=[ja...]
    ppermute x17, waiting for transfers between devices: 20.5 us -> 23.3 us  [swap(): return lax.ppermute(value, axis, [(i, i ^ step) for i in range(count)])]
  transfers between devices with their start and end apart: 21 -> 21, of which waited for: 8 -> 9; matrix products, arithmetic and copies ran while one was open for 18% -> 15% of each run, Pallas kernels for 3% -> 6%
where the time goes in v5:
time: 83.7 us; the launch traced here: 83.5 us
  starting transfers between devices  29 us (35%)
  waiting for transfers between devices  26.6 us (32%)
  local copies, waits for them, and re-layouts  13.8 us (16%)
  Pallas kernels  11.8 us (14%)
  other arithmetic  1.37 us (2%)
    ppermute x17, waiting for transfers between devices, swap(): return lax.ppermute(value, axis, [(i, i ^ step) for i in range(count)])  23.3 us
    ppermute x17, starting transfers between devices, swap(): return lax.ppermute(value, axis, [(i, i ^ step) for i in range(count)])  20.5 us
    ppermute x4, starting transfers between devices, routed(): return lax.ppermute(value, ('ao', 'rep'), pairs)  8.44 us
    optimization_barrier x1, local copies, waits for them, and re-layouts, after(): return lax.optimization_barrier((value,) + others)[0]  6.47 us
    pallas_call x1, Pallas kernels, early_terms(): pl.pallas_call(functools.partial(early_kernel, len(parts)), out_shape=[ja...  5.3 us
    pallas_call x1, Pallas kernels, contract(): pl.pallas_call(functools.partial(contract_kernel, planes), out_shape=[jax...  3.47 us
    ppermute x4, waiting for transfers between devices, routed(): return lax.ppermute(value, ('ao', 'rep'), pairs)  3.27 us
    pallas_call x1, Pallas kernels, final_terms(): pl.pallas_call(final_kernel, out_shape=jax.ShapeDtypeStruct((count, count...  2.99 us
  transfers between devices with their start and end apart: 21, of which 9 were waited for; matrix products, arithmetic and copies ran while one was open for 15% of the time, Pallas kernels for 6%

profile of v5, /device:TPU:1, one launch (start us, length us, event | category | flops | bytes accessed | tf_op | source)
XLA Modules:
  0.0 83.5 jit_solution(9803382078828368265)
XLA Ops:
  0.0 0.9 %broadcast_select_fusion.2 = bf16[2,3,64,64]{3,2,1,0:T(8,128)(2,1)S(1)} fusion(bf16[2,3,64,64]{3,2,1,0:T(8,128)(2,1)} %param.7, bf16[2,3,64,64]{3,2,1,0:T(8,128)(2,1)} %param.8, pred[]{:T(512)S(6)} %eq.12), kind=kLoop, calls=%fused_computation.19 | loop fusion | flops 24576 | bytes 147457 | tf_op jit(solution)/shard_map/jit(_where)/select_n | solution.py:300
  1.1 1.0 %constant_dynamic-slice_fusion = (bf16[8,8,1024]{2,1,0:T(8,128)(2,1)S(1)}, bf16[8,8,1024]{2,1,0:T(8,128)(2,1)S(1)}) fusion(bf16[256,8,1024]{2,1,0:T(8,128)(2,1)} %param.5, s32[]{:T(128)S(6)} %select_n.134, s32[]{:T(128)S(6)} %select_n.133), kind=kLoop, calls=%fused_computation.51 | loop fusion | bytes 524296 | tf_op jit(solution)/shard_map/dynamic_slice | solution.py:298
  2.1 3.2 %collective-permute-start.1 = (bf16[11,8,1024]{2,1,0:T(8,128)(2,1)S(1)}, bf16[11,8,1024]{2,1,0:T(8,128)(2,1)S(1)}, u32[]{:S(2)}, u32[]{:S(2)}) collective-permute-start(bf16[11,8,1024]{2,1,0:T(8,128)(2,1)S(1)} %get-tuple-element.54), channel_id=1, source_target_pairs={{0,8},{4,12},{8,0},{12,4},{1,9},{5,13},{9,1},{13,5},{2,10},{6,14},... | collective-permute-start | bytes 540680 | tf_op jit(solution)/shard_map/ppermute | solution.py:62
  5.3 1.1 %constant_dynamic-slice_fusion.2 = (bf16[16,8,1024]{2,1,0:T(8,128)(2,1)S(1)}, bf16[16,8,1024]{2,1,0:T(8,128)(2,1)S(1)}) fusion(bf16[256,8,1024]{2,1,0:T(8,128)(2,1)} %param.5, s32[]{:T(128)S(6)} %select_n.130, s32[]{:T(128)S(6)} %select_n.129), kind=kLoop, calls=%fused_computation.53 | loop fusion | bytes 1048584 | tf_op jit(solution)/shard_map/dynamic_slice | solution.py:301
  6.4 1.4 %collective-permute-start = (bf16[19,8,1024]{2,1,0:T(8,128)(2,1)S(1)}, bf16[19,8,1024]{2,1,0:T(8,128)(2,1)S(1)}, u32[]{:S(2)}, u32[]{:S(2)}) collective-permute-start(bf16[19,8,1024]{2,1,0:T(8,128)(2,1)S(1)} %pad_maximum_fusion.1), channel_id=1, source_target_pairs={{0,4},{4,0},{8,12},{12,8},{1,5},{5,1},{9,13},{13,9},{2,6},{6,2},{1... | collective-permute-start | bytes 933896 | tf_op jit(solution)/shard_map/ppermute | solution.py:62
  7.8 0.8 constant_dynamic-slice_fusion.5
  8.6 0.7 gather_fusion.2
  9.5 0.1 stack_reshape.3
  9.7 3.8 %collective-permute-done.1.refs_2_ = bf16[11,8,1024]{2,1,0:T(8,128)(2,1)S(1)} collective-permute-done((bf16[11,8,1024]{2,1,0:T(8,128)(2,1)S(1)}, bf16[11,8,1024]{2,1,0:T(8,128)(2,1)S(1)}, u32[]{:S(2)}, u32[]{:S(2)}) %collective-permute-start.1) | collective-permute-done | bytes 180256 | tf_op jit(solution)/shard_map/ppermute | solution.py:62
  13.5 1.1 %collective-permute-start.2 = (bf16[8,8,1024]{2,1,0:T(8,128)(2,1)S(1)}, bf16[8,8,1024]{2,1,0:T(8,128)(2,1)S(1)}, u32[]{:S(2)}, u32[]{:S(2)}) collective-permute-start(bf16[8,8,1024]{2,1,0:T(8,128)(2,1)S(1)} %slice.48), channel_id=1, source_target_pairs={{0,16},{16,0},{1,17},{17,1},{2,18},{18,2},{3,19},{19,3},{4,20},{20... | collective-permute-start | bytes 393224 | tf_op jit(solution)/shard_map/ppermute | solution.py:62
  14.5 4.3 %collective-permute-start.3 = (bf16[11,8,1024]{2,1,0:T(8,128)(2,1)S(1)}, bf16[11,8,1024]{2,1,0:T(8,128)(2,1)S(1)}, u32[]{:S(2)}, u32[]{:S(2)}) collective-permute-start(bf16[11,8,1024]{2,1,0:T(8,128)(2,1)S(1)} %get-tuple-element.24), channel_id=1, source_target_pairs={{0,12},{4,8},{8,4},{12,0},{1,13},{5,9},{9,5},{13,1},{2,14},{6,10},... | collective-permute-start | bytes 540680 | tf_op jit(solution)/shard_map/ppermute | solution.py:62
  18.8 6.5 %copy.16 = bf16[256,8,1024]{2,0,1:T(8,128)(2,1)} copy(bf16[256,8,1024]{2,1,0:T(8,128)(2,1)} %param.5) | data formatting | bytes 8388608 | tf_op jit(solution)/shard_map/optimization_barrier | solution.py:282
  25.4 1.2 %collective-permute-start.5 = (bf16[4,3,8,1024]{3,2,1,0:T(8,128)(2,1)S(1)}, bf16[4,3,8,1024]{3,2,1,0:T(8,128)(2,1)S(1)}, u32[]{:S(2)}, u32[]{:S(2)}) collective-permute-start(bf16[4,3,8,1024]{3,2,1,0:T(8,128)(2,1)S(1)} %pad_maximum_fusion.4), channel_id=1, source_target_pairs={{0,1},{1,0},{2,3},{3,2},{4,5},{5,4},{6,7},{7,6},{8,9},{9,8},{10,11... | collective-permute-start | bytes 589832 | tf_op jit(solution)/shard_map/ppermute | solution.py:62
  26.6 0.3 collective-permute-start.4
  26.9 0.6 gather_fusion
  27.4 0.2 collective-permute-done.5
  27.6 0.6 gather_fusion.1
  28.2 0.3 select_n.142
  28.5 0.7 fusion
  29.2 0.2 copy.13.refs_6_
  29.4 0.3 select_n.145
  29.8 0.2 pad_bitcast_fusion.1
  30.1 1.6 %collective-permute-done.4.refs_5_ = bf16[8,8,1024]{2,1,0:T(8,128)(2,1)S(1)} collective-permute-done((bf16[8,8,1024]{2,1,0:T(8,128)(2,1)S(1)}, bf16[8,8,1024]{2,1,0:T(8,128)(2,1)S(1)}, u32[]{:S(2)}, u32[]{:S(2)}) %collective-permute-start.4) | collective-permute-done | bytes 131104 | tf_op jit(solution)/shard_map/ppermute | solution.py:62
  31.8 3.5 %contract_slab.1 = (bf16[8,16,1024]{2,1,0:T(8,128)(2,1)S(1)}, bf16[8,16,1024]{2,1,0:T(8,128)(2,1)S(1)}, bf16[8,16,1024]{2,1,0:T(8,128)(2,1)S(1)}, bf16[4,16,1024...) custom-call(s32[1]{0:T(128)} %bitcast.4.part_ref, bf16[16,8,1024]{2,1,0:T(8,128)(2,1)S(1)} %get-tuple-element.44.refs_0_, ...), custom_call_target="tpu_custom_call" | custom-call | flops 1 | bytes 1 | tf_op jit(solution)/shard_map/contract_slab/pallas_call | solution.py:157
  35.2 0.9 %collective-permute-start.16 = (bf16[8,256,1024]{2,1,0:T(8,128)(2,1)}, bf16[8,256,1024]{2,1,0:T(8,128)(2,1)}, u32[]{:S(2)}, u32[]{:S(2)}) collective-permute-start(bf16[8,256,1024]{2,1,0:T(8,128)(2,1)} %bitcast.60.refs_6_), channel_id=1, source_target_pairs={{0,1},{1,0},{2,3},{3,2},{4,5},{5,4},{6,7},{7,6},{8,9},{9,8},{10,11... | collective-permute-start | bytes 12582920 | tf_op jit(solution)/shard_map/ppermute | solution.py:62
  36.1 1.2 %collective-permute-start.6 = (bf16[8,16,1024]{2,1,0:T(8,128)(2,1)S(1)}, bf16[8,16,1024]{2,1,0:T(8,128)(2,1)S(1)}, u32[]{:S(2)}, u32[]{:S(2)}) collective-permute-start(bf16[8,16,1024]{2,1,0:T(8,128)(2,1)S(1)} %get-tuple-element.29), channel_id=1, source_target_pairs={{0,2},{2,0},{1,3},{3,1},{4,6},{6,4},{5,7},{7,5},{8,10},{10,8},{9,1... | collective-permute-start | bytes 786440 | tf_op jit(solution)/shard_map/ppermute | solution.py:62
  37.3 0.4 collective-permute-start.8
  37.7 0.3 collective-permute-start.9
  37.9 1.1 %collective-permute-start.14 = (bf16[8,16,1024]{2,1,0:T(8,128)(2,1)S(1)}, bf16[8,16,1024]{2,1,0:T(8,128)(2,1)S(1)}, u32[]{:S(2)}, u32[]{:S(2)}) collective-permute-start(bf16[8,16,1024]{2,1,0:T(8,128)(2,1)S(1)} %get-tuple-element.35), channel_id=1, source_target_pairs={{0,8},{4,12},{8,0},{12,4},{1,9},{5,13},{9,1},{13,5},{2,10},{6,14},... | collective-permute-start | bytes 786440 | tf_op jit(solution)/shard_map/ppermute | solution.py:62
  39.0 5.0 %collective-permute-done.6 = bf16[8,16,1024]{2,1,0:T(8,128)(2,1)S(1)} collective-permute-done((bf16[8,16,1024]{2,1,0:T(8,128)(2,1)S(1)}, bf16[8,16,1024]{2,1,0:T(8,128)(2,1)S(1)}, u32[]{:S(2)}, u32[]{:S(2)}) %collective-permute-start.6) | collective-permute-done | bytes 262176 | tf_op jit(solution)/shard_map/ppermute | solution.py:62
  44.0 0.4 collective-permute-start.11
  44.3 4.3 %collective-permute-done.8.refs_2_ = bf16[8,16,1024]{2,1,0:T(8,128)(2,1)S(1)} collective-permute-done((bf16[8,16,1024]{2,1,0:T(8,128)(2,1)S(1)}, bf16[8,16,1024]{2,1,0:T(8,128)(2,1)S(1)}, u32[]{:S(2)}, u32[]{:S(2)}) %collective-permute-start.8) | collective-permute-done | bytes 262176 | tf_op jit(solution)/shard_map/ppermute | solution.py:62
  48.7 0.9 %collective-permute-done.9.refs_1_ = bf16[8,16,1024]{2,1,0:T(8,128)(2,1)S(1)} collective-permute-done((bf16[8,16,1024]{2,1,0:T(8,128)(2,1)S(1)}, bf16[8,16,1024]{2,1,0:T(8,128)(2,1)S(1)}, u32[]{:S(2)}, u32[]{:S(2)}) %collective-permute-start.9) | collective-permute-done | bytes 262176 | tf_op jit(solution)/shard_map/ppermute | solution.py:62
  49.6 1.9 %collective-permute-start.10 = (bf16[4,16,1024]{2,1,0:T(8,128)(2,1)S(1)}, bf16[4,16,1024]{2,1,0:T(8,128)(2,1)S(1)}, u32[]{:S(2)}, u32[]{:S(2)}) collective-permute-start(bf16[4,16,1024]{2,1,0:T(8,128)(2,1)S(1)} %get-tuple-element.33), channel_id=1, source_target_pairs={{0,12},{4,8},{8,4},{12,0},{1,13},{5,9},{9,5},{13,1},{2,14},{6,10},... | collective-permute-start | bytes 393224 | tf_op jit(solution)/shard_map/ppermute | solution.py:62
  51.5 1.4 %collective-permute-start.7 = (bf16[4,16,1024]{2,1,0:T(8,128)(2,1)S(1)}, bf16[4,16,1024]{2,1,0:T(8,128)(2,1)S(1)}, u32[]{:S(2)}, u32[]{:S(2)}) collective-permute-start(bf16[4,16,1024]{2,1,0:T(8,128)(2,1)S(1)} %get-tuple-element.30), channel_id=1, source_target_pairs={{0,12},{4,8},{8,4},{12,0},{1,13},{5,9},{9,5},{13,1},{2,14},{6,10},... | collective-permute-start | bytes 393224 | tf_op jit(solution)/shard_map/ppermute | solution.py:62
  52.9 1.2 %collective-permute-start.15 = (bf16[8,16,1024]{2,1,0:T(8,128)(2,1)S(1)}, bf16[8,16,1024]{2,1,0:T(8,128)(2,1)S(1)}, u32[]{:S(2)}, u32[]{:S(2)}) collective-permute-start(bf16[8,16,1024]{2,1,0:T(8,128)(2,1)S(1)} %collective-permute-done.14.refs_4_), channel_id=1, source_target_pairs={{0,2},{2,0},{1,3},{3,1},{4,6},{6,4},{5,7},{7,5},{8,10},{10,8},{9,1... | collective-permute-start | bytes 786440 | tf_op jit(solution)/shard_map/ppermute | solution.py:62
  54.1 4.9 %collective-permute-done.10.refs_1_ = bf16[4,16,1024]{2,1,0:T(8,128)(2,1)S(1)} collective-permute-done((bf16[4,16,1024]{2,1,0:T(8,128)(2,1)S(1)}, bf16[4,16,1024]{2,1,0:T(8,128)(2,1)S(1)}, u32[]{:S(2)}, u32[]{:S(2)}) %collective-permute-start.10) | collective-permute-done | bytes 131104 | tf_op jit(solution)/shard_map/ppermute | solution.py:62
  59.0 0.3 collective-permute-start.13
  59.3 2.5 %collective-permute-done.7.refs_0_ = bf16[4,16,1024]{2,1,0:T(8,128)(2,1)S(1)} collective-permute-done((bf16[4,16,1024]{2,1,0:T(8,128)(2,1)S(1)}, bf16[4,16,1024]{2,1,0:T(8,128)(2,1)S(1)}, u32[]{:S(2)}, u32[]{:S(2)}) %collective-permute-start.7) | collective-permute-done | bytes 131104 | tf_op jit(solution)/shard_map/ppermute | solution.py:62
  61.8 0.3 collective-permute-start.12
  62.2 5.3 %early_terms.1 = (f32[2,256,128]{2,1,0:T(8,128)S(1)}, bf16[8,256,1024]{2,1,0:T(8,128)(2,1)S(1)}, bf16[8,256,1024]{2,1,0:T(8,128)(2,1)S(1)}) custom-call(f32[2,2,8]{2,1,0:T(2,128)S(1)} %add_convert_fusion.keep_ref, bf16[8,16,1024]{2,1,0:T(8,128)(2,1)S(1)} %get-tuple-element.32.refs_0_, bf16[8,16,1024]{2,1,0:T(8,128)(2,1)S(1)} %collective-permute-done.9.refs_1_, ...), custom_call_target="tpu_custom_call" | custom-call | flops 1 | bytes 1 | tf_op jit(solution)/shard_map/early_terms/pallas_call | solution.py:214
  67.5 3.0 %final_terms.1 = bf16[4,64,256]{2,1,0:T(8,128)(2,1)S(1)} custom-call(s32[2]{0:T(128)S(1)} %pad_add_fusion.place_ref, f32[2,2,8]{2,1,0:T(2,128)S(1)} %add_convert_fusion.keep_ref, bf16[4,16,1024]{2,1,0:T(8,128)(2,1)S(1)} %collective-permute-done.7.refs_0_, bf16[4,16,1024]{2,1,0:T(8,128)(2,1)S(1)} %collective-permute-done.10.refs_1_, ...), custom_call_target="tpu_custom_call" | custom-call | flops 1 | bytes 1 | tf_op jit(solution)/shard_map/final_terms/pallas_call | solution.py:256
  70.5 2.2 %collective-permute-start.20 = (bf16[64,256]{1,0:T(8,128)(2,1)S(1)}, bf16[64,256]{1,0:T(8,128)(2,1)S(1)}, u32[]{:S(2)}, u32[]{:S(2)}) collective-permute-start(bf16[64,256]{1,0:T(8,128)(2,1)S(1)} %get-tuple-element.50), channel_id=1, source_target_pairs={{0,9},{1,13},{4,8},{5,12},{8,1},{9,5},{12,0},{13,4},{2,11},{3,15},... | collective-permute-start | bytes 98312 | tf_op jit(solution)/shard_map/ppermute | solution.py:278
  72.7 2.6 %collective-permute-start.19 = (bf16[64,256]{1,0:T(8,128)(2,1)S(1)}, bf16[64,256]{1,0:T(8,128)(2,1)S(1)}, u32[]{:S(2)}, u32[]{:S(2)}) collective-permute-start(bf16[64,256]{1,0:T(8,128)(2,1)S(1)} %get-tuple-element.51), channel_id=1, source_target_pairs={{0,8},{1,12},{4,9},{5,13},{8,0},{9,4},{12,1},{13,5},{2,10},{3,14},... | collective-permute-start | bytes 98312 | tf_op jit(solution)/shard_map/ppermute | solution.py:278
  75.4 1.7 %collective-permute-start.18 = (bf16[64,256]{1,0:T(8,128)(2,1)S(1)}, bf16[64,256]{1,0:T(8,128)(2,1)S(1)}, u32[]{:S(2)}, u32[]{:S(2)}) collective-permute-start(bf16[64,256]{1,0:T(8,128)(2,1)S(1)} %get-tuple-element.52), channel_id=1, source_target_pairs={{0,1},{1,5},{4,0},{5,4},{8,9},{9,13},{12,8},{13,12},{2,3},{3,7},{6... | collective-permute-start | bytes 98312 | tf_op jit(solution)/shard_map/ppermute | solution.py:278
  77.0 1.9 %collective-permute-start.17 = (bf16[64,256]{1,0:T(8,128)(2,1)S(1)}, bf16[64,256]{1,0:T(8,128)(2,1)S(1)}, u32[]{:S(2)}, u32[]{:S(2)}) collective-permute-start(bf16[64,256]{1,0:T(8,128)(2,1)S(1)} %get-tuple-element.49), channel_id=1, source_target_pairs={{0,0},{1,4},{4,1},{5,5},{8,8},{9,12},{12,9},{13,13},{2,2},{3,6},{6... | collective-permute-start | bytes 98312 | tf_op jit(solution)/shard_map/ppermute | solution.py:278
  79.0 3.3 %collective-permute-done.17 = bf16[64,256]{1,0:T(8,128)(2,1)S(1)} collective-permute-done((bf16[64,256]{1,0:T(8,128)(2,1)S(1)}, bf16[64,256]{1,0:T(8,128)(2,1)S(1)}, u32[]{:S(2)}, u32[]{:S(2)}) %collective-permute-start.17) | collective-permute-done | bytes 32800 | tf_op jit(solution)/shard_map/ppermute | solution.py:278
  82.3 1.2 %gather_fusion.3 = f32[8,8,256]{2,1,0:T(8,128)} fusion(f32[8,8,256]{2,1,0:T(8,128)S(1)} %add_bitcast_fusion, s32[1024]{0:T(1024)S(1)} %pad_clamp_fusion), kind=kCustom, calls=%fused_computation.3 | custom fusion | bytes 131104 | tf_op jit(solution)/shard_map/gather | solution.py:360
  (42 shorter events, 0.9 us)
Async XLA Ops:
  0.0 9.4 %copy-start = (s32[8,3]{0,1:T(4,128)S(1)}, s32[8,3]{0,1:T(4,128)}, u32[]{:S(2)}) copy-start(s32[8,3]{0,1:T(4,128)} %param.9) | copy-start | bytes 292
  2.1 11.3 %collective-permute-start.1 = (bf16[11,8,1024]{2,1,0:T(8,128)(2,1)S(1)}, bf16[11,8,1024]{2,1,0:T(8,128)(2,1)S(1)}, u32[]{:S(2)}, u32[]{:S(2)}) collective-permute-start(bf16[11,8,1024]{2,1,0:T(8,128)(2,1)S(1)} %get-tuple-element.54), channel_id=1, source_target_pairs={{0,8},{4,12},{8,0},{12,4},{1,9},{5,13},{9,1},{13,5},{2,10},{6,14},... | collective-permute-start | bytes 540680 | tf_op jit(solution)/shard_map/ppermute | solution.py:62
  6.4 18.9 %collective-permute-start = (bf16[19,8,1024]{2,1,0:T(8,128)(2,1)S(1)}, bf16[19,8,1024]{2,1,0:T(8,128)(2,1)S(1)}, u32[]{:S(2)}, u32[]{:S(2)}) collective-permute-start(bf16[19,8,1024]{2,1,0:T(8,128)(2,1)S(1)} %pad_maximum_fusion.1), channel_id=1, source_target_pairs={{0,4},{4,0},{8,12},{12,8},{1,5},{5,1},{9,13},{13,9},{2,6},{6,2},{1... | collective-permute-start | bytes 933896 | tf_op jit(solution)/shard_map/ppermute | solution.py:62
  13.5 13.1 %collective-permute-start.2 = (bf16[8,8,1024]{2,1,0:T(8,128)(2,1)S(1)}, bf16[8,8,1024]{2,1,0:T(8,128)(2,1)S(1)}, u32[]{:S(2)}, u32[]{:S(2)}) collective-permute-start(bf16[8,8,1024]{2,1,0:T(8,128)(2,1)S(1)} %slice.48), channel_id=1, source_target_pairs={{0,16},{16,0},{1,17},{17,1},{2,18},{18,2},{3,19},{19,3},{4,20},{20... | collective-permute-start | bytes 393224 | tf_op jit(solution)/shard_map/ppermute | solution.py:62
  14.5 10.8 %collective-permute-start.3 = (bf16[11,8,1024]{2,1,0:T(8,128)(2,1)S(1)}, bf16[11,8,1024]{2,1,0:T(8,128)(2,1)S(1)}, u32[]{:S(2)}, u32[]{:S(2)}) collective-permute-start(bf16[11,8,1024]{2,1,0:T(8,128)(2,1)S(1)} %get-tuple-element.24), channel_id=1, source_target_pairs={{0,12},{4,8},{8,4},{12,0},{1,13},{5,9},{9,5},{13,1},{2,14},{6,10},... | collective-permute-start | bytes 540680 | tf_op jit(solution)/shard_map/ppermute | solution.py:62
  25.4 2.3 %collective-permute-start.5 = (bf16[4,3,8,1024]{3,2,1,0:T(8,128)(2,1)S(1)}, bf16[4,3,8,1024]{3,2,1,0:T(8,128)(2,1)S(1)}, u32[]{:S(2)}, u32[]{:S(2)}) collective-permute-start(bf16[4,3,8,1024]{3,2,1,0:T(8,128)(2,1)S(1)} %pad_maximum_fusion.4), channel_id=1, source_target_pairs={{0,1},{1,0},{2,3},{3,2},{4,5},{5,4},{6,7},{7,6},{8,9},{9,8},{10,11... | collective-permute-start | bytes 589832 | tf_op jit(solution)/shard_map/ppermute | solution.py:62
  26.6 5.2 %collective-permute-start.4 = (bf16[8,8,1024]{2,1,0:T(8,128)(2,1)S(1)}, bf16[8,8,1024]{2,1,0:T(8,128)(2,1)S(1)}, u32[]{:S(2)}, u32[]{:S(2)}) collective-permute-start(bf16[8,8,1024]{2,1,0:T(8,128)(2,1)S(1)} %slice.31), channel_id=1, source_target_pairs={{0,16},{16,0},{1,17},{17,1},{2,18},{18,2},{3,19},{19,3},{4,20},{20... | collective-permute-start | bytes 393224 | tf_op jit(solution)/shard_map/ppermute | solution.py:62
  35.2 26.9 %collective-permute-start.16 = (bf16[8,256,1024]{2,1,0:T(8,128)(2,1)}, bf16[8,256,1024]{2,1,0:T(8,128)(2,1)}, u32[]{:S(2)}, u32[]{:S(2)}) collective-permute-start(bf16[8,256,1024]{2,1,0:T(8,128)(2,1)} %bitcast.60.refs_6_), channel_id=1, source_target_pairs={{0,1},{1,0},{2,3},{3,2},{4,5},{5,4},{6,7},{7,6},{8,9},{9,8},{10,11... | collective-permute-start | bytes 12582920 | tf_op jit(solution)/shard_map/ppermute | solution.py:62
  36.1 7.9 %collective-permute-start.6 = (bf16[8,16,1024]{2,1,0:T(8,128)(2,1)S(1)}, bf16[8,16,1024]{2,1,0:T(8,128)(2,1)S(1)}, u32[]{:S(2)}, u32[]{:S(2)}) collective-permute-start(bf16[8,16,1024]{2,1,0:T(8,128)(2,1)S(1)} %get-tuple-element.29), channel_id=1, source_target_pairs={{0,2},{2,0},{1,3},{3,1},{4,6},{6,4},{5,7},{7,5},{8,10},{10,8},{9,1... | collective-permute-start | bytes 786440 | tf_op jit(solution)/shard_map/ppermute | solution.py:62
  37.3 11.4 %collective-permute-start.8 = (bf16[8,16,1024]{2,1,0:T(8,128)(2,1)S(1)}, bf16[8,16,1024]{2,1,0:T(8,128)(2,1)S(1)}, u32[]{:S(2)}, u32[]{:S(2)}) collective-permute-start(bf16[8,16,1024]{2,1,0:T(8,128)(2,1)S(1)} %get-tuple-element.29), channel_id=1, source_target_pairs={{0,4},{4,0},{8,12},{12,8},{1,5},{5,1},{9,13},{13,9},{2,6},{6,2},{1... | collective-permute-start | bytes 786440 | tf_op jit(solution)/shard_map/ppermute | solution.py:62
  37.7 11.9 %collective-permute-start.9 = (bf16[8,16,1024]{2,1,0:T(8,128)(2,1)S(1)}, bf16[8,16,1024]{2,1,0:T(8,128)(2,1)S(1)}, u32[]{:S(2)}, u32[]{:S(2)}) collective-permute-start(bf16[8,16,1024]{2,1,0:T(8,128)(2,1)S(1)} %get-tuple-element.32.refs_0_), channel_id=1, source_target_pairs={{0,2},{2,0},{1,3},{3,1},{4,6},{6,4},{5,7},{7,5},{8,10},{10,8},{9,1... | collective-permute-start | bytes 786440 | tf_op jit(solution)/shard_map/ppermute | solution.py:62
  37.9 14.9 %collective-permute-start.14 = (bf16[8,16,1024]{2,1,0:T(8,128)(2,1)S(1)}, bf16[8,16,1024]{2,1,0:T(8,128)(2,1)S(1)}, u32[]{:S(2)}, u32[]{:S(2)}) collective-permute-start(bf16[8,16,1024]{2,1,0:T(8,128)(2,1)S(1)} %get-tuple-element.35), channel_id=1, source_target_pairs={{0,8},{4,12},{8,0},{12,4},{1,9},{5,13},{9,1},{13,5},{2,10},{6,14},... | collective-permute-start | bytes 786440 | tf_op jit(solution)/shard_map/ppermute | solution.py:62
  44.0 17.8 %collective-permute-start.11 = (bf16[8,16,1024]{2,1,0:T(8,128)(2,1)S(1)}, bf16[8,16,1024]{2,1,0:T(8,128)(2,1)S(1)}, u32[]{:S(2)}, u32[]{:S(2)}) collective-permute-start(bf16[8,16,1024]{2,1,0:T(8,128)(2,1)S(1)} %collective-permute-done.6), channel_id=1, source_target_pairs={{0,4},{4,0},{8,12},{12,8},{1,5},{5,1},{9,13},{13,9},{2,6},{6,2},{1... | collective-permute-start | bytes 786440 | tf_op jit(solution)/shard_map/ppermute | solution.py:62
  49.6 9.4 %collective-permute-start.10 = (bf16[4,16,1024]{2,1,0:T(8,128)(2,1)S(1)}, bf16[4,16,1024]{2,1,0:T(8,128)(2,1)S(1)}, u32[]{:S(2)}, u32[]{:S(2)}) collective-permute-start(bf16[4,16,1024]{2,1,0:T(8,128)(2,1)S(1)} %get-tuple-element.33), channel_id=1, source_target_pairs={{0,12},{4,8},{8,4},{12,0},{1,13},{5,9},{9,5},{13,1},{2,14},{6,10},... | collective-permute-start | bytes 393224 | tf_op jit(solution)/shard_map/ppermute | solution.py:62
  51.5 10.3 %collective-permute-start.7 = (bf16[4,16,1024]{2,1,0:T(8,128)(2,1)S(1)}, bf16[4,16,1024]{2,1,0:T(8,128)(2,1)S(1)}, u32[]{:S(2)}, u32[]{:S(2)}) collective-permute-start(bf16[4,16,1024]{2,1,0:T(8,128)(2,1)S(1)} %get-tuple-element.30), channel_id=1, source_target_pairs={{0,12},{4,8},{8,4},{12,0},{1,13},{5,9},{9,5},{13,1},{2,14},{6,10},... | collective-permute-start | bytes 393224 | tf_op jit(solution)/shard_map/ppermute | solution.py:62
  52.9 9.3 %collective-permute-start.15 = (bf16[8,16,1024]{2,1,0:T(8,128)(2,1)S(1)}, bf16[8,16,1024]{2,1,0:T(8,128)(2,1)S(1)}, u32[]{:S(2)}, u32[]{:S(2)}) collective-permute-start(bf16[8,16,1024]{2,1,0:T(8,128)(2,1)S(1)} %collective-permute-done.14.refs_4_), channel_id=1, source_target_pairs={{0,2},{2,0},{1,3},{3,1},{4,6},{6,4},{5,7},{7,5},{8,10},{10,8},{9,1... | collective-permute-start | bytes 786440 | tf_op jit(solution)/shard_map/ppermute | solution.py:62
  59.0 8.5 %collective-permute-start.13 = (bf16[4,16,1024]{2,1,0:T(8,128)(2,1)S(1)}, bf16[4,16,1024]{2,1,0:T(8,128)(2,1)S(1)}, u32[]{:S(2)}, u32[]{:S(2)}) collective-permute-start(bf16[4,16,1024]{2,1,0:T(8,128)(2,1)S(1)} %collective-permute-done.10.refs_1_), channel_id=1, source_target_pairs={{0,2},{2,0},{1,3},{3,1},{4,6},{6,4},{5,7},{7,5},{8,10},{10,8},{9,1... | collective-permute-start | bytes 393224 | tf_op jit(solution)/shard_map/ppermute | solution.py:62
  61.8 5.7 %collective-permute-start.12 = (bf16[4,16,1024]{2,1,0:T(8,128)(2,1)S(1)}, bf16[4,16,1024]{2,1,0:T(8,128)(2,1)S(1)}, u32[]{:S(2)}, u32[]{:S(2)}) collective-permute-start(bf16[4,16,1024]{2,1,0:T(8,128)(2,1)S(1)} %collective-permute-done.7.refs_0_), channel_id=1, source_target_pairs={{0,2},{2,0},{1,3},{3,1},{4,6},{6,4},{5,7},{7,5},{8,10},{10,8},{9,1... | collective-permute-start | bytes 393224 | tf_op jit(solution)/shard_map/ppermute | solution.py:62
  70.5 8.5 %collective-permute-start.20 = (bf16[64,256]{1,0:T(8,128)(2,1)S(1)}, bf16[64,256]{1,0:T(8,128)(2,1)S(1)}, u32[]{:S(2)}, u32[]{:S(2)}) collective-permute-start(bf16[64,256]{1,0:T(8,128)(2,1)S(1)} %get-tuple-element.50), channel_id=1, source_target_pairs={{0,9},{1,13},{4,8},{5,12},{8,1},{9,5},{12,0},{13,4},{2,11},{3,15},... | collective-permute-start | bytes 98312 | tf_op jit(solution)/shard_map/ppermute | solution.py:278
  72.7 6.2 %collective-permute-start.19 = (bf16[64,256]{1,0:T(8,128)(2,1)S(1)}, bf16[64,256]{1,0:T(8,128)(2,1)S(1)}, u32[]{:S(2)}, u32[]{:S(2)}) collective-permute-start(bf16[64,256]{1,0:T(8,128)(2,1)S(1)} %get-tuple-element.51), channel_id=1, source_target_pairs={{0,8},{1,12},{4,9},{5,13},{8,0},{9,4},{12,1},{13,5},{2,10},{3,14},... | collective-permute-start | bytes 98312 | tf_op jit(solution)/shard_map/ppermute | solution.py:278
  75.4 3.6 %collective-permute-start.18 = (bf16[64,256]{1,0:T(8,128)(2,1)S(1)}, bf16[64,256]{1,0:T(8,128)(2,1)S(1)}, u32[]{:S(2)}, u32[]{:S(2)}) collective-permute-start(bf16[64,256]{1,0:T(8,128)(2,1)S(1)} %get-tuple-element.52), channel_id=1, source_target_pairs={{0,1},{1,5},{4,0},{5,4},{8,9},{9,13},{12,8},{13,12},{2,3},{3,7},{6... | collective-permute-start | bytes 98312 | tf_op jit(solution)/shard_map/ppermute | solution.py:278
  77.0 5.2 %collective-permute-start.17 = (bf16[64,256]{1,0:T(8,128)(2,1)S(1)}, bf16[64,256]{1,0:T(8,128)(2,1)S(1)}, u32[]{:S(2)}, u32[]{:S(2)}) collective-permute-start(bf16[64,256]{1,0:T(8,128)(2,1)S(1)} %get-tuple-element.49), channel_id=1, source_target_pairs={{0,0},{1,4},{4,1},{5,5},{8,8},{9,12},{12,9},{13,13},{2,2},{3,6},{6... | collective-permute-start | bytes 98312 | tf_op jit(solution)/shard_map/ppermute | solution.py:278
